TPU v7x, 256 devices: a whole 4x4x8 slice. The times are simulated.
256 devices in a mesh: seq: 64 (over z, y_hi, x), head: 4 (over y_lo, core).
Axes of the slice: x: 4, y: 4 (y_hi: 2, y_lo: 2; y = y_hi * 2 + y_lo), z: 8, core: 2. Of those that a mesh axis runs over, the one named last changes fastest.
Arguments:
- q_shared: bfloat16 [8192, 512], P('seq'), may hold values from -4 to 4
- k_shared: bfloat16 [8192, 512], P('seq'), may hold values from -4 to 4
- mixing: float32 [64, 512], P('head'), may hold values from 0.25 to 2
- values: bfloat16 [8192, 8192], P('seq', 'head'), may hold values from -6 to 6
- cotangent: bfloat16 [8192, 8192], P('seq', 'head'), may hold values from -24 to 24
Outputs:
- d_query: bfloat16 [8192, 512], P('seq', 'head')
- d_key: bfloat16 [8192, 512], P('seq', 'head')
- d_values: bfloat16 [8192, 8192], P('seq', 'head')
- d_mixing: float32 [64, 512], P('head')
All inputs are finite; a program needn't handle non-finite values.
Results may differ from a plain program's by a relative error of at most 0.011.
Values may be sent and summed in bfloat16 or wider, within the bound.
No kernel may reach another device: no remote copies, remote signals or barrier semaphores. Data moves between devices by JAX's collectives and lax.ppermute only.
A program may use at most 128 MiB of HBM per device.

v0:
```python
from functools import reduce
import math

import jax
import jax.numpy as jnp
from jax import lax
from jax.sharding import PartitionSpec as P

WINDOW = 512
TOK_DEV = 128


def from_behind(x, axis, by):
    peers = lax.axis_size(axis)
    pairs = [(i, i + by) for i in range(peers) if 0 <= i + by < peers]
    return lax.ppermute(x, axis, pairs)


def per_device(q_shared, k_shared, mixing, values, cotangent):
    tok_rows = q_shared.shape[0]
    qk_width = q_shared.shape[1]
    local_heads = mixing.shape[0]
    head_width = values.shape[1] // local_heads
    score_scale = 1.0 / math.sqrt(qk_width)
    reach_blocks = WINDOW // TOK_DEV
    best = lax.Precision.HIGHEST
    offset = lax.axis_index("seq") * tok_rows
    heads_done = False
    mixed_query = (q_shared[None].astype(jnp.float32) * mixing[:, None, :]).astype(jnp.bfloat16)
    upstream = cotangent.reshape(tok_rows, local_heads, head_width)
    query_pos = offset + jnp.arange(tok_rows, dtype=jnp.int32)
    payload = jnp.concatenate([k_shared, values], 1)
    blocks = [payload]
    moving = payload
    for distance in range(1, reach_blocks + 1):
        moving = from_behind(moving, "seq", 1)
        blocks.append(moving)
    scores = []
    slopes = []
    for distance, incoming in enumerate(blocks):
        key_rows = incoming[:, :qk_width]
        value_rows = incoming[:, qk_width:].reshape(tok_rows, local_heads, head_width)
        key_pos = offset - distance * tok_rows + jnp.arange(tok_rows, dtype=jnp.int32)
        key_lag = query_pos[:, None] - key_pos[None, :]
        inside = (key_pos[None, :] >= 0) & (key_lag >= 0) & (key_lag < WINDOW)
        logits = (
            jnp.einsum("hqw,kw->hqk", mixed_query, key_rows, preferred_element_type=jnp.float32)
            * score_scale
        )
        scores.append(jnp.where(inside[None], logits, -jnp.inf))
        slopes.append(
            jnp.einsum("qhe,khe->hqk", upstream, value_rows, preferred_element_type=jnp.float32)
        )
    row_max = reduce(jnp.maximum, [jnp.max(logits, -1) for logits in scores])
    row_total = reduce(
        jnp.add, [jnp.sum(jnp.exp(logits - row_max[..., None]), -1) for logits in scores]
    )
    log_norm = row_max + jnp.log(row_total)
    weights = [jnp.exp(logits - log_norm[..., None]) for logits in scores]
    row_delta = reduce(
        jnp.add, [jnp.sum(weight * slope, -1) for weight, slope in zip(weights, slopes)]
    )
    query_grad = jnp.zeros((local_heads, tok_rows, qk_width), jnp.float32)
    key_parts = []
    value_parts = []
    for distance, incoming in enumerate(blocks):
        key_rows = incoming[:, :qk_width]
        score_grad = weights[distance] * (slopes[distance] - row_delta[..., None])
        weight_half = weights[distance].astype(jnp.bfloat16)
        grad_half = score_grad.astype(jnp.bfloat16)
        value_parts.append(
            jnp.einsum(
                "hqk,qhe->khe", weight_half, upstream, preferred_element_type=jnp.float32
            ).reshape(tok_rows, local_heads * head_width)
        )
        key_parts.append(
            jnp.einsum("hqk,hqw->kw", grad_half, mixed_query, preferred_element_type=jnp.float32)
            * score_scale
        )
        query_grad = query_grad + jnp.einsum(
            "hqk,kw->hqw", grad_half, key_rows, preferred_element_type=jnp.float32
        )
    query_grad = query_grad * score_scale
    query_part = jnp.einsum("hqw,hw->qw", query_grad, mixing, precision=best)
    mixing_part = jnp.einsum("hqw,qw->hw", query_grad, q_shared.astype(jnp.float32), precision=best)
    key_width = key_parts[0].shape[1]
    returns = [
        jnp.concatenate([key_parts[position], value_parts[position]], 1)
        for position in range(reach_blocks + 1)
    ]
    gathered = returns[reach_blocks]
    for hop_index in range(1, reach_blocks + 1):
        gathered = from_behind(gathered, "seq", -1) + returns[reach_blocks - hop_index]
    key_sum = gathered[:, :key_width]
    value_sum = gathered[:, key_width:]
    d_mixing = lax.psum(mixing_part, "seq")
    d_key, d_query = (
        lax.psum_scatter(key_sum, "head", scatter_dimension=1, tiled=True),
        lax.psum_scatter(query_part, "head", scatter_dimension=1, tiled=True),
    )
    return (
        d_query.astype(jnp.bfloat16),
        d_key.astype(jnp.bfloat16),
        value_sum.astype(jnp.bfloat16),
        d_mixing,
    )


def solution(mesh):
    placed = (P("seq", None), P("seq", None), P("head", None), P("seq", "head"), P("seq", "head"))
    return jax.shard_map(
        per_device,
        mesh=mesh,
        in_specs=placed,
        out_specs=(P("seq", "head"), P("seq", "head"), P("seq", "head"), P("head", None)),
        check_vma=False,
    )
```

profile of v0, /device:TPU:128, one launch (start us, length us, event | category | flops | bytes accessed | tf_op | source)
XLA Modules:
  0.0 626.7 jit_solution(12492264185016370010)
XLA Ops:
  8.4 3.4 collective-permute-start
  11.8 1.3 copy.64
  13.2 19.3 %collective-permute-done = bf16[128,2560]{1,0:T(8,128)(2,1)S(1)} collective-permute-done((bf16[128,2560]{1,0:T(8,128)(2,1)S(1)}, bf16[128,2560]{1,0:T(8,128)(2,1)S(1)}, u32[]{:S(2)}, u32[]{:S(2)}) %collective-permute-start) | collective-permute-done | bytes 655392 | tf_op jit(solution)/shard_map/ppermute | solution.py:16
  32.4 1.9 collective-permute-start.1
  35.7 2.4 fusion.73
  38.1 17.6 %collective-permute-done.1 = bf16[128,2560]{1,0:T(8,128)(2,1)S(1)} collective-permute-done((bf16[128,2560]{1,0:T(8,128)(2,1)S(1)}, bf16[128,2560]{1,0:T(8,128)(2,1)S(1)}, u32[]{:S(2)}, u32[]{:S(2)}) %collective-permute-start.1) | collective-permute-done | bytes 655392 | tf_op jit(solution)/shard_map/ppermute | solution.py:16
  55.7 1.9 collective-permute-start.2
  58.4 1.8 fusion.101
  61.5 16.4 %collective-permute-done.2 = bf16[128,2560]{1,0:T(8,128)(2,1)S(1)} collective-permute-done((bf16[128,2560]{1,0:T(8,128)(2,1)S(1)}, bf16[128,2560]{1,0:T(8,128)(2,1)S(1)}, u32[]{:S(2)}, u32[]{:S(2)}) %collective-permute-start.2) | collective-permute-done | bytes 655392 | tf_op jit(solution)/shard_map/ppermute | solution.py:16
  77.9 1.9 collective-permute-start.3
  81.6 1.4 convolution_bitcast_fusion.1
  82.9 16.4 %collective-permute-done.3 = bf16[128,2560]{1,0:T(8,128)(2,1)S(1)} collective-permute-done((bf16[128,2560]{1,0:T(8,128)(2,1)S(1)}, bf16[128,2560]{1,0:T(8,128)(2,1)S(1)}, u32[]{:S(2)}, u32[]{:S(2)}) %collective-permute-start.3) | collective-permute-done | bytes 655392 | tf_op jit(solution)/shard_map/ppermute | solution.py:16
  101.1 1.4 exponential_reduce_fusion.3
  102.4 1.5 fusion.55
  103.9 2.6 copy.26
  106.5 1.3 convolution_bitcast_fusion
  107.9 4.2 multiply_reduce_fusion.5
  112.7 2.3 multiply_convert_fusion.51
  116.7 1.9 collective-permute-start.4
  118.6 1.5 fusion.57
  120.0 2.6 copy.29
  122.6 1.7 fusion.48
  124.3 21.4 %collective-permute-done.4 = f32[128,2560]{1,0:T(8,128)} collective-permute-done((f32[128,2560]{1,0:T(8,128)}, f32[128,2560]{1,0:T(8,128)}, u32[]{:S(2)}, u32[]{:S(2)}) %collective-permute-start.4) | collective-permute-done | bytes 1310752 | tf_op jit(solution)/shard_map/ppermute | solution.py:16
  145.7 2.9 maximum_add_fusion
  148.6 8.1 %collective-permute-start.5 = (f32[128,2560]{1,0:T(8,128)}, f32[128,2560]{1,0:T(8,128)}, u32[]{:S(2)}, u32[]{:S(2)}) collective-permute-start(f32[128,2560]{1,0:T(8,128)} %maximum_add_fusion), channel_id=1, source_target_pairs={{4,0},{8,4},{12,8},{16,12},{20,16},{24,20},{28,24},{32,28},{36,32}... | collective-permute-start | bytes 3932168 | tf_op jit(solution)/shard_map/ppermute | solution.py:16
  156.7 1.6 fusion.59
  158.3 2.5 copy.32
  160.8 1.7 fusion.47
  162.5 1.6 fusion.61
  164.1 16.5 %collective-permute-done.5 = f32[128,2560]{1,0:T(8,128)} collective-permute-done((f32[128,2560]{1,0:T(8,128)}, f32[128,2560]{1,0:T(8,128)}, u32[]{:S(2)}, u32[]{:S(2)}) %collective-permute-start.5) | collective-permute-done | bytes 1310752 | tf_op jit(solution)/shard_map/ppermute | solution.py:16
  180.6 2.6 maximum_add_fusion.1
  183.2 10.1 %collective-permute-start.6 = (f32[128,2560]{1,0:T(8,128)}, f32[128,2560]{1,0:T(8,128)}, u32[]{:S(2)}, u32[]{:S(2)}) collective-permute-start(f32[128,2560]{1,0:T(8,128)} %maximum_add_fusion.1), channel_id=1, source_target_pairs={{4,0},{8,4},{12,8},{16,12},{20,16},{24,20},{28,24},{32,28},{36,32}... | collective-permute-start | bytes 3932168 | tf_op jit(solution)/shard_map/ppermute | solution.py:16
  193.3 1.5 fusion.63
  196.1 1.6 copy.38
  197.7 1.6 fusion.46
  200.0 1.7 fusion.85
  201.8 1.7 fusion.84
  203.5 12.9 %collective-permute-done.6 = f32[128,2560]{1,0:T(8,128)} collective-permute-done((f32[128,2560]{1,0:T(8,128)}, f32[128,2560]{1,0:T(8,128)}, u32[]{:S(2)}, u32[]{:S(2)}) %collective-permute-start.6) | collective-permute-done | bytes 1310752 | tf_op jit(solution)/shard_map/ppermute | solution.py:16
  216.4 2.6 maximum_add_fusion.2
  219.0 10.1 %collective-permute-start.7 = (f32[128,2560]{1,0:T(8,128)}, f32[128,2560]{1,0:T(8,128)}, u32[]{:S(2)}, u32[]{:S(2)}) collective-permute-start(f32[128,2560]{1,0:T(8,128)} %maximum_add_fusion.2), channel_id=1, source_target_pairs={{4,0},{8,4},{12,8},{16,12},{20,16},{24,20},{28,24},{32,28},{36,32}... | collective-permute-start | bytes 3932168 | tf_op jit(solution)/shard_map/ppermute | solution.py:16
  229.1 1.6 fusion.86
  230.8 5.3 multiply_reduce_fusion.1
  236.7 14.6 %collective-permute-done.7 = f32[128,2560]{1,0:T(8,128)} collective-permute-done((f32[128,2560]{1,0:T(8,128)}, f32[128,2560]{1,0:T(8,128)}, u32[]{:S(2)}, u32[]{:S(2)}) %collective-permute-start.7) | collective-permute-done | bytes 1310752 | tf_op jit(solution)/shard_map/ppermute | solution.py:16
  251.3 1.5 maximum_add_fusion.3
  253.5 2.8 multiply_reduce_fusion
  256.3 359.8 %psum.7 = f32[16,512]{1,0:T(8,128)} all-reduce(f32[16,512]{1,0:T(8,128)S(1)} %bitcast.159), channel_id=1, replica_groups=mesh['seq'=64,'head'=4] {'seq'}, use_global_device_ids=true, to_apply=%region_17.18 | all-reduce | flops 8192 | bytes 65536 | tf_op jit(solution)/shard_map/psum | solution.py:96
  616.1 1.5 convert_element_type.52
  618.4 1.5 convert_element_type.58
  (90 shorter events, 14.5 us)
Async XLA Ops:
  7.2 50.4 %copy-start.23 = (bf16[128,512]{1,0:T(8,128)(2,1)S(1)}, bf16[128,512]{1,0:T(8,128)(2,1)}, u32[]{:S(2)}) copy-start(bf16[128,512]{1,0:T(8,128)(2,1)} %param.6) | copy-start | bytes 393220
  7.2 50.4 %copy-start.27 = (f32[16,512]{1,0:T(8,128)S(1)}, f32[16,512]{1,0:T(8,128)}, u32[]{:S(2)}) copy-start(f32[16,512]{1,0:T(8,128)} %param.7) | copy-start | bytes 98308
  7.2 608.9 %reduce-scatter.3.cloned.1.call-start = ((), (), s32[]{:S(2)}) async-start(), calls=%async_computation.2 | async-start | bytes 327680 | tf_op jit(solution)/shard_map/reduce_scatter | solution.py:99
  8.4 24.1 %collective-permute-start = (bf16[128,2560]{1,0:T(8,128)(2,1)S(1)}, bf16[128,2560]{1,0:T(8,128)(2,1)S(1)}, u32[]{:S(2)}, u32[]{:S(2)}) collective-permute-start(bf16[128,2560]{1,0:T(8,128)(2,1)S(1)} %pad_maximum_fusion.1), channel_id=1, source_target_pairs={{0,4},{4,8},{8,12},{12,16},{16,20},{20,24},{24,28},{28,32},{32,36}... | collective-permute-start | bytes 1966088 | tf_op jit(solution)/shard_map/ppermute | solution.py:16
  32.4 25.1 %copy-start.20 = (bf16[128,2560]{1,0:T(8,128)(2,1)}, bf16[128,2560]{1,0:T(8,128)(2,1)S(1)}, u32[]{:S(2)}) copy-start(bf16[128,2560]{1,0:T(8,128)(2,1)S(1)} %collective-permute-done) | copy-start | bytes 1966084
  32.4 23.2 %collective-permute-start.1 = (bf16[128,2560]{1,0:T(8,128)(2,1)S(1)}, bf16[128,2560]{1,0:T(8,128)(2,1)S(1)}, u32[]{:S(2)}, u32[]{:S(2)}) collective-permute-start(bf16[128,2560]{1,0:T(8,128)(2,1)S(1)} %collective-permute-done), channel_id=1, source_target_pairs={{0,4},{4,8},{8,12},{12,16},{16,20},{20,24},{24,28},{28,32},{32,36}... | collective-permute-start | bytes 1966088 | tf_op jit(solution)/shard_map/ppermute | solution.py:16
  35.6 63.7 %copy-start.24 = (f32[128,512]{1,0:T(8,128)}, f32[128,512]{1,0:T(8,128)S(1)}, u32[]{:S(2)}) copy-start(f32[128,512]{1,0:T(8,128)S(1)} %get-tuple-element.15) | copy-start | bytes 786436
  55.6 24.2 %copy-start.21 = (bf16[128,2560]{1,0:T(8,128)(2,1)}, bf16[128,2560]{1,0:T(8,128)(2,1)S(1)}, u32[]{:S(2)}) copy-start(bf16[128,2560]{1,0:T(8,128)(2,1)S(1)} %collective-permute-done.1) | copy-start | bytes 1966084
  55.7 22.3 %collective-permute-start.2 = (bf16[128,2560]{1,0:T(8,128)(2,1)S(1)}, bf16[128,2560]{1,0:T(8,128)(2,1)S(1)}, u32[]{:S(2)}, u32[]{:S(2)}) collective-permute-start(bf16[128,2560]{1,0:T(8,128)(2,1)S(1)} %collective-permute-done.1), channel_id=1, source_target_pairs={{0,4},{4,8},{8,12},{12,16},{16,20},{20,24},{24,28},{28,32},{32,36}... | collective-permute-start | bytes 1966088 | tf_op jit(solution)/shard_map/ppermute | solution.py:16
  77.9 5.0 copy-start.22
  77.9 21.4 %collective-permute-start.3 = (bf16[128,2560]{1,0:T(8,128)(2,1)S(1)}, bf16[128,2560]{1,0:T(8,128)(2,1)S(1)}, u32[]{:S(2)}, u32[]{:S(2)}) collective-permute-start(bf16[128,2560]{1,0:T(8,128)(2,1)S(1)} %collective-permute-done.2), channel_id=1, source_target_pairs={{0,4},{4,8},{8,12},{12,16},{16,20},{20,24},{24,28},{28,32},{32,36}... | collective-permute-start | bytes 1966088 | tf_op jit(solution)/shard_map/ppermute | solution.py:16
  80.7 20.3 %copy-start = (f32[16,128,128]{1,2,0:T(8,128)}, f32[16,128,128]{1,2,0:T(8,128)S(1)}, u32[]{:S(2)}) copy-start(f32[16,128,128]{1,2,0:T(8,128)S(1)} %get-tuple-element.31) | copy-start | bytes 3145732
  81.6 20.8 %copy-start.3 = (f32[16,128,128]{1,2,0:T(8,128)}, f32[16,128,128]{1,2,0:T(8,128)S(1)}, u32[]{:S(2)}) copy-start(f32[16,128,128]{1,2,0:T(8,128)S(1)} %get-tuple-element.29) | copy-start | bytes 3145732
  99.3 0.9 copy-start.19
  101.0 1.4 copy-start.5
  107.8 4.3 copy-start.1
  107.9 4.3 copy-start.4
  107.9 4.3 copy-start.6
  107.9 4.3 copy-start.7
  107.9 4.5 copy-start.8
  107.9 4.8 copy-start.9
  112.7 2.3 copy-start.25
  112.7 2.3 copy-start.28
  112.7 2.8 copy-start.10
  115.0 5.1 copy-start.14
  116.7 29.1 %collective-permute-start.4 = (f32[128,2560]{1,0:T(8,128)}, f32[128,2560]{1,0:T(8,128)}, u32[]{:S(2)}, u32[]{:S(2)}) collective-permute-start(f32[128,2560]{1,0:T(8,128)} %pad_maximum_fusion), channel_id=1, source_target_pairs={{4,0},{8,4},{12,8},{16,12},{20,16},{24,20},{28,24},{32,28},{36,32}... | collective-permute-start | bytes 3932168 | tf_op jit(solution)/shard_map/ppermute | solution.py:16
  122.6 34.1 %copy-start.2 = (f32[16,128,128]{1,2,0:T(8,128)S(1)}, f32[16,128,128]{1,2,0:T(8,128)}, u32[]{:S(2)}) copy-start(f32[16,128,128]{1,2,0:T(8,128)} %copy-done) | copy-start | bytes 3145732
  148.6 32.0 %collective-permute-start.5 = (f32[128,2560]{1,0:T(8,128)}, f32[128,2560]{1,0:T(8,128)}, u32[]{:S(2)}, u32[]{:S(2)}) collective-permute-start(f32[128,2560]{1,0:T(8,128)} %maximum_add_fusion), channel_id=1, source_target_pairs={{4,0},{8,4},{12,8},{16,12},{20,16},{24,20},{28,24},{32,28},{36,32}... | collective-permute-start | bytes 3932168 | tf_op jit(solution)/shard_map/ppermute | solution.py:16
  160.8 19.8 %copy-start.13 = (f32[128,2048]{1,0:T(8,128)S(1)}, f32[128,2048]{1,0:T(8,128)}, u32[]{:S(2)}) copy-start(f32[128,2048]{1,0:T(8,128)} %copy.32) | copy-start | bytes 3145732
  164.1 30.7 %copy-start.11 = (f32[16,128,128]{1,2,0:T(8,128)S(1)}, f32[16,128,128]{1,2,0:T(8,128)}, u32[]{:S(2)}) copy-start(f32[16,128,128]{1,2,0:T(8,128)} %fusion.61) | copy-start | bytes 3145732
  183.2 33.2 %collective-permute-start.6 = (f32[128,2560]{1,0:T(8,128)}, f32[128,2560]{1,0:T(8,128)}, u32[]{:S(2)}, u32[]{:S(2)}) collective-permute-start(f32[128,2560]{1,0:T(8,128)} %maximum_add_fusion.1), channel_id=1, source_target_pairs={{4,0},{8,4},{12,8},{16,12},{20,16},{24,20},{28,24},{32,28},{36,32}... | collective-permute-start | bytes 3932168 | tf_op jit(solution)/shard_map/ppermute | solution.py:16
  196.0 3.9 copy-start.18
  199.3 2.5 copy-start.17
  200.0 16.4 %copy-start.12 = (f32[128,2048]{1,0:T(8,128)S(1)}, f32[128,2048]{1,0:T(8,128)}, u32[]{:S(2)}) copy-start(f32[128,2048]{1,0:T(8,128)} %copy.35) | copy-start | bytes 3145732
  201.7 27.4 %copy-start.16 = (bf16[16,128,128]{1,2,0:T(8,128)(2,1)S(1)}, bf16[16,128,128]{1,2,0:T(8,128)(2,1)}, u32[]{:S(2)}) copy-start(bf16[16,128,128]{1,2,0:T(8,128)(2,1)} %get-tuple-element.19) | copy-start | bytes 1572868
  203.4 27.3 %copy-start.15 = (bf16[16,128,128]{1,2,0:T(8,128)(2,1)S(1)}, bf16[16,128,128]{1,2,0:T(8,128)(2,1)}, u32[]{:S(2)}) copy-start(bf16[16,128,128]{1,2,0:T(8,128)(2,1)} %copy-done.14) | copy-start | bytes 1572868
  203.4 27.3 %copy-start.29 = (f32[16,512]{1,0:T(8,128)S(1)}, f32[16,512]{1,0:T(8,128)}, u32[]{:S(2)}) copy-start(f32[16,512]{1,0:T(8,128)} %param.7) | copy-start | bytes 98308
  219.0 32.3 %collective-permute-start.7 = (f32[128,2560]{1,0:T(8,128)}, f32[128,2560]{1,0:T(8,128)}, u32[]{:S(2)}, u32[]{:S(2)}) collective-permute-start(f32[128,2560]{1,0:T(8,128)} %maximum_add_fusion.2), channel_id=1, source_target_pairs={{4,0},{8,4},{12,8},{16,12},{20,16},{24,20},{28,24},{32,28},{36,32}... | collective-permute-start | bytes 3932168 | tf_op jit(solution)/shard_map/ppermute | solution.py:16
  230.8 5.4 copy-start.26
  236.1 382.3 %reduce-scatter.5.cloned.1.call-start = ((), (), s32[]{:S(2)}) async-start(), calls=%async_computation.3 | async-start | bytes 327680 | tf_op jit(solution)/shard_map/reduce_scatter | solution.py:98
Sparse Core Ops, SparseCore 0:
  236.3 17.2 reduce-scatter.2
  256.2 24.8 reduce-scatter.4
where the time goes:
time: 628 us; the launch traced here: 627 us
  blocking collectives  360 us (57%)
  waiting for transfers between devices  135 us (21%)
  matrix products  40.2 us (6%)
  starting transfers between devices  39.4 us (6%)
  other arithmetic  22.5 us (4%)
  local copies, waits for them, and re-layouts  15 us (2%)
  between operations  14.6 us (2%)
    psum x1, blocking collectives, per_device(): d_mixing = lax.psum(mixing_part, 'seq')  360 us
    ppermute x8, waiting for transfers between devices, from_behind(): return lax.ppermute(x, axis, pairs)  135 us
    ppermute x8, starting transfers between devices, from_behind(): return lax.ppermute(x, axis, pairs)  39.3 us
  transfers between devices with their start and end apart: 10, of which 8 were waited for; matrix products, arithmetic and copies ran while one was open for 8% of the time, Pallas kernels for 0%

commit v1 on v0

v1 whole, which is shorter than its diff:
```python
import functools
import math

import jax
import jax.numpy as jnp
from jax import lax
from jax.experimental import pallas as pl
from jax.experimental.pallas import tpu as pltpu
from jax.sharding import PartitionSpec as P

GROUP = 4
HALF = 256
NEG = -1e30
LOG2E = 1.4426950408889634

NT = (((1,), (1,)), ((), ()))
NN = (((1,), (0,)), ((), ()))
TN = (((0,), (0,)), ((), ()))


def dot(a, b, dims):
    return lax.dot_general(a, b, dims, preferred_element_type=jnp.float32)


def own_kernel(scale, first_ref, mix_ref, v_ref, km_ref, c_ref, qm_ref, ko_ref, qo_ref,
               vp_ref, kpm_ref, kpo_ref, stats_ref, dqm_ref, dqo_ref, dk_ref, dv_ref,
               dmix_ref, k_all, q_all, v_all, dq_acc):
    head = pl.program_id(0)
    span = q_all.shape[0]
    tile = span // 2
    half = km_ref.shape[1]

    @pl.when(head == 0)
    def _():
        k_all[:span, :half] = kpm_ref[...]
        k_all[:span, half:] = kpo_ref[...]
        k_all[span:, :half] = km_ref[...]
        k_all[span:, half:] = ko_ref[...]
        q_all[:, :half] = qm_ref[...]
        q_all[:, half:] = qo_ref[...]
        dk_ref[...] = jnp.zeros_like(dk_ref)
        dq_acc[...] = jnp.zeros_like(dq_acc)

    v_all[:span, :] = vp_ref[...]
    v_all[span:, :] = v_ref[...]
    mix = mix_ref[0]
    is_first = first_ref[0] == 1
    row = lax.broadcasted_iota(jnp.int32, (tile, tile), 0)
    col = lax.broadcasted_iota(jnp.int32, (tile, tile), 1)
    dmix = jnp.zeros((1, mix.shape[1]), jnp.float32)
    for t in (1, 0):
        lo = t * tile
        q_f32 = q_all[lo:lo + tile, :].astype(jnp.float32)
        mq = (q_f32 * mix).astype(jnp.bfloat16)
        up = c_ref[lo:lo + tile, :]
        keys = k_all[lo:lo + 3 * tile, :]
        s = dot(keys, mq, NT) * (scale * LOG2E)
        d = dot(v_all[lo:lo + 3 * tile, :], up, NT)
        s0 = jnp.where((row > col) & jnp.logical_not(is_first), s[:tile], NEG)
        s1 = s[tile:2 * tile]
        if t == 0:
            s1 = jnp.where(is_first, NEG, s1)
        s2 = jnp.where(row <= col, s[2 * tile:], NEG)
        top = jnp.max(jnp.maximum(jnp.maximum(s0, s1), s2), 0, keepdims=True)
        p = [jnp.exp2(part - top) for part in (s0, s1, s2)]
        total = jnp.sum(p[0] + p[1] + p[2], 0, keepdims=True)
        inv = 1.0 / total
        w = [part * inv for part in p]
        ds = [d[:tile], d[tile:2 * tile], d[2 * tile:]]
        delta = jnp.sum(w[0] * ds[0] + w[1] * ds[1] + w[2] * ds[2], 0, keepdims=True)
        grad = jnp.concatenate(
            [(a * (b - delta)).astype(jnp.bfloat16) for a, b in zip(w, ds)], 0)
        stats_ref[0, 0:1, lo:lo + tile] = top + jnp.log2(total)
        stats_ref[0, 1:2, lo:lo + tile] = delta
        qg = dot(grad, keys, TN) * scale
        dq_acc[lo:lo + tile, :] += qg * mix
        dmix = dmix + jnp.sum(qg * q_f32, 0, keepdims=True)
        if t == 1:
            w_own = jnp.concatenate([w[1].astype(jnp.bfloat16), w[2].astype(jnp.bfloat16)], 0)
            dv_ref[...] = dot(w_own, up, NN)
            dk_ref[...] += dot(grad[tile:], mq, NN)
        else:
            dv_ref[:tile, :] += dot(w[2].astype(jnp.bfloat16), up, NN)
            dk_ref[:tile, :] += dot(grad[2 * tile:], mq, NN)
    dmix_ref[0] = dmix

    @pl.when(head == pl.num_programs(0) - 1)
    def _():
        dqm_ref[...] = dq_acc[:, :half]
        dqo_ref[...] = dq_acc[:, half:].astype(jnp.bfloat16)


def next_kernel(scale, mix_ref, v_ref, km_ref, ko_ref, cn_ref, qnm_ref, qno_ref, stats_ref,
                dk_ref, dv_ref, dkm_ref, dko_ref, dvo_ref, k_all, q_all, dk_acc):
    head = pl.program_id(0)
    span = q_all.shape[0]
    tile = span // 2
    half = km_ref.shape[1]

    @pl.when(head == 0)
    def _():
        k_all[:, :half] = km_ref[...]
        k_all[:, half:] = ko_ref[...]
        q_all[:, :half] = qnm_ref[...]
        q_all[:, half:] = qno_ref[...]
        dk_acc[...] = dk_ref[...]

    mix = mix_ref[0]
    row = lax.broadcasted_iota(jnp.int32, (tile, tile), 0)
    col = lax.broadcasted_iota(jnp.int32, (tile, tile), 1)
    dv = [dv_ref[:tile, :], dv_ref[tile:, :]]
    for t in (0, 1):
        lo = t * tile
        mq = (q_all[lo:lo + tile, :].astype(jnp.float32) * mix).astype(jnp.bfloat16)
        up = cn_ref[lo:lo + tile, :]
        lse = stats_ref[0, 0:1, lo:lo + tile]
        delta = stats_ref[0, 1:2, lo:lo + tile]
        s = dot(k_all[lo:, :], mq, NT) * (scale * LOG2E)
        d = dot(v_ref[lo:, :], up, NT)
        w = jnp.exp2(jnp.where(row > col, s[:tile] - lse, NEG))
        if t == 0:
            w = jnp.concatenate([w, jnp.exp2(s[tile:] - lse)], 0)
        grad = (w * (d - delta)).astype(jnp.bfloat16)
        add = dot(w.astype(jnp.bfloat16), up, NN)
        if t == 0:
            dv = [dv[0] + add[:tile], dv[1] + add[tile:]]
        else:
            dv[1] = dv[1] + add
        dk_acc[lo:, :] += dot(grad, mq, NN)
    dvo_ref[:tile, :] = dv[0].astype(jnp.bfloat16)
    dvo_ref[tile:, :] = dv[1].astype(jnp.bfloat16)

    @pl.when(head == pl.num_programs(0) - 1)
    def _():
        dkm_ref[...] = dk_acc[:, :half] * scale
        dko_ref[...] = (dk_acc[:, half:] * scale).astype(jnp.bfloat16)


def own_part(scale, first, mix, x1, kq_other, x2, kp_other):
    heads, _, width = mix.shape
    span = x1.shape[0]
    half = width // 2
    f32, b16 = jnp.float32, jnp.bfloat16
    by_head = lambda base: pl.BlockSpec((span, 128), lambda h, base=base: (0, base + h))
    fixed = lambda at: pl.BlockSpec((span, half), lambda h, at=at: (0, at))
    whole = lambda c: pl.BlockSpec((span, c), lambda h: (0, 0))
    return pl.pallas_call(
        functools.partial(own_kernel, scale),
        grid=(heads,),
        in_specs=[
            pl.BlockSpec(memory_space=pltpu.SMEM),
            pl.BlockSpec((1, 1, width), lambda h: (h, 0, 0)),
            by_head(0), fixed(2), by_head(6), fixed(5),
            fixed(0), fixed(1),
            by_head(0), fixed(2), whole(half),
        ],
        out_specs=[
            pl.BlockSpec((1, 2, span), lambda h: (h, 0, 0)),
            whole(half), whole(half), whole(width), by_head(0),
            pl.BlockSpec((1, 1, width), lambda h: (h, 0, 0)),
        ],
        out_shape=[
            jax.ShapeDtypeStruct((heads, 2, span), f32),
            jax.ShapeDtypeStruct((span, half), f32),
            jax.ShapeDtypeStruct((span, half), b16),
            jax.ShapeDtypeStruct((span, width), f32),
            jax.ShapeDtypeStruct((span, heads * 128), f32),
            jax.ShapeDtypeStruct((heads, 1, width), f32),
        ],
        scratch_shapes=[
            pltpu.VMEM((2 * span, width), b16),
            pltpu.VMEM((span, width), b16),
            pltpu.VMEM((2 * span, 128), b16),
            pltpu.VMEM((span, width), f32),
        ],
        compiler_params=pltpu.CompilerParams(vmem_limit_bytes=40 * 2**20),
        cost_estimate=pl.CostEstimate(flops=5_000_000_000, bytes_accessed=8_000_000, transcendentals=1_600_000),
    )(first, mix, x1, x1, x1, x1, kq_other, kq_other, x2, x2, kp_other)


def next_part(scale, mix, x1, kq_other, x3, qn_other, stats, dk, dv):
    heads, _, width = mix.shape
    span = x1.shape[0]
    half = width // 2
    f32, b16 = jnp.float32, jnp.bfloat16
    by_head = lambda base: pl.BlockSpec((span, 128), lambda h, base=base: (0, base + h))
    fixed = lambda at: pl.BlockSpec((span, half), lambda h, at=at: (0, at))
    whole = lambda c: pl.BlockSpec((span, c), lambda h: (0, 0))
    return pl.pallas_call(
        functools.partial(next_kernel, scale),
        grid=(heads,),
        in_specs=[
            pl.BlockSpec((1, 1, width), lambda h: (h, 0, 0)),
            by_head(0), fixed(2), fixed(0), by_head(0), fixed(2), whole(half),
            pl.BlockSpec((1, 2, span), lambda h: (h, 0, 0)),
            whole(width), by_head(0),
        ],
        out_specs=[whole(half), whole(half), by_head(0)],
        out_shape=[
            jax.ShapeDtypeStruct((span, half), f32),
            jax.ShapeDtypeStruct((span, half), b16),
            jax.ShapeDtypeStruct((span, heads * 128), b16),
        ],
        scratch_shapes=[
            pltpu.VMEM((span, width), b16),
            pltpu.VMEM((span, width), b16),
            pltpu.VMEM((span, width), f32),
        ],
        compiler_params=pltpu.CompilerParams(vmem_limit_bytes=40 * 2**20),
        cost_estimate=pl.CostEstimate(flops=2_500_000_000, bytes_accessed=7_000_000, transcendentals=800_000),
    )(mix, x1, x1, kq_other, x3, x3, qn_other, stats, dk, dv)


def per_device(q_shared, k_shared, mixing, values, cotangent):
    tok, width = q_shared.shape
    peers = lax.axis_size("seq")
    groups = [[GROUP * g + x for x in range(GROUP)] for g in range(peers // GROUP)]
    scale = 1.0 / math.sqrt(width)
    me = lax.axis_index("seq")
    place = me % GROUP
    head_at = lax.axis_index("head")
    core = head_at % 2
    y_lo = head_at // 2
    heads = mixing.shape[0] // GROUP
    cols = values.shape[1] // GROUP

    def along_groups(x, by):
        pairs = [(i, i + GROUP * by) for i in range(peers) if 0 <= i + GROUP * by < peers]
        return lax.ppermute(x, "seq", pairs)

    def core_swap(x):
        return lax.ppermute(x, "head", [(0, 1), (1, 0), (2, 3), (3, 2)])

    def trade(x):
        return lax.all_to_all(x, "seq", 0, 0, axis_index_groups=groups, tiled=True)

    def half_of(x, which):
        blocks = x.reshape(x.shape[0], 2, 2, 128)
        return lax.dynamic_index_in_dim(blocks, which, 2, keepdims=False).reshape(x.shape[0], 256)

    def split(x):
        return x.reshape(tok, GROUP, cols).transpose(1, 0, 2)

    def spread(x):
        return jnp.broadcast_to(x[None], (GROUP,) + x.shape)

    k_half = half_of(k_shared, core)
    q_half = half_of(q_shared, core)

    raw = along_groups(jnp.concatenate([values, k_half], 1), 1)
    pay1 = jnp.concatenate([split(values), spread(k_half), split(cotangent), spread(q_half)], 2)
    x1 = trade(pay1.reshape(GROUP * tok, -1))
    n_v = heads * 128
    pay2 = jnp.concatenate([split(raw[:, :GROUP * cols]), spread(raw[:, GROUP * cols:])], 2)
    x2 = trade(pay2.reshape(GROUP * tok, -1))
    x3 = along_groups(x1[:, n_v + HALF:], -1)
    kq_other = core_swap(jnp.concatenate([x1[:, n_v:n_v + HALF], x1[:, 2 * n_v + HALF:]], 1))
    kp_other = core_swap(x2[:, n_v:])
    qn_other = core_swap(x3[:, n_v:])

    mix = lax.dynamic_slice_in_dim(mixing, place * heads, heads, 0)
    mix = mix.reshape(heads, 2, 2, 128).transpose(0, 2, 1, 3)
    mix = jnp.where(core == 0, mix, mix[:, ::-1]).reshape(heads, 1, width)
    first = (me < GROUP).astype(jnp.int32).reshape(1)

    stats, dq_mine, dq_other, dk, dv, dmix = own_part(scale, first, mix, x1, kq_other, x2, kp_other)
    next_stats = along_groups(stats, -1)
    dk_mine, dk_other, dv = next_part(scale, mix, x1, kq_other, x3, qn_other, next_stats, dk, dv)

    dq_sum = dq_mine + core_swap(dq_other)
    dk_sum = dk_mine + core_swap(dk_other)
    back = trade(jnp.concatenate(
        [dv, dk_sum.astype(jnp.bfloat16), dq_sum.astype(jnp.bfloat16)], 1))
    back = back.reshape(GROUP, tok, -1)
    d_values = back[:, :, :n_v].transpose(1, 0, 2).reshape(tok, GROUP * n_v)
    sums = jnp.sum(back[:, :, n_v:].astype(jnp.float32), 0).reshape(tok, 2, 2, 128)
    keep = lax.dynamic_index_in_dim(sums, y_lo, 2, keepdims=False)
    give = lax.dynamic_index_in_dim(sums, 1 - y_lo, 2, keepdims=False)
    got = lax.ppermute(give.reshape(tok, 256), "head", [(0, 2), (1, 3), (2, 0), (3, 1)])
    done = (keep.reshape(tok, 256) + got).astype(jnp.bfloat16)
    d_key = done[:, :128]
    d_query = done[:, 128:]

    dmix = dmix.reshape(heads, width)
    step = GROUP
    while step < peers:
        dmix = dmix + lax.ppermute(dmix, "seq", [(i, i ^ step) for i in range(peers)])
        step *= 2
    wide = lax.dynamic_update_slice_in_dim(
        jnp.zeros((GROUP * heads, width), jnp.float32), dmix, place * heads, 0)
    for step in (1, 2):
        wide = wide + lax.ppermute(wide, "seq", [(i, i ^ step) for i in range(peers)])
    wide = wide.reshape(GROUP * heads, 2, 2, 128)
    wide = jnp.where(core == 0, wide, wide[:, ::-1])
    d_mixing = wide.transpose(0, 2, 1, 3).reshape(GROUP * heads, width)
    return d_query, d_key, d_values, d_mixing


def solution(mesh):
    placed = (P("seq", None), P("seq", None), P("head", None), P("seq", "head"), P("seq", "head"))
    return jax.shard_map(
        per_device,
        mesh=mesh,
        in_specs=placed,
        out_specs=(P("seq", "head"), P("seq", "head"), P("seq", "head"), P("head", None)),
        check_vma=False,
    )
```

time: 628 us -> 128 us (0.20)
  the two profiles are of different devices: /device:TPU:128 before, /device:TPU:8 now
where the time goes in v1:
time: 128 us; the launch traced here: 126 us
  waiting for transfers between devices  52.4 us (41%)
  starting transfers between devices  43.3 us (34%)
  Pallas kernels  17.4 us (14%)
  local copies, waits for them, and re-layouts  7.85 us (6%)
  other arithmetic  4.51 us (4%)
    ppermute x3, waiting for transfers between devices, along_groups(): return lax.ppermute(x, 'seq', pairs)  28.1 us
    ppermute x4, starting transfers between devices, per_device(): lax.ppermute(dmix, 'seq', [(i, i ^ step) for i in range(peers)])  16.3 us
    all_to_all x3, starting transfers between devices, trade(): return lax.all_to_all(x, 'seq', 0, 0, axis_index_groups=groups, tiled=True)  12.3 us
    pallas_call x1, Pallas kernels, own_part(): pl.pallas_call(functools.partial(own_kernel, scale), grid=(heads,), in_sp...  11.4 us
    all_to_all x3, waiting for transfers between devices, trade(): return lax.all_to_all(x, 'seq', 0, 0, axis_index_groups=groups, tiled=True)  11.3 us
    ppermute x3, starting transfers between devices, along_groups(): return lax.ppermute(x, 'seq', pairs)  6.81 us
    ppermute x4, waiting for transfers between devices, per_device(): lax.ppermute(dmix, 'seq', [(i, i ^ step) for i in range(peers)])  6.43 us
    pallas_call x1, Pallas kernels, next_part(): pl.pallas_call(functools.partial(next_kernel, scale), grid=(heads,), in_s...  5.96 us
  transfers between devices with their start and end apart: 18, of which 11 were waited for; matrix products, arithmetic and copies ran while one was open for 5% of the time, Pallas kernels for 14%

profile of v1, /device:TPU:8, one launch (start us, length us, event | category | flops | bytes accessed | tf_op | source)
XLA Modules:
  0.0 126.5 jit_solution(18033860475877086277)
XLA Ops:
  0.6 0.0 copy-start
  0.7 1.1 copy.38
  1.8 0.1 copy.39
  1.9 1.1 copy.61
  3.1 0.4 dynamic-slice_reduce_fusion
  3.6 1.3 %pad_maximum_fusion = bf16[4,128,1536]{2,1,0:T(8,128)(2,1)} fusion(bf16[4,128,256]{2,1,0:T(8,128)(2,1)S(1)} %broadcast_in_dim.26, bf16[4,128,512]{2,1,0:T(8,128)(2,1)S(1)} %bitcast.68, bf16[4,128,256]{2,1,0:T(8,128)(2,1)S(1)} %broadcast_in_dim.24, bf16[4,128,512]{2,1,0:T(8,128)(2,1)S(1)} %bitcast.69), kind=kLoop, calls=%fused_computation | loop fusion | flops 6291456 | bytes 3145728 | tf_op jit(solution)/shard_map/concatenate | solution.py:251
  4.9 4.3 %all-to-all-start = ((bf16[4,128,1536]{2,1,0:T(8,128)(2,1)}), bf16[4,128,1536]{2,1,0:T(8,128)(2,1)S(1)}, u32[]{:S(2)}, u32[]{:S(2)}) async-start(bf16[4,128,1536]{2,1,0:T(8,128)(2,1)} %pad_maximum_fusion), calls=%async_computation | async-start | bytes 3145728 | tf_op jit(solution)/shard_map/all_to_all | solution.py:235
  9.2 4.2 %collective-permute-start.3 = (bf16[128,2304]{1,0:T(8,128)(2,1)S(1)}, bf16[128,2304]{1,0:T(8,128)(2,1)S(1)}, u32[]{:S(2)}, u32[]{:S(2)}) collective-permute-start(bf16[128,2304]{1,0:T(8,128)(2,1)S(1)} %pad_maximum_fusion.3), channel_id=1, source_target_pairs={{0,16},{4,20},{8,24},{12,28},{16,32},{20,36},{24,40},{28,44},{32,4... | collective-permute-start | bytes 1769480 | tf_op jit(solution)/shard_map/ppermute | solution.py:229
  13.5 12.3 %collective-permute-done.3 = bf16[128,2304]{1,0:T(8,128)(2,1)S(1)} collective-permute-done((bf16[128,2304]{1,0:T(8,128)(2,1)S(1)}, bf16[128,2304]{1,0:T(8,128)(2,1)S(1)}, u32[]{:S(2)}, u32[]{:S(2)}) %collective-permute-start.3) | collective-permute-done | bytes 589856 | tf_op jit(solution)/shard_map/ppermute | solution.py:229
  25.9 0.9 pad_maximum_fusion.2
  26.8 3.1 %all-to-all-done = bf16[4,128,1536]{2,1,0:T(8,128)(2,1)S(1)} async-done(((bf16[4,128,1536]{2,1,0:T(8,128)(2,1)}), bf16[4,128,1536]{2,1,0:T(8,128)(2,1)S(1)}, u32[]{:S(2)}, u32[]{:S(2)}) %all-to-all-start) | async-done | bytes 1572896 | tf_op jit(solution)/shard_map/all_to_all | solution.py:235
  29.9 3.5 %all-to-all-start.1 = ((bf16[4,128,768]{2,1,0:T(8,128)(2,1)}), bf16[4,128,768]{2,1,0:T(8,128)(2,1)S(1)}, u32[]{:S(2)}, u32[]{:S(2)}) async-start(bf16[4,128,768]{2,1,0:T(8,128)(2,1)} %pad_maximum_fusion.2), calls=%async_computation.1 | async-start | bytes 1572864 | tf_op jit(solution)/shard_map/all_to_all | solution.py:235
  33.4 0.9 slice.46
  34.3 1.3 %collective-permute-start.1 = (bf16[512,768]{1,0:T(8,128)(2,1)}, bf16[512,768]{1,0:T(8,128)(2,1)S(1)}, u32[]{:S(2)}, u32[]{:S(2)}) collective-permute-start(bf16[512,768]{1,0:T(8,128)(2,1)} %slice.46), channel_id=1, source_target_pairs={{16,0},{20,4},{24,8},{28,12},{32,16},{36,20},{40,24},{44,28},{48,3... | collective-permute-start | bytes 2359304 | tf_op jit(solution)/shard_map/ppermute | solution.py:229
  35.7 0.8 pad_maximum_fusion.4
  36.5 8.2 %all-to-all-done.1 = bf16[4,128,768]{2,1,0:T(8,128)(2,1)S(1)} async-done(((bf16[4,128,768]{2,1,0:T(8,128)(2,1)}), bf16[4,128,768]{2,1,0:T(8,128)(2,1)S(1)}, u32[]{:S(2)}, u32[]{:S(2)}) %all-to-all-start.1) | async-done | bytes 786464 | tf_op jit(solution)/shard_map/all_to_all | solution.py:235
  44.7 0.7 slice.50
  45.5 10.5 %collective-permute-done.1.cn_ref.qnm_ref = bf16[512,768]{1,0:T(8,128)(2,1)S(1)} collective-permute-done((bf16[512,768]{1,0:T(8,128)(2,1)}, bf16[512,768]{1,0:T(8,128)(2,1)S(1)}, u32[]{:S(2)}, u32[]{:S(2)}) %collective-permute-start.1) | collective-permute-done | bytes 786464 | tf_op jit(solution)/shard_map/ppermute | solution.py:229
  56.0 0.1 collective-permute-start.2
  56.2 11.4 %shard_map.84 = (f32[4,2,512]{2,1,0:T(2,128)S(1)}, f32[512,256]{1,0:T(8,128)S(1)}, bf16[512,256]{1,0:T(8,128)(2,1)S(1)}, f32[512,512]{1,0:T(8,128)S(1)}, f32[512...) custom-call(s32[1]{0:T(128)} %bitcast.9.first_ref, f32[4,1,512]{2,1,0:T(1,128)S(1)} %bitcast.63, ...), custom_call_target="tpu_custom_call" | custom-call | flops 5000000000 | bytes 8000000 | tf_op jit(solution)/shard_map/pallas_call | solution.py:147
  67.6 1.3 %collective-permute-start.5 = (f32[4,2,512]{2,1,0:T(2,128)S(1)}, f32[4,2,512]{2,1,0:T(2,128)S(1)}, u32[]{:S(2)}, u32[]{:S(2)}) collective-permute-start(f32[4,2,512]{2,1,0:T(2,128)S(1)} %get-tuple-element.13), channel_id=1, source_target_pairs={{16,0},{20,4},{24,8},{28,12},{32,16},{36,20},{40,24},{44,28},{48,3... | collective-permute-start | bytes 49160 | tf_op jit(solution)/shard_map/ppermute | solution.py:229
  68.9 0.5 collective-permute-start.7
  69.5 5.3 %collective-permute-done.5.stats_ref = f32[4,2,512]{2,1,0:T(2,128)S(1)} collective-permute-done((f32[4,2,512]{2,1,0:T(2,128)S(1)}, f32[4,2,512]{2,1,0:T(2,128)S(1)}, u32[]{:S(2)}, u32[]{:S(2)}) %collective-permute-start.5) | collective-permute-done | bytes 16416 | tf_op jit(solution)/shard_map/ppermute | solution.py:229
  74.8 6.0 %shard_map.85 = (f32[512,256]{1,0:T(8,128)S(1)}, bf16[512,256]{1,0:T(8,128)(2,1)S(1)}, bf16[512,512]{1,0:T(8,128)(2,1)S(1)}) custom-call(f32[4,1,512]{2,1,0:T(1,128)S(1)} %bitcast.64, bf16[512,1536]{1,0:T(8,128)(2,1)S(1)} %bitcast.58, bf16[512,1536]{1,0:T(8,128)(2,1)S(1)} %bitcast.59, bf16[512,512]{1,0:T(8,128)(2,1)} %collective-permute-done.ko_ref.qo_ref, ...), custom_call_target="tpu_custom_call" | custom-call | flops 2500000000 | bytes 7000000 | tf_op jit(solution)/shard_map/pallas_call | solution.py:189
  80.7 0.1 collective-permute-start.6
  80.8 4.2 %collective-permute-start.9 = (f32[4,512]{1,0:T(4,128)S(1)}, f32[4,512]{1,0:T(4,128)S(1)}, u32[]{:S(2)}, u32[]{:S(2)}) collective-permute-start(f32[4,512]{1,0:T(4,128)S(1)} %bitcast.80), channel_id=1, source_target_pairs={{0,16},{4,20},{8,24},{12,28},{16,0},{20,4},{24,8},{28,12},{32,48},... | collective-permute-start | bytes 24584 | tf_op jit(solution)/shard_map/ppermute | solution.py:287
  85.0 0.1 add_convert_fusion
  85.1 0.1 add_convert_fusion.1
  85.2 1.1 pad_maximum_fusion.1
  86.3 4.5 %all-to-all-start.2 = ((bf16[4,128,1024]{2,1,0:T(8,128)(2,1)}), bf16[4,128,1024]{2,1,0:T(8,128)(2,1)S(1)}, u32[]{:S(2)}, u32[]{:S(2)}) async-start(bf16[4,128,1024]{2,1,0:T(8,128)(2,1)} %bitcast.12), calls=%async_computation.2 | async-start | bytes 2097152 | tf_op jit(solution)/shard_map/all_to_all | solution.py:235
  90.8 2.0 %collective-permute-start.10 = (f32[4,512]{1,0:T(4,128)S(1)}, f32[4,512]{1,0:T(4,128)S(1)}, u32[]{:S(2)}, u32[]{:S(2)}) collective-permute-start(f32[4,512]{1,0:T(4,128)S(1)} %fusion.2), channel_id=1, source_target_pairs={{0,32},{4,36},{8,40},{12,44},{16,48},{20,52},{24,56},{28,60},{32,0... | collective-permute-start | bytes 24584 | tf_op jit(solution)/shard_map/ppermute | solution.py:287
  92.8 1.7 %collective-permute-done.10 = f32[4,512]{1,0:T(4,128)S(1)} collective-permute-done((f32[4,512]{1,0:T(4,128)S(1)}, f32[4,512]{1,0:T(4,128)S(1)}, u32[]{:S(2)}, u32[]{:S(2)}) %collective-permute-start.10) | collective-permute-done | bytes 8224 | tf_op jit(solution)/shard_map/ppermute | solution.py:287
  94.5 5.6 %collective-permute-start.11 = (f32[4,512]{1,0:T(4,128)S(1)}, f32[4,512]{1,0:T(4,128)S(1)}, u32[]{:S(2)}, u32[]{:S(2)}) collective-permute-start(f32[4,512]{1,0:T(4,128)S(1)} %add.63), channel_id=1, source_target_pairs={{0,64},{4,68},{8,72},{12,76},{16,80},{20,84},{24,88},{28,92},{32,9... | collective-permute-start | bytes 24584 | tf_op jit(solution)/shard_map/ppermute | solution.py:287
  100.1 1.6 %collective-permute-done.11 = f32[4,512]{1,0:T(4,128)S(1)} collective-permute-done((f32[4,512]{1,0:T(4,128)S(1)}, f32[4,512]{1,0:T(4,128)S(1)}, u32[]{:S(2)}, u32[]{:S(2)}) %collective-permute-start.11) | collective-permute-done | bytes 8224 | tf_op jit(solution)/shard_map/ppermute | solution.py:287
  101.7 4.5 %collective-permute-start.12 = (f32[4,512]{1,0:T(4,128)S(1)}, f32[4,512]{1,0:T(4,128)S(1)}, u32[]{:S(2)}, u32[]{:S(2)}) collective-permute-start(f32[4,512]{1,0:T(4,128)S(1)} %add.64), channel_id=1, source_target_pairs={{0,128},{4,132},{8,136},{12,140},{16,144},{20,148},{24,152},{28,15... | collective-permute-start | bytes 24584 | tf_op jit(solution)/shard_map/ppermute | solution.py:287
  106.3 3.1 %collective-permute-done.12 = f32[4,512]{1,0:T(4,128)S(1)} collective-permute-done((f32[4,512]{1,0:T(4,128)S(1)}, f32[4,512]{1,0:T(4,128)S(1)}, u32[]{:S(2)}, u32[]{:S(2)}) %collective-permute-start.12) | collective-permute-done | bytes 8224 | tf_op jit(solution)/shard_map/ppermute | solution.py:287
  109.4 2.1 %collective-permute-start.13 = (f32[16,512]{1,0:T(8,128)S(1)}, f32[16,512]{1,0:T(8,128)S(1)}, u32[]{:S(2)}, u32[]{:S(2)}) collective-permute-start(f32[16,512]{1,0:T(8,128)S(1)} %get-tuple-element.30), channel_id=1, source_target_pairs={{0,4},{4,0},{8,12},{12,8},{16,20},{20,16},{24,28},{28,24},{32,36},... | collective-permute-start | bytes 98312 | tf_op jit(solution)/shard_map/ppermute | solution.py:292
  111.4 1.9 %collective-permute-done.13 = f32[16,512]{1,0:T(8,128)S(1)} collective-permute-done((f32[16,512]{1,0:T(8,128)S(1)}, f32[16,512]{1,0:T(8,128)S(1)}, u32[]{:S(2)}, u32[]{:S(2)}) %collective-permute-start.13) | collective-permute-done | bytes 32800 | tf_op jit(solution)/shard_map/ppermute | solution.py:292
  113.4 3.7 %collective-permute-start.14 = (f32[16,512]{1,0:T(8,128)S(1)}, f32[16,512]{1,0:T(8,128)S(1)}, u32[]{:S(2)}, u32[]{:S(2)}) collective-permute-start(f32[16,512]{1,0:T(8,128)S(1)} %add_dynamic-update-slice_fusion), channel_id=1, source_target_pairs={{0,8},{4,12},{8,0},{12,4},{16,24},{20,28},{24,16},{28,20},{32,40},... | collective-permute-start | bytes 98312 | tf_op jit(solution)/shard_map/ppermute | solution.py:292
  117.0 1.9 %collective-permute-done.14 = f32[16,512]{1,0:T(8,128)S(1)} collective-permute-done((f32[16,512]{1,0:T(8,128)S(1)}, f32[16,512]{1,0:T(8,128)S(1)}, u32[]{:S(2)}, u32[]{:S(2)}) %collective-permute-start.14) | collective-permute-done | bytes 32800 | tf_op jit(solution)/shard_map/ppermute | solution.py:292
  119.0 0.6 reshape.91
  119.7 0.1 convert_reduce_fusion
  119.8 0.1 copy.41
  119.9 1.4 %collective-permute-start.8 = (f32[128,256]{0,1:T(8,128)S(1)}, f32[128,256]{0,1:T(8,128)S(1)}, u32[]{:S(2)}, u32[]{:S(2)}) collective-permute-start(f32[128,256]{0,1:T(8,128)S(1)} %bitcast.78), channel_id=1, source_target_pairs={{0,2},{1,3},{2,0},{3,1},{4,6},{5,7},{6,4},{7,5},{8,10},{9,11},{10,... | collective-permute-start | bytes 393224 | tf_op jit(solution)/shard_map/ppermute | solution.py:279
  121.4 0.8 copy.51
  122.2 2.7 %collective-permute-done.8 = f32[128,256]{0,1:T(8,128)S(1)} collective-permute-done((f32[128,256]{0,1:T(8,128)S(1)}, f32[128,256]{0,1:T(8,128)S(1)}, u32[]{:S(2)}, u32[]{:S(2)}) %collective-permute-start.8) | collective-permute-done | bytes 131104 | tf_op jit(solution)/shard_map/ppermute | solution.py:279
  125.0 0.7 copy.44
  125.7 0.7 copy.45
  (45 shorter events, 0.6 us)
Async XLA Ops:
  0.6 44.8 %copy-start = (f32[16,512]{1,0:T(8,128)S(1)}, f32[16,512]{1,0:T(8,128)}, u32[]{:S(2)}) copy-start(f32[16,512]{1,0:T(8,128)} %param.7) | copy-start | bytes 98308
  0.6 2.4 %copy-start.2 = (bf16[128,512]{1,0:T(8,128)(2,1)S(1)}, bf16[128,512]{1,0:T(8,128)(2,1)}, u32[]{:S(2)}) copy-start(bf16[128,512]{1,0:T(8,128)(2,1)} %param.6) | copy-start | bytes 393220
  0.7 2.9 %copy-start.1 = (bf16[128,2048]{1,0:T(8,128)(2,1)S(1)}, bf16[128,2048]{1,0:T(8,128)(2,1)}, u32[]{:S(2)}) copy-start(bf16[128,2048]{1,0:T(8,128)(2,1)} %param.8) | copy-start | bytes 1572868
  4.9 25.0 %all-to-all-start = ((bf16[4,128,1536]{2,1,0:T(8,128)(2,1)}), bf16[4,128,1536]{2,1,0:T(8,128)(2,1)S(1)}, u32[]{:S(2)}, u32[]{:S(2)}) async-start(bf16[4,128,1536]{2,1,0:T(8,128)(2,1)} %pad_maximum_fusion), calls=%async_computation | async-start | bytes 3145728 | tf_op jit(solution)/shard_map/all_to_all | solution.py:235
  9.2 16.5 %collective-permute-start.3 = (bf16[128,2304]{1,0:T(8,128)(2,1)S(1)}, bf16[128,2304]{1,0:T(8,128)(2,1)S(1)}, u32[]{:S(2)}, u32[]{:S(2)}) collective-permute-start(bf16[128,2304]{1,0:T(8,128)(2,1)S(1)} %pad_maximum_fusion.3), channel_id=1, source_target_pairs={{0,16},{4,20},{8,24},{12,28},{16,32},{20,36},{24,40},{28,44},{32,4... | collective-permute-start | bytes 1769480 | tf_op jit(solution)/shard_map/ppermute | solution.py:229
  29.9 14.8 %all-to-all-start.1 = ((bf16[4,128,768]{2,1,0:T(8,128)(2,1)}), bf16[4,128,768]{2,1,0:T(8,128)(2,1)S(1)}, u32[]{:S(2)}, u32[]{:S(2)}) async-start(bf16[4,128,768]{2,1,0:T(8,128)(2,1)} %pad_maximum_fusion.2), calls=%async_computation.1 | async-start | bytes 1572864 | tf_op jit(solution)/shard_map/all_to_all | solution.py:235
  34.3 21.7 %collective-permute-start.1 = (bf16[512,768]{1,0:T(8,128)(2,1)}, bf16[512,768]{1,0:T(8,128)(2,1)S(1)}, u32[]{:S(2)}, u32[]{:S(2)}) collective-permute-start(bf16[512,768]{1,0:T(8,128)(2,1)} %slice.46), channel_id=1, source_target_pairs={{16,0},{20,4},{24,8},{28,12},{32,16},{36,20},{40,24},{44,28},{48,3... | collective-permute-start | bytes 2359304 | tf_op jit(solution)/shard_map/ppermute | solution.py:229
  36.5 19.7 %collective-permute-start = (bf16[512,512]{1,0:T(8,128)(2,1)}, bf16[512,512]{1,0:T(8,128)(2,1)}, u32[]{:S(2)}, u32[]{:S(2)}) collective-permute-start(bf16[512,512]{1,0:T(8,128)(2,1)} %pad_maximum_fusion.4), channel_id=1, source_target_pairs={{0,1},{1,0},{2,3},{3,2},{4,5},{5,4},{6,7},{7,6},{8,9},{9,8},{10,11... | collective-permute-start | bytes 1572872 | tf_op jit(solution)/shard_map/ppermute | solution.py:232
  45.5 10.7 %collective-permute-start.4 = (bf16[512,256]{1,0:T(8,128)(2,1)}, bf16[512,256]{1,0:T(8,128)(2,1)S(1)}, u32[]{:S(2)}, u32[]{:S(2)}) collective-permute-start(bf16[512,256]{1,0:T(8,128)(2,1)} %slice.50), channel_id=1, source_target_pairs={{0,1},{1,0},{2,3},{3,2},{4,5},{5,4},{6,7},{7,6},{8,9},{9,8},{10,11... | collective-permute-start | bytes 786440 | tf_op jit(solution)/shard_map/ppermute | solution.py:232
  56.0 18.7 %collective-permute-start.2 = (bf16[512,256]{1,0:T(8,128)(2,1)S(1)}, bf16[512,256]{1,0:T(8,128)(2,1)S(1)}, u32[]{:S(2)}, u32[]{:S(2)}) collective-permute-start(bf16[512,256]{1,0:T(8,128)(2,1)S(1)} %slice.47), channel_id=1, source_target_pairs={{0,1},{1,0},{2,3},{3,2},{4,5},{5,4},{6,7},{7,6},{8,9},{9,8},{10,11... | collective-permute-start | bytes 786440 | tf_op jit(solution)/shard_map/ppermute | solution.py:232
  67.6 7.1 %collective-permute-start.5 = (f32[4,2,512]{2,1,0:T(2,128)S(1)}, f32[4,2,512]{2,1,0:T(2,128)S(1)}, u32[]{:S(2)}, u32[]{:S(2)}) collective-permute-start(f32[4,2,512]{2,1,0:T(2,128)S(1)} %get-tuple-element.13), channel_id=1, source_target_pairs={{16,0},{20,4},{24,8},{28,12},{32,16},{36,20},{40,24},{44,28},{48,3... | collective-permute-start | bytes 49160 | tf_op jit(solution)/shard_map/ppermute | solution.py:229
  68.9 16.1 %collective-permute-start.7 = (bf16[512,256]{1,0:T(8,128)(2,1)S(1)}, bf16[512,256]{1,0:T(8,128)(2,1)S(1)}, u32[]{:S(2)}, u32[]{:S(2)}) collective-permute-start(bf16[512,256]{1,0:T(8,128)(2,1)S(1)} %get-tuple-element.20), channel_id=1, source_target_pairs={{0,1},{1,0},{2,3},{3,2},{4,5},{5,4},{6,7},{7,6},{8,9},{9,8},{10,11... | collective-permute-start | bytes 786440 | tf_op jit(solution)/shard_map/ppermute | solution.py:232
  80.7 4.4 %collective-permute-start.6 = (bf16[512,256]{1,0:T(8,128)(2,1)S(1)}, bf16[512,256]{1,0:T(8,128)(2,1)S(1)}, u32[]{:S(2)}, u32[]{:S(2)}) collective-permute-start(bf16[512,256]{1,0:T(8,128)(2,1)S(1)} %get-tuple-element.18), channel_id=1, source_target_pairs={{0,1},{1,0},{2,3},{3,2},{4,5},{5,4},{6,7},{7,6},{8,9},{9,8},{10,11... | collective-permute-start | bytes 786440 | tf_op jit(solution)/shard_map/ppermute | solution.py:232
  80.8 9.9 %collective-permute-start.9 = (f32[4,512]{1,0:T(4,128)S(1)}, f32[4,512]{1,0:T(4,128)S(1)}, u32[]{:S(2)}, u32[]{:S(2)}) collective-permute-start(f32[4,512]{1,0:T(4,128)S(1)} %bitcast.80), channel_id=1, source_target_pairs={{0,16},{4,20},{8,24},{12,28},{16,0},{20,4},{24,8},{28,12},{32,48},... | collective-permute-start | bytes 24584 | tf_op jit(solution)/shard_map/ppermute | solution.py:287
  86.3 33.4 %all-to-all-start.2 = ((bf16[4,128,1024]{2,1,0:T(8,128)(2,1)}), bf16[4,128,1024]{2,1,0:T(8,128)(2,1)S(1)}, u32[]{:S(2)}, u32[]{:S(2)}) async-start(bf16[4,128,1024]{2,1,0:T(8,128)(2,1)} %bitcast.12), calls=%async_computation.2 | async-start | bytes 2097152 | tf_op jit(solution)/shard_map/all_to_all | solution.py:235
  90.8 3.7 %collective-permute-start.10 = (f32[4,512]{1,0:T(4,128)S(1)}, f32[4,512]{1,0:T(4,128)S(1)}, u32[]{:S(2)}, u32[]{:S(2)}) collective-permute-start(f32[4,512]{1,0:T(4,128)S(1)} %fusion.2), channel_id=1, source_target_pairs={{0,32},{4,36},{8,40},{12,44},{16,48},{20,52},{24,56},{28,60},{32,0... | collective-permute-start | bytes 24584 | tf_op jit(solution)/shard_map/ppermute | solution.py:287
  94.5 7.2 %collective-permute-start.11 = (f32[4,512]{1,0:T(4,128)S(1)}, f32[4,512]{1,0:T(4,128)S(1)}, u32[]{:S(2)}, u32[]{:S(2)}) collective-permute-start(f32[4,512]{1,0:T(4,128)S(1)} %add.63), channel_id=1, source_target_pairs={{0,64},{4,68},{8,72},{12,76},{16,80},{20,84},{24,88},{28,92},{32,9... | collective-permute-start | bytes 24584 | tf_op jit(solution)/shard_map/ppermute | solution.py:287
  101.7 7.6 %collective-permute-start.12 = (f32[4,512]{1,0:T(4,128)S(1)}, f32[4,512]{1,0:T(4,128)S(1)}, u32[]{:S(2)}, u32[]{:S(2)}) collective-permute-start(f32[4,512]{1,0:T(4,128)S(1)} %add.64), channel_id=1, source_target_pairs={{0,128},{4,132},{8,136},{12,140},{16,144},{20,148},{24,152},{28,15... | collective-permute-start | bytes 24584 | tf_op jit(solution)/shard_map/ppermute | solution.py:287
  109.4 4.0 %collective-permute-start.13 = (f32[16,512]{1,0:T(8,128)S(1)}, f32[16,512]{1,0:T(8,128)S(1)}, u32[]{:S(2)}, u32[]{:S(2)}) collective-permute-start(f32[16,512]{1,0:T(8,128)S(1)} %get-tuple-element.30), channel_id=1, source_target_pairs={{0,4},{4,0},{8,12},{12,8},{16,20},{20,16},{24,28},{28,24},{32,36},... | collective-permute-start | bytes 98312 | tf_op jit(solution)/shard_map/ppermute | solution.py:292
  113.4 5.6 %collective-permute-start.14 = (f32[16,512]{1,0:T(8,128)S(1)}, f32[16,512]{1,0:T(8,128)S(1)}, u32[]{:S(2)}, u32[]{:S(2)}) collective-permute-start(f32[16,512]{1,0:T(8,128)S(1)} %add_dynamic-update-slice_fusion), channel_id=1, source_target_pairs={{0,8},{4,12},{8,0},{12,4},{16,24},{20,28},{24,16},{28,20},{32,40},... | collective-permute-start | bytes 98312 | tf_op jit(solution)/shard_map/ppermute | solution.py:292
  119.9 5.1 %collective-permute-start.8 = (f32[128,256]{0,1:T(8,128)S(1)}, f32[128,256]{0,1:T(8,128)S(1)}, u32[]{:S(2)}, u32[]{:S(2)}) collective-permute-start(f32[128,256]{0,1:T(8,128)S(1)} %bitcast.78), channel_id=1, source_target_pairs={{0,2},{1,3},{2,0},{3,1},{4,6},{5,7},{6,4},{7,5},{8,10},{9,11},{10,... | collective-permute-start | bytes 393224 | tf_op jit(solution)/shard_map/ppermute | solution.py:279

commit v2 on v1

v2 whole, which is shorter than its diff:
```python
import functools
import math

import jax
import jax.numpy as jnp
from jax import lax
from jax.experimental import pallas as pl
from jax.experimental.pallas import tpu as pltpu
from jax.sharding import PartitionSpec as P

GROUP = 4
HALF = 256
NEG = -1e30
LOG2E = 1.4426950408889634

NT = (((1,), (1,)), ((), ()))
NN = (((1,), (0,)), ((), ()))
TN = (((0,), (0,)), ((), ()))


def dot(a, b, dims):
    return lax.dot_general(a, b, dims, preferred_element_type=jnp.float32)


def blocks_of(at_ref):
    core = at_ref[0]
    return core, 2 + core, 1 - core, 3 - core


def rows_from(at_ref, by):
    src = lax.rem(at_ref[1] + GROUP - by, GROUP)
    return pl.ds(pl.multiple_of(src * 128, 128), 128)


def scores_kernel(scale, at_ref, mix_ref, v_ref, km_ref, c_ref, qm_ref, ko_ref, qo_ref,
                  vp0_ref, vp1_ref, vp2_ref, vp3_ref, kpm_ref, kpo_ref,
                  stats_ref, grad_ref, w_ref, k_all_ref, q_all_ref, k_all, q_all, v_all):
    head = pl.program_id(0)
    span = q_all.shape[0]
    tile = span // 2
    half = km_ref.shape[1]

    @pl.when(head == 0)
    def _():
        k_all[:span, :half] = kpm_ref[...]
        k_all[:span, half:] = kpo_ref[...]
        k_all[span:, :half] = km_ref[...]
        k_all[span:, half:] = ko_ref[...]
        q_all[:, :half] = qm_ref[...]
        q_all[:, half:] = qo_ref[...]
        k_all_ref[...] = k_all[...]
        q_all_ref[...] = q_all[...]

    for e, ref in enumerate((vp0_ref, vp1_ref, vp2_ref, vp3_ref)):
        v_all[rows_from(at_ref, e), :] = ref[...]
    v_all[span:, :] = v_ref[...]
    mix = mix_ref[0]
    is_first = at_ref[2] == 0
    row = lax.broadcasted_iota(jnp.int32, (tile, tile), 0)
    col = lax.broadcasted_iota(jnp.int32, (tile, tile), 1)
    for t in (0, 1):
        lo = t * tile
        mq = (q_all[lo:lo + tile, :].astype(jnp.float32) * mix).astype(jnp.bfloat16)
        up = c_ref[lo:lo + tile, :]
        s = dot(k_all[lo:lo + 3 * tile, :], mq, NT) * (scale * LOG2E)
        d = dot(v_all[lo:lo + 3 * tile, :], up, NT)
        s0 = jnp.where((row > col) & jnp.logical_not(is_first), s[:tile], NEG)
        s1 = s[tile:2 * tile]
        if t == 0:
            s1 = jnp.where(is_first, NEG, s1)
        s2 = jnp.where(row <= col, s[2 * tile:], NEG)
        top = jnp.max(jnp.maximum(jnp.maximum(s0, s1), s2), 0, keepdims=True)
        p = [jnp.exp2(part - top) for part in (s0, s1, s2)]
        total = jnp.sum(p[0] + p[1] + p[2], 0, keepdims=True)
        inv = 1.0 / total
        ds = [d[:tile], d[tile:2 * tile], d[2 * tile:]]
        delta = jnp.sum(p[0] * ds[0] + p[1] * ds[1] + p[2] * ds[2], 0, keepdims=True) * inv
        stats_ref[0, 0:1, lo:lo + tile] = top + jnp.log2(total)
        stats_ref[0, 1:2, lo:lo + tile] = delta
        for i in range(3):
            w = p[i] * inv
            grad_ref[0, t, i * tile:(i + 1) * tile, :] = (w * (ds[i] - delta)).astype(jnp.bfloat16)
            if i == 2:
                w_ref[0, 2 * t, :, :] = w.astype(jnp.bfloat16)
            if i == 1 and t == 1:
                w_ref[0, 1, :, :] = w.astype(jnp.bfloat16)


def query_kernel(scale, at_ref, mix_ref, k_ref, q_ref, grad_ref, dqm_ref, dqo_ref, dmix_ref, dq_acc):
    head = pl.program_id(0)
    span, width = q_ref.shape
    tile = span // 2

    @pl.when(head == 0)
    def _():
        dq_acc[...] = jnp.zeros_like(dq_acc)

    mix = mix_ref[0]
    dmix = jnp.zeros((1, width), jnp.float32)
    for t in (0, 1):
        lo = t * tile
        qg = dot(grad_ref[0, t], k_ref[lo:lo + 3 * tile, :], TN) * scale
        dq_acc[lo:lo + tile, :] += qg * mix
        dmix = dmix + jnp.sum(qg * q_ref[lo:lo + tile, :].astype(jnp.float32), 0, keepdims=True)
    for m, block in enumerate(blocks_of(at_ref)):
        dmix_ref[0, :, pl.ds(pl.multiple_of(block * 128, 128), 128)] = dmix[:, m * 128:(m + 1) * 128]

    @pl.when(head == pl.num_programs(0) - 1)
    def _():
        dqm_ref[...] = dq_acc[:, :width // 2]
        dqo_ref[...] = dq_acc[:, width // 2:].astype(jnp.bfloat16)


def key_kernel(mix_ref, c_ref, q_ref, grad_ref, w_ref, dk_ref, dv_ref):
    head = pl.program_id(0)
    span = q_ref.shape[0]
    tile = span // 2

    @pl.when(head == 0)
    def _():
        dk_ref[...] = jnp.zeros_like(dk_ref)

    mix = mix_ref[0]
    mq = (q_ref[...].astype(jnp.float32) * mix).astype(jnp.bfloat16)
    dk_ref[...] += dot(grad_ref[0, 1, tile:, :], mq[tile:], NN)
    dk_ref[:tile, :] += dot(grad_ref[0, 0, 2 * tile:, :], mq[:tile], NN)
    dv_ref[tile:, :] = dot(w_ref[0, 2], c_ref[tile:, :], NN)
    dv_ref[:tile, :] = dot(w_ref[0, 1], c_ref[tile:, :], NN) + dot(w_ref[0, 0], c_ref[:tile, :], NN)


def next_kernel(scale, mix_ref, v_ref, km_ref, ko_ref, cn_ref, qnm_ref, qno_ref, stats_ref,
                dk_ref, dv_ref, dkm_ref, dko_ref, dvo_ref, k_all, q_all, dk_acc):
    head = pl.program_id(0)
    span = q_all.shape[0]
    tile = span // 2
    half = km_ref.shape[1]

    @pl.when(head == 0)
    def _():
        k_all[:, :half] = km_ref[...]
        k_all[:, half:] = ko_ref[...]
        q_all[:, :half] = qnm_ref[...]
        q_all[:, half:] = qno_ref[...]
        dk_acc[...] = dk_ref[...]

    mix = mix_ref[0]
    row = lax.broadcasted_iota(jnp.int32, (tile, tile), 0)
    col = lax.broadcasted_iota(jnp.int32, (tile, tile), 1)
    dv = [dv_ref[:tile, :], dv_ref[tile:, :]]
    for t in (0, 1):
        lo = t * tile
        mq = (q_all[lo:lo + tile, :].astype(jnp.float32) * mix).astype(jnp.bfloat16)
        up = cn_ref[lo:lo + tile, :]
        lse = stats_ref[0, 0:1, lo:lo + tile]
        delta = stats_ref[0, 1:2, lo:lo + tile]
        s = dot(k_all[lo:, :], mq, NT) * (scale * LOG2E)
        d = dot(v_ref[lo:, :], up, NT)
        w = jnp.exp2(jnp.where(row > col, s[:tile] - lse, NEG))
        if t == 0:
            w = jnp.concatenate([w, jnp.exp2(s[tile:] - lse)], 0)
        grad = (w * (d - delta)).astype(jnp.bfloat16)
        add = dot(w.astype(jnp.bfloat16), up, NN)
        if t == 0:
            dv = [dv[0] + add[:tile], dv[1] + add[tile:]]
        else:
            dv[1] = dv[1] + add
        dk_acc[lo:, :] += dot(grad, mq, NN)
    dvo_ref[:tile, :] = dv[0].astype(jnp.bfloat16)
    dvo_ref[tile:, :] = dv[1].astype(jnp.bfloat16)

    @pl.when(head == pl.num_programs(0) - 1)
    def _():
        dkm_ref[...] = dk_acc[:, :half] * scale
        dko_ref[...] = (dk_acc[:, half:] * scale).astype(jnp.bfloat16)


def load_kernel(at_ref, v_ref, c_ref, k_ref, q_ref, own0_ref, own1_ref, own2_ref, own3_ref,
                ahead_ref, k_in, q_in, sems):
    core, place = at_ref[0], at_ref[1]
    wide = v_ref.shape[1]
    cols = wide // GROUP
    pending = []

    def send(src, dst):
        copy = pltpu.make_async_copy(src, dst, sems.at[len(pending)])
        copy.start()
        pending.append(copy)
        return copy

    shared = [send(k_ref, k_in), send(q_ref, q_in)]
    send(v_ref, ahead_ref.at[:, :wide])
    owns = (own0_ref, own1_ref, own2_ref, own3_ref)
    for e, own in enumerate(owns):
        src = pl.ds(pl.multiple_of(lax.rem(place + e, GROUP) * cols, 128), cols)
        send(v_ref.at[:, src], own.at[:, :cols])
        send(c_ref.at[:, src], own.at[:, cols + 2 * HALF:])
    for copy in shared:
        copy.wait()
    for m in range(2):
        src = pl.ds(pl.multiple_of((2 * m + core) * 128, 128), 128)
        k_block, q_block = k_in[:, src], q_in[:, src]
        ahead_ref[:, wide + m * 128:wide + (m + 1) * 128] = k_block
        for own in owns:
            own[:, cols + m * 128:cols + (m + 1) * 128] = k_block
            own[:, cols + HALF + m * 128:cols + HALF + (m + 1) * 128] = q_block
    for copy in pending[2:]:
        copy.wait()


def split_kernel(at_ref, raw_ref, *hops):
    cols = hops[0].shape[1] - HALF
    for e, hop in enumerate(hops):
        src = lax.rem(at_ref[1] + e, GROUP) * cols
        hop[:, :cols] = raw_ref[:, pl.ds(pl.multiple_of(src, 128), cols)]
        hop[:, cols:] = raw_ref[:, GROUP * cols:]


def gather_kernel(at_ref, p0_ref, p1_ref, p2_ref, p3_ref, vk_ref, qc_ref, kq_ref):
    half = vk_ref.shape[1]
    for e, ref in enumerate((p0_ref, p1_ref, p2_ref, p3_ref)):
        rows = rows_from(at_ref, e)
        vk_ref[rows, :] = ref[:, :half]
        qc_ref[rows, :] = ref[:, half:]
        kq_ref[rows, :] = ref[:, half - HALF:half + HALF]


def collect_kernel(at_ref, mixing_ref, k0_ref, k1_ref, k2_ref, k3_ref, k_ref, mix_ref):
    core, place = at_ref[0], at_ref[1]
    for e, ref in enumerate((k0_ref, k1_ref, k2_ref, k3_ref)):
        k_ref[rows_from(at_ref, e), :] = ref[...]
    for h in range(mix_ref.shape[0]):
        row = mixing_ref[pl.ds(place * mix_ref.shape[0] + h, 1), :]
        blocks = [row[:, i * 128:(i + 1) * 128] for i in range(4)]
        for m, (even, odd) in enumerate(((0, 1), (2, 3), (1, 0), (3, 2))):
            mix_ref[h, :, m * 128:(m + 1) * 128] = jnp.where(core == 0, blocks[even], blocks[odd])


def pack_kernel(at_ref, dv_ref, dk_ref, dk_got_ref, dq_ref, dq_got_ref, *outs):
    cols = dv_ref.shape[1]
    for e, out in enumerate(outs):
        dest = lax.rem(at_ref[1] + e, GROUP)
        rows = pl.ds(pl.multiple_of(dest * 128, 128), 128)
        out[:, :cols] = dv_ref[rows, :]
        dk = dk_ref[rows, :] + dk_got_ref[rows, :].astype(jnp.float32)
        dq = dq_ref[rows, :] + dq_got_ref[rows, :].astype(jnp.float32)
        out[:, cols:cols + HALF] = dk.astype(jnp.bfloat16)
        out[:, cols + HALF:] = dq.astype(jnp.bfloat16)


def sums_kernel(at_ref, *refs):
    parts, (keep_ref, give_ref) = refs[:-2], refs[-2:]
    wide = parts[0].shape[1] - 2 * HALF
    y_lo = at_ref[3]
    for m in range(2):
        for ref, which in ((keep_ref, y_lo), (give_ref, 1 - y_lo)):
            src = pl.ds(pl.multiple_of(wide + m * HALF + which * 128, 128), 128)
            total = parts[0][:, src].astype(jnp.float32)
            for part in parts[1:]:
                total = total + part[:, src].astype(jnp.float32)
            ref[:, m * 128:(m + 1) * 128] = total


def values_kernel(at_ref, *refs):
    out = refs[-1]
    cols = out.shape[1] // GROUP
    for e, ref in enumerate(refs[:-1]):
        src = lax.rem(at_ref[1] + GROUP - e, GROUP) * cols
        out[:, pl.ds(pl.multiple_of(src, 128), cols)] = ref[:, :cols]


def last_kernel(keep_ref, got_ref, dk_ref, dq_ref):
    done = (keep_ref[...] + got_ref[...]).astype(jnp.bfloat16)
    dk_ref[...] = done[:, :128]
    dq_ref[...] = done[:, 128:]


def mixing_kernel(at_ref, *refs):
    out = refs[-1]
    for e, ref in enumerate(refs[:-1]):
        src = lax.rem(at_ref[1] + GROUP - e, GROUP)
        for h in range(ref.shape[0]):
            out[pl.ds(src * ref.shape[0] + h, 1), :] = ref[h:h + 1, :]


SMEM = pl.BlockSpec(memory_space=pltpu.SMEM)
VMEM = pl.BlockSpec(memory_space=pltpu.VMEM)
ANY = pl.BlockSpec(memory_space=pl.ANY)
F32, B16 = jnp.float32, jnp.bfloat16


def call(body, grid, ins, outs, scratch, args, micros, vmem=40):
    return pl.pallas_call(
        body,
        grid=grid,
        in_specs=ins,
        out_specs=[spec for spec, _, _ in outs],
        out_shape=[jax.ShapeDtypeStruct(shape, kind) for _, shape, kind in outs],
        scratch_shapes=scratch,
        compiler_params=pltpu.CompilerParams(vmem_limit_bytes=vmem * 2**20),
        cost_estimate=pl.CostEstimate(
            flops=int(micros * 1e9), bytes_accessed=1_000_000, transcendentals=0),
    )(*args)


def fixed(shape, *at):
    return pl.BlockSpec(shape, lambda h: at or (0,) * len(shape))


def by_head(rows, base=0):
    return pl.BlockSpec((rows, 128), lambda h: (0, base + h))


def head_first(*shape):
    return pl.BlockSpec((1,) + shape, lambda h: (h,) + (0,) * len(shape))


def per_device(q_shared, k_shared, mixing, values, cotangent):
    tok, width = q_shared.shape
    peers = lax.axis_size("seq")
    scale = 1.0 / math.sqrt(width)
    me = lax.axis_index("seq")
    head_at = lax.axis_index("head")
    heads = mixing.shape[0] // GROUP
    n_v = heads * 128
    span = GROUP * tok
    at = jnp.stack([lax.rem(head_at, 2), lax.rem(me, GROUP), lax.div(me, GROUP), lax.div(head_at, 2)])

    def to_group(x, by):
        pairs = [(i, i + GROUP * by) for i in range(peers) if 0 <= i + GROUP * by < peers]
        return lax.ppermute(x, "seq", pairs)

    def turn(x, by):
        pairs = [(i, i - i % GROUP + (i + by) % GROUP) for i in range(peers)]
        return lax.ppermute(x, "seq", pairs)

    def turns(parts):
        return [parts[0]] + [turn(part, e) for e, part in enumerate(parts) if e]

    def core_swap(x):
        return lax.ppermute(x, "head", [(0, 1), (1, 0), (2, 3), (3, 2)])

    whole = lambda x: fixed(x.shape)
    wide = n_v + HALF
    *own, ahead = call(
        load_kernel, (), [SMEM] + [ANY] * 4,
        [(VMEM, (tok, 2 * wide), B16)] * GROUP + [(VMEM, (tok, GROUP * n_v + HALF), B16)],
        [pltpu.VMEM((tok, width), B16)] * 2 + [pltpu.SemaphoreType.DMA((11,))],
        (at, values, cotangent, k_shared, q_shared), 3, vmem=56)
    ahead = to_group(ahead, 1)
    own = turns(own)
    before = call(split_kernel, (1,), [SMEM, whole(ahead)],
                  [(fixed((tok, wide)), (tok, wide), B16)] * GROUP, [], (at, ahead), 1)
    before = list(before)
    own[0], before[0] = lax.optimization_barrier((own[0], before[0]))
    before = turns(before)
    vk, qc, kq = call(
        gather_kernel, (1,), [SMEM] + [whole(own[0])] * GROUP,
        [(fixed((span, wide)), (span, wide), B16)] * 2
        + [(fixed((span, 2 * HALF)), (span, 2 * HALF), B16)], [], (at, *own), 8)
    x3 = to_group(qc, -1)
    kq_other = core_swap(kq)
    kp, mix = call(
        collect_kernel, (1,),
        [SMEM, fixed((GROUP * heads, width))] + [fixed((tok, HALF), 0, 2)] * GROUP,
        [(fixed((span, HALF)), (span, HALF), B16),
         (fixed((heads, 1, width)), (heads, 1, width), F32)],
        [], (at, mixing, *before), 1)
    kp_other = core_swap(kp)

    stats, grad, w, k_all, q_all = call(
        functools.partial(scores_kernel, scale), (heads,),
        [SMEM, head_first(1, width), by_head(span), fixed((span, HALF), 0, 2), by_head(span, 2),
         fixed((span, HALF), 0, 0), fixed((span, HALF), 0, 0), fixed((span, HALF), 0, 1)]
        + [by_head(tok)] * GROUP + [fixed((span, HALF))] * 2,
        [(head_first(2, span), (heads, 2, span), F32),
         (head_first(2, 768, 256), (heads, 2, 768, 256), B16),
         (head_first(3, 256, 256), (heads, 3, 256, 256), B16),
         (fixed((2 * span, width)), (2 * span, width), B16),
         (fixed((span, width)), (span, width), B16)],
        [pltpu.VMEM((2 * span, width), B16), pltpu.VMEM((span, width), B16),
         pltpu.VMEM((2 * span, 128), B16)],
        (at, mix, vk, vk, qc, qc, kq_other, kq_other, *before, kp, kp_other), 0.1)
    next_stats = to_group(stats, -1)
    dq_mine, dq_other, dmix = call(
        functools.partial(query_kernel, scale), (heads,),
        [SMEM, head_first(1, width), fixed((2 * span, width)), fixed((span, width)),
         head_first(2, 768, 256)],
        [(fixed((span, HALF)), (span, HALF), F32), (fixed((span, HALF)), (span, HALF), B16),
         (head_first(1, width), (heads, 1, width), F32)],
        [pltpu.VMEM((span, width), F32)],
        (at, mix, k_all, q_all, grad), 0.3)

    def from_peer(x, by):
        return lax.ppermute(x, "seq", [(i, i ^ by) for i in range(peers)])

    def exchange(x, a, b):
        return (x + from_peer(x, a)) + (from_peer(x, b) + from_peer(x, a ^ b))

    dk, dv = call(
        key_kernel, (heads,),
        [head_first(1, width), by_head(span, 2), fixed((span, width)),
         head_first(2, 768, 256), head_first(3, 256, 256)],
        [(fixed((span, width)), (span, width), F32), (by_head(span), (span, n_v), F32)],
        [], (mix, qc, q_all, grad, w), 0.3)
    x3, dk = lax.optimization_barrier((x3, dk))
    qn_other = core_swap(x3[:, :HALF])
    dk_mine, dk_other, dv = call(
        functools.partial(next_kernel, scale), (heads,),
        [head_first(1, width), by_head(span), fixed((span, HALF), 0, 2),
         fixed((span, HALF), 0, 0), by_head(span, 2), fixed((span, HALF), 0, 0),
         fixed((span, HALF)), head_first(2, span), fixed((span, width)), by_head(span)],
        [(fixed((span, HALF)), (span, HALF), F32), (fixed((span, HALF)), (span, HALF), B16),
         (by_head(span), (span, n_v), B16)],
        [pltpu.VMEM((span, width), B16), pltpu.VMEM((span, width), B16),
         pltpu.VMEM((span, width), F32)],
        (mix, vk, vk, kq_other, x3, x3, qn_other, next_stats, dk, dv), 6)
    dk_other, dq_other, dmix = lax.optimization_barrier((dk_other, dq_other, dmix))
    dmix = exchange(dmix.reshape(heads, width), GROUP, 2 * GROUP)

    dk_got, dq_got = core_swap(dk_other), core_swap(dq_other)
    back = call(
        pack_kernel, (1,), [SMEM, whole(dv), whole(dk_mine), whole(dk_got), whole(dq_mine), whole(dq_got)],
        [(fixed((tok, n_v + 2 * HALF)), (tok, n_v + 2 * HALF), B16)] * GROUP, [],
        (at, dv, dk_mine, dk_got, dq_mine, dq_got), 1)
    back = turns(back)
    keep, give = call(sums_kernel, (1,), [SMEM] + [whole(back[0])] * GROUP,
                      [(fixed((tok, HALF)), (tok, HALF), F32)] * 2, [], (at, *back), 1)
    dmix = exchange(dmix, 4 * GROUP, 8 * GROUP)
    dmix, give = lax.optimization_barrier((dmix, give))
    got = lax.ppermute(give, "head", [(0, 2), (1, 3), (2, 0), (3, 1)])
    (d_values,) = call(values_kernel, (1,), [SMEM] + [whole(back[0])] * GROUP,
                       [(fixed((tok, GROUP * n_v)), (tok, GROUP * n_v), B16)], [], (at, *back), 1)
    d_key, d_query = call(last_kernel, (1,), [whole(keep)] * 2,
                          [(fixed((tok, 128)), (tok, 128), B16)] * 2, [], (keep, got), 1)

    dmix = turns([dmix] * GROUP)
    (d_mixing,) = call(mixing_kernel, (1,), [SMEM] + [whole(dmix[0])] * GROUP,
                       [(fixed((GROUP * heads, width)), (GROUP * heads, width), F32)], [], (at, *dmix), 1)
    return d_query, d_key, d_values, d_mixing


def solution(mesh):
    placed = (P("seq", None), P("seq", None), P("head", None), P("seq", "head"), P("seq", "head"))
    return jax.shard_map(
        per_device,
        mesh=mesh,
        in_specs=placed,
        out_specs=(P("seq", "head"), P("seq", "head"), P("seq", "head"), P("head", None)),
        check_vma=False,
    )
```

time: 128 us -> 108 us (0.84); the launches traced: 126 us -> 108 us
  waiting for transfers between devices: 52.4 us -> 32.2 us
  Pallas kernels: 17.4 us -> 27.5 us
  local copies, waits for them, and re-layouts: 7.85 us -> 0.04 us
  other arithmetic: 4.51 us -> 0.59 us
  starting transfers between devices: 43.3 us -> 46.6 us
    ppermute x10 -> x22, starting transfers between devices: 30.3 us -> 45.7 us  [the longest x12 20 us: turn(): return lax.ppermute(x, 'seq', pairs)]
    all_to_all x3 -> x0, starting transfers between devices: 12.3 us -> none  [trade(): return lax.all_to_all(x, 'seq', 0, 0, axis_index_groups=groups, tiled=True)]
    all_to_all x3 -> x0, waiting for transfers between devices: 11.3 us -> none  [trade(): return lax.all_to_all(x, 'seq', 0, 0, axis_index_groups=groups, tiled=True)]
    ppermute x10 -> x22, waiting for transfers between devices: 41.1 us -> 30.7 us  [the longest x12 15.5 us: turn(): return lax.ppermute(x, 'seq', pairs)]
    pallas_call x2 -> x13, Pallas kernels: 17.4 us -> 27.5 us  [call(): pl.pallas_call(body, grid=grid, in_specs=ins, out_specs=[spec for spec, _...]
    concatenate x5 -> x0, other arithmetic: 4.21 us -> none  [the longest x1 1.27 us: per_device(): jnp.concatenate([split(values), spread(k_half), split(cotangent), spread(...]
    reshape x7 -> x0, local copies, waits for them, and re-layouts: 2.71 us -> none  [the longest x3 1.16 us: split(): return x.reshape(tok, GROUP, cols).transpose(1, 0, 2)]
    unnamed x12 -> x7, local copies, waits for them, and re-layouts: 2.6 us -> 0.02 us
  transfers between devices with their start and end apart: 18 -> 27, of which waited for: 11 -> 10; matrix products, arithmetic and copies ran while one was open for 5% -> 0% of each run, Pallas kernels for 14% -> 15%
where the time goes in v2:
time: 108 us
  starting transfers between devices  46.6 us (43%)
  waiting for transfers between devices  32.2 us (30%)
  Pallas kernels  27.5 us (25%)
    pallas_call x13, Pallas kernels, call(): pl.pallas_call(body, grid=grid, in_specs=ins, out_specs=[spec for spec, _...  27.5 us
    ppermute x12, starting transfers between devices, turn(): return lax.ppermute(x, 'seq', pairs)  20 us
    ppermute x6, starting transfers between devices, from_peer(): return lax.ppermute(x, 'seq', [(i, i ^ by) for i in range(peers)])  17.4 us
    ppermute x12, waiting for transfers between devices, turn(): return lax.ppermute(x, 'seq', pairs)  15.5 us
    ppermute x3, waiting for transfers between devices, to_group(): return lax.ppermute(x, 'seq', pairs)  9.88 us
    ppermute x3, starting transfers between devices, to_group(): return lax.ppermute(x, 'seq', pairs)  6.94 us
    ppermute x6, waiting for transfers between devices, from_peer(): return lax.ppermute(x, 'seq', [(i, i ^ by) for i in range(peers)])  4.32 us
  transfers between devices with their start and end apart: 27, of which 10 were waited for; matrix products, arithmetic and copies ran while one was open for 0% of the time, Pallas kernels for 15%

profile of v2, /device:TPU:8, one launch (start us, length us, event | category | flops | bytes accessed | tf_op | source)
XLA Modules:
  0.0 107.8 jit_solution(12359350604641062937)
XLA Ops:
  0.6 0.6 pad_add_fusion.at_ref
  1.2 3.7 %shard_map.84 = (bf16[128,1536]{1,0:T(8,128)(2,1)}, bf16[128,1536]{1,0:T(8,128)(2,1)}, bf16[128,1536]{1,0:T(8,128)(2,1)}, bf16[128,1536]{1,0:T(8,128)(2,1)}, bf16[128,2304]{1,0:T(8,128)(2,1)}) custom-call(s32[4]{0:T(128)} %pad_add_fusion.at_ref, bf16[128,2048]{1,0:T(8,128)(2,1)} %v_ref.1, bf16[128,2048]{1,0:T(8,128)(2,1)} %c_ref.1, bf16[128,512]{1,0:T(8,128)(2,1)} %k_ref.1, ...), custom_call_target="tpu_custom_call" | custom-call | flops 3000000000 | bytes 1000000 | tf_op jit(solution)/shard_map/pallas_call | solution.py:292
  4.9 4.4 %collective-permute-start = (bf16[128,2304]{1,0:T(8,128)(2,1)}, bf16[128,2304]{1,0:T(8,128)(2,1)S(1)}, u32[]{:S(2)}, u32[]{:S(2)}) collective-permute-start(bf16[128,2304]{1,0:T(8,128)(2,1)} %get-tuple-element.49), channel_id=1, source_target_pairs={{0,16},{4,20},{8,24},{12,28},{16,32},{20,36},{24,40},{28,44},{32,4... | collective-permute-start | bytes 1769480 | tf_op jit(solution)/shard_map/ppermute | solution.py:330
  9.3 1.6 %collective-permute-start.4 = (bf16[128,1536]{1,0:T(8,128)(2,1)}, bf16[128,1536]{1,0:T(8,128)(2,1)S(1)}, u32[]{:S(2)}, u32[]{:S(2)}) collective-permute-start(bf16[128,1536]{1,0:T(8,128)(2,1)} %get-tuple-element.57), channel_id=1, source_target_pairs={{0,4},{4,8},{8,12},{12,0},{16,20},{20,24},{24,28},{28,16},{32,36},... | collective-permute-start | bytes 1179656 | tf_op jit(solution)/shard_map/ppermute | solution.py:334
  10.8 2.7 %collective-permute-start.5 = (bf16[128,1536]{1,0:T(8,128)(2,1)}, bf16[128,1536]{1,0:T(8,128)(2,1)S(1)}, u32[]{:S(2)}, u32[]{:S(2)}) collective-permute-start(bf16[128,1536]{1,0:T(8,128)(2,1)} %get-tuple-element.58), channel_id=1, source_target_pairs={{0,8},{4,12},{8,0},{12,4},{16,24},{20,28},{24,16},{28,20},{32,40},... | collective-permute-start | bytes 1179656 | tf_op jit(solution)/shard_map/ppermute | solution.py:334
  13.6 1.4 %collective-permute-start.6 = (bf16[128,1536]{1,0:T(8,128)(2,1)}, bf16[128,1536]{1,0:T(8,128)(2,1)S(1)}, u32[]{:S(2)}, u32[]{:S(2)}) collective-permute-start(bf16[128,1536]{1,0:T(8,128)(2,1)} %get-tuple-element.59), channel_id=1, source_target_pairs={{0,12},{4,0},{8,4},{12,8},{16,28},{20,16},{24,20},{28,24},{32,44},... | collective-permute-start | bytes 1179656 | tf_op jit(solution)/shard_map/ppermute | solution.py:334
  15.0 7.1 %collective-permute-done.raw_ref = bf16[128,2304]{1,0:T(8,128)(2,1)S(1)} collective-permute-done((bf16[128,2304]{1,0:T(8,128)(2,1)}, bf16[128,2304]{1,0:T(8,128)(2,1)S(1)}, u32[]{:S(2)}, u32[]{:S(2)}) %collective-permute-start) | collective-permute-done | bytes 589856 | tf_op jit(solution)/shard_map/ppermute | solution.py:330
  22.1 0.6 shard_map.85
  22.7 8.0 %collective-permute-done.5.p2_ref = bf16[128,1536]{1,0:T(8,128)(2,1)S(1)} collective-permute-done((bf16[128,1536]{1,0:T(8,128)(2,1)}, bf16[128,1536]{1,0:T(8,128)(2,1)S(1)}, u32[]{:S(2)}, u32[]{:S(2)}) %collective-permute-start.5) | collective-permute-done | bytes 393248 | tf_op jit(solution)/shard_map/ppermute | solution.py:334
  30.8 0.7 shard_map.87
  31.5 1.3 %collective-permute-start.8 = (bf16[512,768]{1,0:T(8,128)(2,1)S(1)}, bf16[512,768]{1,0:T(8,128)(2,1)S(1)}, u32[]{:S(2)}, u32[]{:S(2)}) collective-permute-start(bf16[512,768]{1,0:T(8,128)(2,1)S(1)} %get-tuple-element.62.c_ref.qm_ref), channel_id=1, source_target_pairs={{16,0},{20,4},{24,8},{28,12},{32,16},{36,20},{40,24},{44,28},{48,3... | collective-permute-start | bytes 2359304 | tf_op jit(solution)/shard_map/ppermute | solution.py:330
  32.8 1.4 %collective-permute-start.1 = (bf16[128,768]{1,0:T(8,128)(2,1)S(1)}, bf16[128,768]{1,0:T(8,128)(2,1)S(1)}, u32[]{:S(2)}, u32[]{:S(2)}) collective-permute-start(bf16[128,768]{1,0:T(8,128)(2,1)S(1)} %get-tuple-element.52), channel_id=1, source_target_pairs={{0,4},{4,8},{8,12},{12,0},{16,20},{20,24},{24,28},{28,16},{32,36},... | collective-permute-start | bytes 589832 | tf_op jit(solution)/shard_map/ppermute | solution.py:334
  34.2 2.4 %collective-permute-start.2 = (bf16[128,768]{1,0:T(8,128)(2,1)S(1)}, bf16[128,768]{1,0:T(8,128)(2,1)S(1)}, u32[]{:S(2)}, u32[]{:S(2)}) collective-permute-start(bf16[128,768]{1,0:T(8,128)(2,1)S(1)} %get-tuple-element.53), channel_id=1, source_target_pairs={{0,8},{4,12},{8,0},{12,4},{16,24},{20,28},{24,16},{28,20},{32,40},... | collective-permute-start | bytes 589832 | tf_op jit(solution)/shard_map/ppermute | solution.py:334
  36.6 1.6 %collective-permute-start.3 = (bf16[128,768]{1,0:T(8,128)(2,1)S(1)}, bf16[128,768]{1,0:T(8,128)(2,1)S(1)}, u32[]{:S(2)}, u32[]{:S(2)}) collective-permute-start(bf16[128,768]{1,0:T(8,128)(2,1)S(1)} %get-tuple-element.54), channel_id=1, source_target_pairs={{0,12},{4,0},{8,4},{12,8},{16,28},{20,16},{24,20},{28,24},{32,44},... | collective-permute-start | bytes 589832 | tf_op jit(solution)/shard_map/ppermute | solution.py:334
  38.1 2.1 %collective-permute-done.1.k1_ref.vp1_ref = bf16[128,768]{1,0:T(8,128)(2,1)S(1)} collective-permute-done((bf16[128,768]{1,0:T(8,128)(2,1)S(1)}, bf16[128,768]{1,0:T(8,128)(2,1)S(1)}, u32[]{:S(2)}, u32[]{:S(2)}) %collective-permute-start.1) | collective-permute-done | bytes 196640 | tf_op jit(solution)/shard_map/ppermute | solution.py:334
  40.2 5.4 %collective-permute-done.2.k2_ref.vp2_ref = bf16[128,768]{1,0:T(8,128)(2,1)S(1)} collective-permute-done((bf16[128,768]{1,0:T(8,128)(2,1)S(1)}, bf16[128,768]{1,0:T(8,128)(2,1)S(1)}, u32[]{:S(2)}, u32[]{:S(2)}) %collective-permute-start.2) | collective-permute-done | bytes 196640 | tf_op jit(solution)/shard_map/ppermute | solution.py:334
  45.6 0.6 shard_map.86
  46.3 1.5 %collective-permute-done.9.kpo_ref = bf16[512,256]{1,0:T(8,128)(2,1)S(1)} collective-permute-done((bf16[512,256]{1,0:T(8,128)(2,1)S(1)}, bf16[512,256]{1,0:T(8,128)(2,1)S(1)}, u32[]{:S(2)}, u32[]{:S(2)}) %collective-permute-start.9) | collective-permute-done | bytes 262176 | tf_op jit(solution)/shard_map/ppermute | solution.py:340
  47.8 6.5 %shard_map.88 = (f32[4,2,512]{2,1,0:T(2,128)S(1)}, bf16[4,2,768,256]{3,2,1,0:T(8,128)(2,1)S(1)}, bf16[4,3,256,256]{3,2,1,0:T(8,128)(2,1)S(1)}, bf16[1024,512]{1,0:T(8,128)(2,1)S(1)}, bf16[512,512]{1,0:T(8,128)(2,1)S(1)}) custom-call(s32[4]{0:T(128)S(1)} %copy-done, f32[4,1,512]{2,1,0:T(1,128)S(1)} %get-tuple-element.55.mix_ref, ...), custom_call_target="tpu_custom_call" | custom-call | flops 100000000 | bytes 1000000 | tf_op jit(solution)/shard_map/pallas_call | solution.py:292
  54.3 2.3 %shard_map.89 = (f32[512,512]{1,0:T(8,128)S(1)}, f32[512,512]{1,0:T(8,128)S(1)}) custom-call(f32[4,1,512]{2,1,0:T(1,128)S(1)} %get-tuple-element.55.mix_ref, bf16[512,768]{1,0:T(8,128)(2,1)S(1)} %get-tuple-element.62.c_ref.qm_ref, bf16[512,512]{1,0:T(8,128)(2,1)S(1)} %get-tuple-element.64.q_ref, bf16[4,2,768,256]{3,2,1,0:T(8,128)(2,1)S(1)} %get-tuple-element.65.grad_ref, ...), custom_call_target="tpu_custom_call" | custom-call | flops 300000000 | bytes 1000000 | tf_op jit(solution)/shard_map/pallas_call | solution.py:292
  56.6 0.2 collective-permute-start.10
  56.8 1.3 %collective-permute-start.11 = (f32[4,2,512]{2,1,0:T(2,128)S(1)}, f32[4,2,512]{2,1,0:T(2,128)S(1)}, u32[]{:S(2)}, u32[]{:S(2)}) collective-permute-start(f32[4,2,512]{2,1,0:T(2,128)S(1)} %get-tuple-element.69), channel_id=1, source_target_pairs={{16,0},{20,4},{24,8},{28,12},{32,16},{36,20},{40,24},{44,28},{48,3... | collective-permute-start | bytes 49160 | tf_op jit(solution)/shard_map/ppermute | solution.py:330
  58.1 3.4 %shard_map.91 = (f32[512,256]{1,0:T(8,128)S(1)}, bf16[512,256]{1,0:T(8,128)(2,1)S(1)}, f32[4,1,512]{2,1,0:T(1,128)S(1)}) custom-call(s32[4]{0:T(128)S(1)} %copy-done, f32[4,1,512]{2,1,0:T(1,128)S(1)} %get-tuple-element.55.mix_ref, bf16[1024,512]{1,0:T(8,128)(2,1)S(1)} %get-tuple-element.75.k_ref, bf16[512,512]{1,0:T(8,128)(2,1)S(1)} %get-tuple-element.64.q_ref, ...), custom_call_target="tpu_custom_call" | custom-call | flops 300000000 | bytes 1000000 | tf_op jit(solution)/shard_map/pallas_call | solution.py:292
  61.5 2.8 %collective-permute-done.11.stats_ref = f32[4,2,512]{2,1,0:T(2,128)S(1)} collective-permute-done((f32[4,2,512]{2,1,0:T(2,128)S(1)}, f32[4,2,512]{2,1,0:T(2,128)S(1)}, u32[]{:S(2)}, u32[]{:S(2)}) %collective-permute-start.11) | collective-permute-done | bytes 16416 | tf_op jit(solution)/shard_map/ppermute | solution.py:330
  64.3 5.2 %shard_map.90 = (f32[512,256]{1,0:T(8,128)S(1)}, bf16[512,256]{1,0:T(8,128)(2,1)S(1)}, bf16[512,512]{1,0:T(8,128)(2,1)S(1)}) custom-call(f32[4,1,512]{2,1,0:T(1,128)S(1)} %get-tuple-element.55.mix_ref, bf16[512,768]{1,0:T(8,128)(2,1)S(1)} %get-tuple-element.60.v_ref.km_ref, bf16[512,768]{1,0:T(8,128)(2,1)S(1)} %get-tuple-element.60.v_ref.km_ref, ...), custom_call_target="tpu_custom_call" | custom-call | flops 6000000000 | bytes 1000000 | tf_op jit(solution)/shard_map/pallas_call | solution.py:292
  69.6 0.5 collective-permute-start.13
  70.1 4.4 %collective-permute-start.17 = (f32[4,512]{1,0:T(4,128)S(1)}, f32[4,512]{1,0:T(4,128)S(1)}, u32[]{:S(2)}, u32[]{:S(2)}) collective-permute-start(f32[4,512]{1,0:T(4,128)S(1)} %bitcast.9), channel_id=1, source_target_pairs={{0,16},{4,20},{8,24},{12,28},{16,0},{20,4},{24,8},{28,12},{32,48},... | collective-permute-start | bytes 24584 | tf_op jit(solution)/shard_map/ppermute | solution.py:394
  74.5 1.9 %collective-permute-start.18 = (f32[4,512]{1,0:T(4,128)S(1)}, f32[4,512]{1,0:T(4,128)S(1)}, u32[]{:S(2)}, u32[]{:S(2)}) collective-permute-start(f32[4,512]{1,0:T(4,128)S(1)} %bitcast.10), channel_id=1, source_target_pairs={{0,32},{4,36},{8,40},{12,44},{16,48},{20,52},{24,56},{28,60},{32,0... | collective-permute-start | bytes 24584 | tf_op jit(solution)/shard_map/ppermute | solution.py:394
  76.4 0.7 collective-permute-start.19
  77.1 0.7 shard_map.92
  77.8 0.6 collective-permute-start.14
  78.4 3.1 %collective-permute-start.15 = (bf16[128,1024]{1,0:T(8,128)(2,1)S(1)}, bf16[128,1024]{1,0:T(8,128)(2,1)S(1)}, u32[]{:S(2)}, u32[]{:S(2)}) collective-permute-start(bf16[128,1024]{1,0:T(8,128)(2,1)S(1)} %get-tuple-element.83), channel_id=1, source_target_pairs={{0,8},{4,12},{8,0},{12,4},{16,24},{20,28},{24,16},{28,20},{32,40},... | collective-permute-start | bytes 786440 | tf_op jit(solution)/shard_map/ppermute | solution.py:334
  81.5 0.2 collective-permute-start.16
  81.7 0.8 collective-permute-done.19
  82.5 5.1 %collective-permute-start.20 = (f32[4,512]{1,0:T(4,128)S(1)}, f32[4,512]{1,0:T(4,128)S(1)}, u32[]{:S(2)}, u32[]{:S(2)}) collective-permute-start(f32[4,512]{1,0:T(4,128)S(1)} %add_add_fusion.1), channel_id=1, source_target_pairs={{0,64},{4,68},{8,72},{12,76},{16,80},{20,84},{24,88},{28,92},{32,9... | collective-permute-start | bytes 24584 | tf_op jit(solution)/shard_map/ppermute | solution.py:394
  87.6 3.0 %collective-permute-start.21 = (f32[4,512]{1,0:T(4,128)S(1)}, f32[4,512]{1,0:T(4,128)S(1)}, u32[]{:S(2)}, u32[]{:S(2)}) collective-permute-start(f32[4,512]{1,0:T(4,128)S(1)} %add_add_fusion.1), channel_id=1, source_target_pairs={{0,128},{4,132},{8,136},{12,140},{16,144},{20,148},{24,152},{28,15... | collective-permute-start | bytes 24584 | tf_op jit(solution)/shard_map/ppermute | solution.py:394
  90.6 2.2 %collective-permute-start.22 = (f32[4,512]{1,0:T(4,128)S(1)}, f32[4,512]{1,0:T(4,128)S(1)}, u32[]{:S(2)}, u32[]{:S(2)}) collective-permute-start(f32[4,512]{1,0:T(4,128)S(1)} %add_add_fusion.1), channel_id=1, source_target_pairs={{0,192},{4,196},{8,200},{12,204},{16,208},{20,212},{24,216},{28,22... | collective-permute-start | bytes 24584 | tf_op jit(solution)/shard_map/ppermute | solution.py:394
  92.9 2.4 %collective-permute-done.21 = f32[4,512]{1,0:T(4,128)S(1)} collective-permute-done((f32[4,512]{1,0:T(4,128)S(1)}, f32[4,512]{1,0:T(4,128)S(1)}, u32[]{:S(2)}, u32[]{:S(2)}) %collective-permute-start.21) | collective-permute-done | bytes 8224 | tf_op jit(solution)/shard_map/ppermute | solution.py:394
  95.2 1.2 %collective-permute-done.22 = f32[4,512]{1,0:T(4,128)S(1)} collective-permute-done((f32[4,512]{1,0:T(4,128)S(1)}, f32[4,512]{1,0:T(4,128)S(1)}, u32[]{:S(2)}, u32[]{:S(2)}) %collective-permute-start.22) | collective-permute-done | bytes 8224 | tf_op jit(solution)/shard_map/ppermute | solution.py:394
  96.4 0.7 shard_map.93
  97.1 1.9 %collective-permute-start.24 = (f32[4,512]{1,0:T(4,128)S(1)}, f32[4,512]{1,0:T(4,128)S(1)}, u32[]{:S(2)}, u32[]{:S(2)}) collective-permute-start(f32[4,512]{1,0:T(4,128)S(1)} %add_add_fusion.refs_0_), channel_id=1, source_target_pairs={{0,4},{4,8},{8,12},{12,0},{16,20},{20,24},{24,28},{28,16},{32,36},... | collective-permute-start | bytes 24584 | tf_op jit(solution)/shard_map/ppermute | solution.py:334
  99.1 0.9 collective-permute-start.25
  100.0 2.2 %collective-permute-start.26 = (f32[4,512]{1,0:T(4,128)S(1)}, f32[4,512]{1,0:T(4,128)S(1)}, u32[]{:S(2)}, u32[]{:S(2)}) collective-permute-start(f32[4,512]{1,0:T(4,128)S(1)} %add_add_fusion.refs_0_), channel_id=1, source_target_pairs={{0,12},{4,0},{8,4},{12,8},{16,28},{20,16},{24,20},{28,24},{32,44},... | collective-permute-start | bytes 24584 | tf_op jit(solution)/shard_map/ppermute | solution.py:334
  102.2 1.4 %collective-permute-start.23 = (f32[128,256]{1,0:T(8,128)S(1)}, f32[128,256]{1,0:T(8,128)S(1)}, u32[]{:S(2)}, u32[]{:S(2)}) collective-permute-start(f32[128,256]{1,0:T(8,128)S(1)} %get-tuple-element.88), channel_id=1, source_target_pairs={{0,2},{1,3},{2,0},{3,1},{4,6},{5,7},{6,4},{7,5},{8,10},{9,11},{10,... | collective-permute-start | bytes 393224 | tf_op jit(solution)/shard_map/ppermute | solution.py:430
  103.6 1.4 %shard_map.95 = bf16[128,2048]{1,0:T(8,128)(2,1)} custom-call(s32[4]{0:T(128)S(1)} %copy-done, bf16[128,1024]{1,0:T(8,128)(2,1)S(1)} %get-tuple-element.81.refs_0_, bf16[128,1024]{1,0:T(8,128)(2,1)S(1)} %collective-permute-done.14.refs_1_, bf16[128,1024]{1,0:T(8,128)(2,1)S(1)} %collective-permute-done.15.refs_2_, ...), custom_call_target="tpu_custom_call" | custom-call | flops 1000000000 | bytes 1000000 | tf_op jit(solution)/shard_map/pallas_call | solution.py:292
  105.0 1.2 %shard_map.96 = f32[16,512]{1,0:T(8,128)} custom-call(s32[4]{0:T(128)S(1)} %copy-done, f32[4,512]{1,0:T(4,128)S(1)} %add_add_fusion.refs_0_, f32[4,512]{1,0:T(4,128)S(1)} %collective-permute-done.24.refs_1_, f32[4,512]{1,0:T(4,128)S(1)} %collective-permute-done.25.refs_2_, f32[4,512]{1,0:T(4,128)S(1)} %collective-permute-done.26.refs_3_), custom_call_target="tpu_custom_call" | custom-call | flops 1000000000 | bytes 1000000 | tf_op jit(solution)/shard_map/pallas_call | solution.py:292
  106.2 1.0 collective-permute-done.23.got_ref
  107.2 0.6 shard_map.94
  (30 shorter events, 0.3 us)
Async XLA Ops:
  1.2 20.9 %copy-start = (s32[4]{0:T(128)S(1)}, s32[4]{0:T(128)}, u32[]{:S(2)}) copy-start(s32[4]{0:T(128)} %pad_add_fusion.at_ref) | copy-start | bytes 52
  4.9 25.9 %copy-start.2 = (bf16[128,1536]{1,0:T(8,128)(2,1)S(1)}, bf16[128,1536]{1,0:T(8,128)(2,1)}, u32[]{:S(2)}) copy-start(bf16[128,1536]{1,0:T(8,128)(2,1)} %get-tuple-element.56.p0_ref) | copy-start | bytes 1179652
  4.9 17.2 %collective-permute-start = (bf16[128,2304]{1,0:T(8,128)(2,1)}, bf16[128,2304]{1,0:T(8,128)(2,1)S(1)}, u32[]{:S(2)}, u32[]{:S(2)}) collective-permute-start(bf16[128,2304]{1,0:T(8,128)(2,1)} %get-tuple-element.49), channel_id=1, source_target_pairs={{0,16},{4,20},{8,24},{12,28},{16,32},{20,36},{24,40},{28,44},{32,4... | collective-permute-start | bytes 1769480 | tf_op jit(solution)/shard_map/ppermute | solution.py:330
  9.3 13.5 %collective-permute-start.4 = (bf16[128,1536]{1,0:T(8,128)(2,1)}, bf16[128,1536]{1,0:T(8,128)(2,1)S(1)}, u32[]{:S(2)}, u32[]{:S(2)}) collective-permute-start(bf16[128,1536]{1,0:T(8,128)(2,1)} %get-tuple-element.57), channel_id=1, source_target_pairs={{0,4},{4,8},{8,12},{12,0},{16,20},{20,24},{24,28},{28,16},{32,36},... | collective-permute-start | bytes 1179656 | tf_op jit(solution)/shard_map/ppermute | solution.py:334
  10.8 19.9 %collective-permute-start.5 = (bf16[128,1536]{1,0:T(8,128)(2,1)}, bf16[128,1536]{1,0:T(8,128)(2,1)S(1)}, u32[]{:S(2)}, u32[]{:S(2)}) collective-permute-start(bf16[128,1536]{1,0:T(8,128)(2,1)} %get-tuple-element.58), channel_id=1, source_target_pairs={{0,8},{4,12},{8,0},{12,4},{16,24},{20,28},{24,16},{28,20},{32,40},... | collective-permute-start | bytes 1179656 | tf_op jit(solution)/shard_map/ppermute | solution.py:334
  13.6 17.2 %collective-permute-start.6 = (bf16[128,1536]{1,0:T(8,128)(2,1)}, bf16[128,1536]{1,0:T(8,128)(2,1)S(1)}, u32[]{:S(2)}, u32[]{:S(2)}) collective-permute-start(bf16[128,1536]{1,0:T(8,128)(2,1)} %get-tuple-element.59), channel_id=1, source_target_pairs={{0,12},{4,0},{8,4},{12,8},{16,28},{20,16},{24,20},{28,24},{32,44},... | collective-permute-start | bytes 1179656 | tf_op jit(solution)/shard_map/ppermute | solution.py:334
  22.7 22.9 %copy-start.1 = (f32[16,512]{1,0:T(8,128)S(1)}, f32[16,512]{1,0:T(8,128)}, u32[]{:S(2)}) copy-start(f32[16,512]{1,0:T(8,128)} %mixing_ref.1) | copy-start | bytes 98308
  31.5 25.1 %collective-permute-start.8 = (bf16[512,768]{1,0:T(8,128)(2,1)S(1)}, bf16[512,768]{1,0:T(8,128)(2,1)S(1)}, u32[]{:S(2)}, u32[]{:S(2)}) collective-permute-start(bf16[512,768]{1,0:T(8,128)(2,1)S(1)} %get-tuple-element.62.c_ref.qm_ref), channel_id=1, source_target_pairs={{16,0},{20,4},{24,8},{28,12},{32,16},{36,20},{40,24},{44,28},{48,3... | collective-permute-start | bytes 2359304 | tf_op jit(solution)/shard_map/ppermute | solution.py:330
  32.8 7.4 %collective-permute-start.1 = (bf16[128,768]{1,0:T(8,128)(2,1)S(1)}, bf16[128,768]{1,0:T(8,128)(2,1)S(1)}, u32[]{:S(2)}, u32[]{:S(2)}) collective-permute-start(bf16[128,768]{1,0:T(8,128)(2,1)S(1)} %get-tuple-element.52), channel_id=1, source_target_pairs={{0,4},{4,8},{8,12},{12,0},{16,20},{20,24},{24,28},{28,16},{32,36},... | collective-permute-start | bytes 589832 | tf_op jit(solution)/shard_map/ppermute | solution.py:334
  34.2 11.4 %collective-permute-start.2 = (bf16[128,768]{1,0:T(8,128)(2,1)S(1)}, bf16[128,768]{1,0:T(8,128)(2,1)S(1)}, u32[]{:S(2)}, u32[]{:S(2)}) collective-permute-start(bf16[128,768]{1,0:T(8,128)(2,1)S(1)} %get-tuple-element.53), channel_id=1, source_target_pairs={{0,8},{4,12},{8,0},{12,4},{16,24},{20,28},{24,16},{28,20},{32,40},... | collective-permute-start | bytes 589832 | tf_op jit(solution)/shard_map/ppermute | solution.py:334
  36.6 9.0 %collective-permute-start.3 = (bf16[128,768]{1,0:T(8,128)(2,1)S(1)}, bf16[128,768]{1,0:T(8,128)(2,1)S(1)}, u32[]{:S(2)}, u32[]{:S(2)}) collective-permute-start(bf16[128,768]{1,0:T(8,128)(2,1)S(1)} %get-tuple-element.54), channel_id=1, source_target_pairs={{0,12},{4,0},{8,4},{12,8},{16,28},{20,16},{24,20},{28,24},{32,44},... | collective-permute-start | bytes 589832 | tf_op jit(solution)/shard_map/ppermute | solution.py:334
  38.1 9.7 %collective-permute-start.7 = (bf16[512,512]{1,0:T(8,128)(2,1)S(1)}, bf16[512,512]{1,0:T(8,128)(2,1)S(1)}, u32[]{:S(2)}, u32[]{:S(2)}) collective-permute-start(bf16[512,512]{1,0:T(8,128)(2,1)S(1)} %get-tuple-element.61), channel_id=1, source_target_pairs={{0,1},{1,0},{2,3},{3,2},{4,5},{5,4},{6,7},{7,6},{8,9},{9,8},{10,11... | collective-permute-start | bytes 1572872 | tf_op jit(solution)/shard_map/ppermute | solution.py:340
  46.2 1.6 %collective-permute-start.9 = (bf16[512,256]{1,0:T(8,128)(2,1)S(1)}, bf16[512,256]{1,0:T(8,128)(2,1)S(1)}, u32[]{:S(2)}, u32[]{:S(2)}) collective-permute-start(bf16[512,256]{1,0:T(8,128)(2,1)S(1)} %get-tuple-element.63.kpm_ref), channel_id=1, source_target_pairs={{0,1},{1,0},{2,3},{3,2},{4,5},{5,4},{6,7},{7,6},{8,9},{9,8},{10,11... | collective-permute-start | bytes 786440 | tf_op jit(solution)/shard_map/ppermute | solution.py:340
  56.6 7.7 %collective-permute-start.10 = (bf16[512,256]{1,0:T(8,128)(2,1)S(1)}, bf16[512,256]{1,0:T(8,128)(2,1)S(1)}, u32[]{:S(2)}, u32[]{:S(2)}) collective-permute-start(bf16[512,256]{1,0:T(8,128)(2,1)S(1)} %slice.3), channel_id=1, source_target_pairs={{0,1},{1,0},{2,3},{3,2},{4,5},{5,4},{6,7},{7,6},{8,9},{9,8},{10,11... | collective-permute-start | bytes 786440 | tf_op jit(solution)/shard_map/ppermute | solution.py:340
  56.8 7.5 %collective-permute-start.11 = (f32[4,2,512]{2,1,0:T(2,128)S(1)}, f32[4,2,512]{2,1,0:T(2,128)S(1)}, u32[]{:S(2)}, u32[]{:S(2)}) collective-permute-start(f32[4,2,512]{2,1,0:T(2,128)S(1)} %get-tuple-element.69), channel_id=1, source_target_pairs={{16,0},{20,4},{24,8},{28,12},{32,16},{36,20},{40,24},{44,28},{48,3... | collective-permute-start | bytes 49160 | tf_op jit(solution)/shard_map/ppermute | solution.py:330
  69.5 7.6 %collective-permute-start.12 = (bf16[512,256]{1,0:T(8,128)(2,1)S(1)}, bf16[512,256]{1,0:T(8,128)(2,1)S(1)}, u32[]{:S(2)}, u32[]{:S(2)}) collective-permute-start(bf16[512,256]{1,0:T(8,128)(2,1)S(1)} %get-tuple-element.78), channel_id=1, source_target_pairs={{0,1},{1,0},{2,3},{3,2},{4,5},{5,4},{6,7},{7,6},{8,9},{9,8},{10,11... | collective-permute-start | bytes 786440 | tf_op jit(solution)/shard_map/ppermute | solution.py:340
  69.6 7.5 %collective-permute-start.13 = (bf16[512,256]{1,0:T(8,128)(2,1)S(1)}, bf16[512,256]{1,0:T(8,128)(2,1)S(1)}, u32[]{:S(2)}, u32[]{:S(2)}) collective-permute-start(bf16[512,256]{1,0:T(8,128)(2,1)S(1)} %get-tuple-element.80), channel_id=1, source_target_pairs={{0,1},{1,0},{2,3},{3,2},{4,5},{5,4},{6,7},{7,6},{8,9},{9,8},{10,11... | collective-permute-start | bytes 786440 | tf_op jit(solution)/shard_map/ppermute | solution.py:340
  70.1 11.4 %collective-permute-start.17 = (f32[4,512]{1,0:T(4,128)S(1)}, f32[4,512]{1,0:T(4,128)S(1)}, u32[]{:S(2)}, u32[]{:S(2)}) collective-permute-start(f32[4,512]{1,0:T(4,128)S(1)} %bitcast.9), channel_id=1, source_target_pairs={{0,16},{4,20},{8,24},{12,28},{16,0},{20,4},{24,8},{28,12},{32,48},... | collective-permute-start | bytes 24584 | tf_op jit(solution)/shard_map/ppermute | solution.py:394
  74.5 7.1 %collective-permute-start.18 = (f32[4,512]{1,0:T(4,128)S(1)}, f32[4,512]{1,0:T(4,128)S(1)}, u32[]{:S(2)}, u32[]{:S(2)}) collective-permute-start(f32[4,512]{1,0:T(4,128)S(1)} %bitcast.10), channel_id=1, source_target_pairs={{0,32},{4,36},{8,40},{12,44},{16,48},{20,52},{24,56},{28,60},{32,0... | collective-permute-start | bytes 24584 | tf_op jit(solution)/shard_map/ppermute | solution.py:394
  76.4 6.1 %collective-permute-start.19 = (f32[4,512]{1,0:T(4,128)S(1)}, f32[4,512]{1,0:T(4,128)S(1)}, u32[]{:S(2)}, u32[]{:S(2)}) collective-permute-start(f32[4,512]{1,0:T(4,128)S(1)} %bitcast.11), channel_id=1, source_target_pairs={{0,48},{4,52},{8,56},{12,60},{16,32},{20,36},{24,40},{28,44},{32,1... | collective-permute-start | bytes 24584 | tf_op jit(solution)/shard_map/ppermute | solution.py:394
  77.8 18.6 %collective-permute-start.14 = (bf16[128,1024]{1,0:T(8,128)(2,1)S(1)}, bf16[128,1024]{1,0:T(8,128)(2,1)S(1)}, u32[]{:S(2)}, u32[]{:S(2)}) collective-permute-start(bf16[128,1024]{1,0:T(8,128)(2,1)S(1)} %get-tuple-element.82), channel_id=1, source_target_pairs={{0,4},{4,8},{8,12},{12,0},{16,20},{20,24},{24,28},{28,16},{32,36},... | collective-permute-start | bytes 786440 | tf_op jit(solution)/shard_map/ppermute | solution.py:334
  78.4 18.0 %collective-permute-start.15 = (bf16[128,1024]{1,0:T(8,128)(2,1)S(1)}, bf16[128,1024]{1,0:T(8,128)(2,1)S(1)}, u32[]{:S(2)}, u32[]{:S(2)}) collective-permute-start(bf16[128,1024]{1,0:T(8,128)(2,1)S(1)} %get-tuple-element.83), channel_id=1, source_target_pairs={{0,8},{4,12},{8,0},{12,4},{16,24},{20,28},{24,16},{28,20},{32,40},... | collective-permute-start | bytes 786440 | tf_op jit(solution)/shard_map/ppermute | solution.py:334
  81.5 14.9 %collective-permute-start.16 = (bf16[128,1024]{1,0:T(8,128)(2,1)S(1)}, bf16[128,1024]{1,0:T(8,128)(2,1)S(1)}, u32[]{:S(2)}, u32[]{:S(2)}) collective-permute-start(bf16[128,1024]{1,0:T(8,128)(2,1)S(1)} %get-tuple-element.84), channel_id=1, source_target_pairs={{0,12},{4,0},{8,4},{12,8},{16,28},{20,16},{24,20},{28,24},{32,44},... | collective-permute-start | bytes 786440 | tf_op jit(solution)/shard_map/ppermute | solution.py:334
  82.5 8.2 %collective-permute-start.20 = (f32[4,512]{1,0:T(4,128)S(1)}, f32[4,512]{1,0:T(4,128)S(1)}, u32[]{:S(2)}, u32[]{:S(2)}) collective-permute-start(f32[4,512]{1,0:T(4,128)S(1)} %add_add_fusion.1), channel_id=1, source_target_pairs={{0,64},{4,68},{8,72},{12,76},{16,80},{20,84},{24,88},{28,92},{32,9... | collective-permute-start | bytes 24584 | tf_op jit(solution)/shard_map/ppermute | solution.py:394
  87.6 7.6 %collective-permute-start.21 = (f32[4,512]{1,0:T(4,128)S(1)}, f32[4,512]{1,0:T(4,128)S(1)}, u32[]{:S(2)}, u32[]{:S(2)}) collective-permute-start(f32[4,512]{1,0:T(4,128)S(1)} %add_add_fusion.1), channel_id=1, source_target_pairs={{0,128},{4,132},{8,136},{12,140},{16,144},{20,148},{24,152},{28,15... | collective-permute-start | bytes 24584 | tf_op jit(solution)/shard_map/ppermute | solution.py:394
  90.6 5.8 %collective-permute-start.22 = (f32[4,512]{1,0:T(4,128)S(1)}, f32[4,512]{1,0:T(4,128)S(1)}, u32[]{:S(2)}, u32[]{:S(2)}) collective-permute-start(f32[4,512]{1,0:T(4,128)S(1)} %add_add_fusion.1), channel_id=1, source_target_pairs={{0,192},{4,196},{8,200},{12,204},{16,208},{20,212},{24,216},{28,22... | collective-permute-start | bytes 24584 | tf_op jit(solution)/shard_map/ppermute | solution.py:394
  97.1 7.8 %collective-permute-start.24 = (f32[4,512]{1,0:T(4,128)S(1)}, f32[4,512]{1,0:T(4,128)S(1)}, u32[]{:S(2)}, u32[]{:S(2)}) collective-permute-start(f32[4,512]{1,0:T(4,128)S(1)} %add_add_fusion.refs_0_), channel_id=1, source_target_pairs={{0,4},{4,8},{8,12},{12,0},{16,20},{20,24},{24,28},{28,16},{32,36},... | collective-permute-start | bytes 24584 | tf_op jit(solution)/shard_map/ppermute | solution.py:334
  99.1 5.9 %collective-permute-start.25 = (f32[4,512]{1,0:T(4,128)S(1)}, f32[4,512]{1,0:T(4,128)S(1)}, u32[]{:S(2)}, u32[]{:S(2)}) collective-permute-start(f32[4,512]{1,0:T(4,128)S(1)} %add_add_fusion.refs_0_), channel_id=1, source_target_pairs={{0,8},{4,12},{8,0},{12,4},{16,24},{20,28},{24,16},{28,20},{32,40},... | collective-permute-start | bytes 24584 | tf_op jit(solution)/shard_map/ppermute | solution.py:334
  100.0 5.0 %collective-permute-start.26 = (f32[4,512]{1,0:T(4,128)S(1)}, f32[4,512]{1,0:T(4,128)S(1)}, u32[]{:S(2)}, u32[]{:S(2)}) collective-permute-start(f32[4,512]{1,0:T(4,128)S(1)} %add_add_fusion.refs_0_), channel_id=1, source_target_pairs={{0,12},{4,0},{8,4},{12,8},{16,28},{20,16},{24,20},{28,24},{32,44},... | collective-permute-start | bytes 24584 | tf_op jit(solution)/shard_map/ppermute | solution.py:334
  102.2 5.0 %collective-permute-start.23 = (f32[128,256]{1,0:T(8,128)S(1)}, f32[128,256]{1,0:T(8,128)S(1)}, u32[]{:S(2)}, u32[]{:S(2)}) collective-permute-start(f32[128,256]{1,0:T(8,128)S(1)} %get-tuple-element.88), channel_id=1, source_target_pairs={{0,2},{1,3},{2,0},{3,1},{4,6},{5,7},{6,4},{7,5},{8,10},{9,11},{10,... | collective-permute-start | bytes 393224 | tf_op jit(solution)/shard_map/ppermute | solution.py:430

commit v3 on v2

--- a/solution.py
+++ b/solution.py
@@ -128,7 +128,7 @@
     dv_ref[:tile, :] = dot(w_ref[0, 1], c_ref[tile:, :], NN) + dot(w_ref[0, 0], c_ref[:tile, :], NN)
 
 
-def next_kernel(scale, mix_ref, v_ref, km_ref, ko_ref, cn_ref, qnm_ref, qno_ref, stats_ref,
+def next_kernel(scale, at_ref, mix_ref, v_ref, km_ref, ko_ref, cn_ref, qnm_ref, qno_ref, stats_ref,
                 dk_ref, dv_ref, dkm_ref, dko_ref, dvo_ref, k_all, q_all, dk_acc):
     head = pl.program_id(0)
     span = q_all.shape[0]
@@ -146,6 +146,8 @@
     mix = mix_ref[0]
     row = lax.broadcasted_iota(jnp.int32, (tile, tile), 0)
     col = lax.broadcasted_iota(jnp.int32, (tile, tile), 1)
+    is_last = at_ref[4] == 1
+    seen = (row > col) & jnp.logical_not(is_last)
     dv = [dv_ref[:tile, :], dv_ref[tile:, :]]
     for t in (0, 1):
         lo = t * tile
@@ -155,9 +157,9 @@
         delta = stats_ref[0, 1:2, lo:lo + tile]
         s = dot(k_all[lo:, :], mq, NT) * (scale * LOG2E)
         d = dot(v_ref[lo:, :], up, NT)
-        w = jnp.exp2(jnp.where(row > col, s[:tile] - lse, NEG))
+        w = jnp.exp2(jnp.where(seen, s[:tile] - lse, NEG))
         if t == 0:
-            w = jnp.concatenate([w, jnp.exp2(s[tile:] - lse)], 0)
+            w = jnp.concatenate([w, jnp.exp2(jnp.where(is_last, NEG, s[tile:] - lse))], 0)
         grad = (w * (d - delta)).astype(jnp.bfloat16)
         add = dot(w.astype(jnp.bfloat16), up, NN)
         if t == 0:
@@ -188,7 +190,6 @@
         return copy
 
     shared = [send(k_ref, k_in), send(q_ref, q_in)]
-    send(v_ref, ahead_ref.at[:, :wide])
     owns = (own0_ref, own1_ref, own2_ref, own3_ref)
     for e, own in enumerate(owns):
         src = pl.ds(pl.multiple_of(lax.rem(place + e, GROUP) * cols, 128), cols)
@@ -199,7 +200,7 @@
     for m in range(2):
         src = pl.ds(pl.multiple_of((2 * m + core) * 128, 128), 128)
         k_block, q_block = k_in[:, src], q_in[:, src]
-        ahead_ref[:, wide + m * 128:wide + (m + 1) * 128] = k_block
+        ahead_ref[:, m * 128:(m + 1) * 128] = k_block
         for own in owns:
             own[:, cols + m * 128:cols + (m + 1) * 128] = k_block
             own[:, cols + HALF + m * 128:cols + HALF + (m + 1) * 128] = q_block
@@ -207,20 +208,21 @@
         copy.wait()
 
 
-def split_kernel(at_ref, raw_ref, *hops):
+def split_kernel(at_ref, raw_ref, k_ref, *hops):
     cols = hops[0].shape[1] - HALF
     for e, hop in enumerate(hops):
         src = lax.rem(at_ref[1] + e, GROUP) * cols
         hop[:, :cols] = raw_ref[:, pl.ds(pl.multiple_of(src, 128), cols)]
-        hop[:, cols:] = raw_ref[:, GROUP * cols:]
-
-
-def gather_kernel(at_ref, p0_ref, p1_ref, p2_ref, p3_ref, vk_ref, qc_ref, kq_ref):
+        hop[:, cols:] = k_ref[...]
+
+
+def gather_kernel(at_ref, p0_ref, p1_ref, p2_ref, p3_ref, vk_ref, q_ref, c_ref, kq_ref):
     half = vk_ref.shape[1]
     for e, ref in enumerate((p0_ref, p1_ref, p2_ref, p3_ref)):
         rows = rows_from(at_ref, e)
         vk_ref[rows, :] = ref[:, :half]
-        qc_ref[rows, :] = ref[:, half:]
+        q_ref[rows, :] = ref[:, half:half + HALF]
+        c_ref[rows, :] = ref[:, half + HALF:]
         kq_ref[rows, :] = ref[:, half - HALF:half + HALF]
 
 
@@ -249,7 +251,7 @@
 
 def sums_kernel(at_ref, *refs):
     parts, (keep_ref, give_ref) = refs[:-2], refs[-2:]
-    wide = parts[0].shape[1] - 2 * HALF
+    wide = 0
     y_lo = at_ref[3]
     for m in range(2):
         for ref, which in ((keep_ref, y_lo), (give_ref, 1 - y_lo)):
@@ -276,10 +278,13 @@
 
 def mixing_kernel(at_ref, *refs):
     out = refs[-1]
-    for e, ref in enumerate(refs[:-1]):
-        src = lax.rem(at_ref[1] + GROUP - e, GROUP)
-        for h in range(ref.shape[0]):
-            out[pl.ds(src * ref.shape[0] + h, 1), :] = ref[h:h + 1, :]
+    rows = refs[0].shape[0]
+    for p in range(GROUP):
+        block = refs[0][...]
+        for e, ref in enumerate(refs[1:-1], 1):
+            src = lax.rem(at_ref[1] + GROUP - e, GROUP)
+            block = jnp.where(src == p, ref[...], block)
+        out[p * rows:(p + 1) * rows, :] = block
 
 
 SMEM = pl.BlockSpec(memory_space=pltpu.SMEM)
@@ -323,10 +328,11 @@
     heads = mixing.shape[0] // GROUP
     n_v = heads * 128
     span = GROUP * tok
-    at = jnp.stack([lax.rem(head_at, 2), lax.rem(me, GROUP), lax.div(me, GROUP), lax.div(head_at, 2)])
+    at = jnp.stack([lax.rem(head_at, 2), lax.rem(me, GROUP), lax.div(me, GROUP), lax.div(head_at, 2),
+                    (me >= peers - GROUP).astype(jnp.int32)])
 
     def to_group(x, by):
-        pairs = [(i, i + GROUP * by) for i in range(peers) if 0 <= i + GROUP * by < peers]
+        pairs = [(i, (i + GROUP * by) % peers) for i in range(peers)]
         return lax.ppermute(x, "seq", pairs)
 
     def turn(x, by):
@@ -341,23 +347,22 @@
 
     whole = lambda x: fixed(x.shape)
     wide = n_v + HALF
+    ahead_v = to_group(values, 1)
     *own, ahead = call(
         load_kernel, (), [SMEM] + [ANY] * 4,
-        [(VMEM, (tok, 2 * wide), B16)] * GROUP + [(VMEM, (tok, GROUP * n_v + HALF), B16)],
-        [pltpu.VMEM((tok, width), B16)] * 2 + [pltpu.SemaphoreType.DMA((11,))],
+        [(VMEM, (tok, 2 * wide), B16)] * GROUP + [(VMEM, (tok, HALF), B16)],
+        [pltpu.VMEM((tok, width), B16)] * 2 + [pltpu.SemaphoreType.DMA((10,))],
         (at, values, cotangent, k_shared, q_shared), 3, vmem=56)
     ahead = to_group(ahead, 1)
     own = turns(own)
-    before = call(split_kernel, (1,), [SMEM, whole(ahead)],
-                  [(fixed((tok, wide)), (tok, wide), B16)] * GROUP, [], (at, ahead), 1)
-    before = list(before)
-    own[0], before[0] = lax.optimization_barrier((own[0], before[0]))
+    before = call(split_kernel, (1,), [SMEM, whole(ahead_v), whole(ahead)],
+                  [(fixed((tok, wide)), (tok, wide), B16)] * GROUP, [], (at, ahead_v, ahead), 1)
     before = turns(before)
-    vk, qc, kq = call(
+    vk, q_half, c_own, kq = call(
         gather_kernel, (1,), [SMEM] + [whole(own[0])] * GROUP,
-        [(fixed((span, wide)), (span, wide), B16)] * 2
-        + [(fixed((span, 2 * HALF)), (span, 2 * HALF), B16)], [], (at, *own), 8)
-    x3 = to_group(qc, -1)
+        [(fixed((span, wide)), (span, wide), B16), (fixed((span, HALF)), (span, HALF), B16),
+         (fixed((span, n_v)), (span, n_v), B16), (fixed((span, 2 * HALF)), (span, 2 * HALF), B16)], [], (at, *own), 1)
+    q_next, c_next = to_group(q_half, -1), to_group(c_own, -1)
     kq_other = core_swap(kq)
     kp, mix = call(
         collect_kernel, (1,),
@@ -369,8 +374,8 @@
 
     stats, grad, w, k_all, q_all = call(
         functools.partial(scores_kernel, scale), (heads,),
-        [SMEM, head_first(1, width), by_head(span), fixed((span, HALF), 0, 2), by_head(span, 2),
-         fixed((span, HALF), 0, 0), fixed((span, HALF), 0, 0), fixed((span, HALF), 0, 1)]
+        [SMEM, head_first(1, width), by_head(span), fixed((span, HALF), 0, 2), by_head(span),
+         fixed((span, HALF)), fixed((span, HALF), 0, 0), fixed((span, HALF), 0, 1)]
         + [by_head(tok)] * GROUP + [fixed((span, HALF))] * 2,
         [(head_first(2, span), (heads, 2, span), F32),
          (head_first(2, 768, 256), (heads, 2, 768, 256), B16),
@@ -379,8 +384,10 @@
          (fixed((span, width)), (span, width), B16)],
         [pltpu.VMEM((2 * span, width), B16), pltpu.VMEM((span, width), B16),
          pltpu.VMEM((2 * span, 128), B16)],
-        (at, mix, vk, vk, qc, qc, kq_other, kq_other, *before, kp, kp_other), 0.1)
+        (at, mix, vk, vk, c_own, q_half, kq_other, kq_other, *before, kp, kp_other), 1)
     next_stats = to_group(stats, -1)
+    q_next, stats = lax.optimization_barrier((q_next, stats))
+    q_next_other = core_swap(q_next)
     dq_mine, dq_other, dmix = call(
         functools.partial(query_kernel, scale), (heads,),
         [SMEM, head_first(1, width), fixed((2 * span, width)), fixed((span, width)),
@@ -398,22 +405,20 @@
 
     dk, dv = call(
         key_kernel, (heads,),
-        [head_first(1, width), by_head(span, 2), fixed((span, width)),
+        [head_first(1, width), by_head(span), fixed((span, width)),
          head_first(2, 768, 256), head_first(3, 256, 256)],
         [(fixed((span, width)), (span, width), F32), (by_head(span), (span, n_v), F32)],
-        [], (mix, qc, q_all, grad, w), 0.3)
-    x3, dk = lax.optimization_barrier((x3, dk))
-    qn_other = core_swap(x3[:, :HALF])
+        [], (mix, c_own, q_all, grad, w), 0.3)
     dk_mine, dk_other, dv = call(
         functools.partial(next_kernel, scale), (heads,),
-        [head_first(1, width), by_head(span), fixed((span, HALF), 0, 2),
-         fixed((span, HALF), 0, 0), by_head(span, 2), fixed((span, HALF), 0, 0),
+        [SMEM, head_first(1, width), by_head(span), fixed((span, HALF), 0, 2),
+         fixed((span, HALF), 0, 0), by_head(span), fixed((span, HALF)),
          fixed((span, HALF)), head_first(2, span), fixed((span, width)), by_head(span)],
         [(fixed((span, HALF)), (span, HALF), F32), (fixed((span, HALF)), (span, HALF), B16),
          (by_head(span), (span, n_v), B16)],
         [pltpu.VMEM((span, width), B16), pltpu.VMEM((span, width), B16),
          pltpu.VMEM((span, width), F32)],
-        (mix, vk, vk, kq_other, x3, x3, qn_other, next_stats, dk, dv), 6)
+        (at, mix, vk, vk, kq_other, c_next, q_next, q_next_other, next_stats, dk, dv), 6)
     dk_other, dq_other, dmix = lax.optimization_barrier((dk_other, dq_other, dmix))
     dmix = exchange(dmix.reshape(heads, width), GROUP, 2 * GROUP)
 
@@ -423,12 +428,11 @@
         [(fixed((tok, n_v + 2 * HALF)), (tok, n_v + 2 * HALF), B16)] * GROUP, [],
         (at, dv, dk_mine, dk_got, dq_mine, dq_got), 1)
     back = turns(back)
-    keep, give = call(sums_kernel, (1,), [SMEM] + [whole(back[0])] * GROUP,
+    keep, give = call(sums_kernel, (1,), [SMEM] + [fixed((tok, 2 * HALF), 0, n_v // (2 * HALF))] * GROUP,
                       [(fixed((tok, HALF)), (tok, HALF), F32)] * 2, [], (at, *back), 1)
     dmix = exchange(dmix, 4 * GROUP, 8 * GROUP)
-    dmix, give = lax.optimization_barrier((dmix, give))
     got = lax.ppermute(give, "head", [(0, 2), (1, 3), (2, 0), (3, 1)])
-    (d_values,) = call(values_kernel, (1,), [SMEM] + [whole(back[0])] * GROUP,
+    (d_values,) = call(values_kernel, (1,), [SMEM] + [fixed((tok, n_v))] * GROUP,
                        [(fixed((tok, GROUP * n_v)), (tok, GROUP * n_v), B16)], [], (at, *back), 1)
     d_key, d_query = call(last_kernel, (1,), [whole(keep)] * 2,
                           [(fixed((tok, 128)), (tok, 128), B16)] * 2, [], (keep, got), 1)

time: 108 us -> 102 us (0.944)
  waiting for transfers between devices: 32.2 us -> 19.9 us
  starting transfers between devices: 46.6 us -> 53.3 us
    ppermute x3 -> x5, starting transfers between devices: 6.94 us -> 16.8 us  [to_group(): return lax.ppermute(x, 'seq', pairs)]
    ppermute x12, waiting for transfers between devices: 15.5 us -> 8.77 us  [turn(): return lax.ppermute(x, 'seq', pairs)]
    ppermute x6, starting transfers between devices: 17.4 us -> 13.5 us  [from_peer(): return lax.ppermute(x, 'seq', [(i, i ^ by) for i in range(peers)])]
    ppermute x3 -> x5, waiting for transfers between devices: 9.88 us -> 6.49 us  [to_group(): return lax.ppermute(x, 'seq', pairs)]
    ppermute x5, waiting for transfers between devices: 1.53 us -> 0.01 us  [core_swap(): return lax.ppermute(x, 'head', [(0, 1), (1, 0), (2, 3), (3, 2)])]
    ppermute x12, starting transfers between devices: 20 us -> 21.4 us  [turn(): return lax.ppermute(x, 'seq', pairs)]
  transfers between devices with their start and end apart: 27 -> 29, of which waited for: 10 -> 8; matrix products, arithmetic and copies ran while one was open for 0% -> 1% of each run, Pallas kernels for 15% -> 21%
where the time goes in v3:
time: 102 us
  starting transfers between devices  53.3 us (52%)
  Pallas kernels  27.5 us (27%)
  waiting for transfers between devices  19.9 us (20%)
    pallas_call x13, Pallas kernels, call(): pl.pallas_call(body, grid=grid, in_specs=ins, out_specs=[spec for spec, _...  27.5 us
    ppermute x12, starting transfers between devices, turn(): return lax.ppermute(x, 'seq', pairs)  21.4 us
    ppermute x5, starting transfers between devices, to_group(): return lax.ppermute(x, 'seq', pairs)  16.8 us
    ppermute x6, starting transfers between devices, from_peer(): return lax.ppermute(x, 'seq', [(i, i ^ by) for i in range(peers)])  13.5 us
    ppermute x12, waiting for transfers between devices, turn(): return lax.ppermute(x, 'seq', pairs)  8.77 us
    ppermute x5, waiting for transfers between devices, to_group(): return lax.ppermute(x, 'seq', pairs)  6.49 us
    ppermute x6, waiting for transfers between devices, from_peer(): return lax.ppermute(x, 'seq', [(i, i ^ by) for i in range(peers)])  3.59 us
  transfers between devices with their start and end apart: 29, of which 8 were waited for; matrix products, arithmetic and copies ran while one was open for 1% of the time, Pallas kernels for 21%

profile of v3, /device:TPU:8, one launch (start us, length us, event | category | flops | bytes accessed | tf_op | source)
XLA Modules:
  0.0 102.1 jit_solution(2990764353146920738)
XLA Ops:
  0.6 2.4 %collective-permute-start = (bf16[128,2048]{1,0:T(8,128)(2,1)}, bf16[128,2048]{1,0:T(8,128)(2,1)S(1)}, u32[]{:S(2)}, u32[]{:S(2)}) collective-permute-start(bf16[128,2048]{1,0:T(8,128)(2,1)} %v_ref.1), channel_id=1, source_target_pairs={{0,16},{4,20},{8,24},{12,28},{16,32},{20,36},{24,40},{28,44},{32,4... | collective-permute-start | bytes 1572872 | tf_op jit(solution)/shard_map/ppermute | solution.py:336
  3.0 0.7 stack.27.at_ref
  3.7 3.3 %shard_map.84 = (bf16[128,1536]{1,0:T(8,128)(2,1)}, bf16[128,1536]{1,0:T(8,128)(2,1)}, bf16[128,1536]{1,0:T(8,128)(2,1)}, bf16[128,1536]{1,0:T(8,128)(2,1)}, bf16[128,256]{1,0:T(8,128)(2,1)}) custom-call(s32[5]{0:T(128)} %stack.27.at_ref, bf16[128,2048]{1,0:T(8,128)(2,1)} %v_ref.1, bf16[128,2048]{1,0:T(8,128)(2,1)} %c_ref.1, bf16[128,512]{1,0:T(8,128)(2,1)} %k_ref.1, ...), custom_call_target="tpu_custom_call" | custom-call | flops 3000000000 | bytes 1000000 | tf_op jit(solution)/shard_map/pallas_call | solution.py:297
  7.0 1.6 %collective-permute-start.5 = (bf16[128,1536]{1,0:T(8,128)(2,1)}, bf16[128,1536]{1,0:T(8,128)(2,1)S(1)}, u32[]{:S(2)}, u32[]{:S(2)}) collective-permute-start(bf16[128,1536]{1,0:T(8,128)(2,1)} %get-tuple-element.51), channel_id=1, source_target_pairs={{0,4},{4,8},{8,12},{12,0},{16,20},{20,24},{24,28},{28,16},{32,36},... | collective-permute-start | bytes 1179656 | tf_op jit(solution)/shard_map/ppermute | solution.py:340
  8.6 2.7 %collective-permute-start.6 = (bf16[128,1536]{1,0:T(8,128)(2,1)}, bf16[128,1536]{1,0:T(8,128)(2,1)S(1)}, u32[]{:S(2)}, u32[]{:S(2)}) collective-permute-start(bf16[128,1536]{1,0:T(8,128)(2,1)} %get-tuple-element.52), channel_id=1, source_target_pairs={{0,8},{4,12},{8,0},{12,4},{16,24},{20,28},{24,16},{28,20},{32,40},... | collective-permute-start | bytes 1179656 | tf_op jit(solution)/shard_map/ppermute | solution.py:340
  11.3 1.4 %collective-permute-start.7 = (bf16[128,1536]{1,0:T(8,128)(2,1)}, bf16[128,1536]{1,0:T(8,128)(2,1)S(1)}, u32[]{:S(2)}, u32[]{:S(2)}) collective-permute-start(bf16[128,1536]{1,0:T(8,128)(2,1)} %get-tuple-element.53), channel_id=1, source_target_pairs={{0,12},{4,0},{8,4},{12,8},{16,28},{20,16},{24,20},{28,24},{32,44},... | collective-permute-start | bytes 1179656 | tf_op jit(solution)/shard_map/ppermute | solution.py:340
  12.8 2.6 %collective-permute-start.1 = (bf16[128,256]{1,0:T(8,128)(2,1)}, bf16[128,256]{1,0:T(8,128)(2,1)S(1)}, u32[]{:S(2)}, u32[]{:S(2)}) collective-permute-start(bf16[128,256]{1,0:T(8,128)(2,1)} %get-tuple-element.44), channel_id=1, source_target_pairs={{0,16},{4,20},{8,24},{12,28},{16,32},{20,36},{24,40},{28,44},{32,4... | collective-permute-start | bytes 196616 | tf_op jit(solution)/shard_map/ppermute | solution.py:336
  15.4 6.5 %collective-permute-done.1.k_ref = bf16[128,256]{1,0:T(8,128)(2,1)S(1)} collective-permute-done((bf16[128,256]{1,0:T(8,128)(2,1)}, bf16[128,256]{1,0:T(8,128)(2,1)S(1)}, u32[]{:S(2)}, u32[]{:S(2)}) %collective-permute-start.1) | collective-permute-done | bytes 65568 | tf_op jit(solution)/shard_map/ppermute | solution.py:336
  21.8 0.6 shard_map.85
  22.4 1.6 %collective-permute-start.2 = (bf16[128,768]{1,0:T(8,128)(2,1)S(1)}, bf16[128,768]{1,0:T(8,128)(2,1)S(1)}, u32[]{:S(2)}, u32[]{:S(2)}) collective-permute-start(bf16[128,768]{1,0:T(8,128)(2,1)S(1)} %get-tuple-element.46), channel_id=1, source_target_pairs={{0,4},{4,8},{8,12},{12,0},{16,20},{20,24},{24,28},{28,16},{32,36},... | collective-permute-start | bytes 589832 | tf_op jit(solution)/shard_map/ppermute | solution.py:340
  24.0 2.7 %collective-permute-start.3 = (bf16[128,768]{1,0:T(8,128)(2,1)S(1)}, bf16[128,768]{1,0:T(8,128)(2,1)S(1)}, u32[]{:S(2)}, u32[]{:S(2)}) collective-permute-start(bf16[128,768]{1,0:T(8,128)(2,1)S(1)} %get-tuple-element.47), channel_id=1, source_target_pairs={{0,8},{4,12},{8,0},{12,4},{16,24},{20,28},{24,16},{28,20},{32,40},... | collective-permute-start | bytes 589832 | tf_op jit(solution)/shard_map/ppermute | solution.py:340
  26.7 1.4 %collective-permute-start.4 = (bf16[128,768]{1,0:T(8,128)(2,1)S(1)}, bf16[128,768]{1,0:T(8,128)(2,1)S(1)}, u32[]{:S(2)}, u32[]{:S(2)}) collective-permute-start(bf16[128,768]{1,0:T(8,128)(2,1)S(1)} %get-tuple-element.48), channel_id=1, source_target_pairs={{0,12},{4,0},{8,4},{12,8},{16,28},{20,16},{24,20},{28,24},{32,44},... | collective-permute-start | bytes 589832 | tf_op jit(solution)/shard_map/ppermute | solution.py:340
  28.2 1.8 %collective-permute-done.6.p2_ref = bf16[128,1536]{1,0:T(8,128)(2,1)S(1)} collective-permute-done((bf16[128,1536]{1,0:T(8,128)(2,1)}, bf16[128,1536]{1,0:T(8,128)(2,1)S(1)}, u32[]{:S(2)}, u32[]{:S(2)}) %collective-permute-start.6) | collective-permute-done | bytes 393248 | tf_op jit(solution)/shard_map/ppermute | solution.py:340
  30.0 0.7 shard_map.87
  30.8 3.4 %collective-permute-done.2.k1_ref.vp1_ref = bf16[128,768]{1,0:T(8,128)(2,1)S(1)} collective-permute-done((bf16[128,768]{1,0:T(8,128)(2,1)S(1)}, bf16[128,768]{1,0:T(8,128)(2,1)S(1)}, u32[]{:S(2)}, u32[]{:S(2)}) %collective-permute-start.2) | collective-permute-done | bytes 196640 | tf_op jit(solution)/shard_map/ppermute | solution.py:340
  34.2 2.7 %collective-permute-done.3.k2_ref.vp2_ref = bf16[128,768]{1,0:T(8,128)(2,1)S(1)} collective-permute-done((bf16[128,768]{1,0:T(8,128)(2,1)S(1)}, bf16[128,768]{1,0:T(8,128)(2,1)S(1)}, u32[]{:S(2)}, u32[]{:S(2)}) %collective-permute-start.3) | collective-permute-done | bytes 196640 | tf_op jit(solution)/shard_map/ppermute | solution.py:340
  36.9 0.6 shard_map.86
  37.6 5.7 %collective-permute-start.10 = (bf16[512,256]{1,0:T(8,128)(2,1)S(1)}, bf16[512,256]{1,0:T(8,128)(2,1)S(1)}, u32[]{:S(2)}, u32[]{:S(2)}) collective-permute-start(bf16[512,256]{1,0:T(8,128)(2,1)S(1)} %get-tuple-element.57.qm_ref), channel_id=1, source_target_pairs={{0,240},{4,244},{8,248},{12,252},{16,0},{20,4},{24,8},{28,12},{32,... | collective-permute-start | bytes 786440 | tf_op jit(solution)/shard_map/ppermute | solution.py:336
  43.3 3.2 %collective-permute-start.9 = (bf16[512,512]{1,0:T(8,128)(2,1)S(1)}, bf16[512,512]{1,0:T(8,128)(2,1)S(1)}, u32[]{:S(2)}, u32[]{:S(2)}) collective-permute-start(bf16[512,512]{1,0:T(8,128)(2,1)S(1)} %get-tuple-element.56.c_ref), channel_id=1, source_target_pairs={{0,240},{4,244},{8,248},{12,252},{16,0},{20,4},{24,8},{28,12},{32,... | collective-permute-start | bytes 1572872 | tf_op jit(solution)/shard_map/ppermute | solution.py:336
  46.6 6.5 %shard_map.88 = (f32[4,2,512]{2,1,0:T(2,128)S(1)}, bf16[4,2,768,256]{3,2,1,0:T(8,128)(2,1)S(1)}, bf16[4,3,256,256]{3,2,1,0:T(8,128)(2,1)S(1)}, bf16[1024,512]{1,0:T(8,128)(2,1)S(1)}, bf16[512,512]{1,0:T(8,128)(2,1)S(1)}) custom-call(s32[5]{0:T(128)S(1)} %copy-done, f32[4,1,512]{2,1,0:T(1,128)S(1)} %get-tuple-element.49.mix_ref, ...), custom_call_target="tpu_custom_call" | custom-call | flops 1000000000 | bytes 1000000 | tf_op jit(solution)/shard_map/pallas_call | solution.py:297
  53.2 2.9 %collective-permute-start.13 = (f32[4,2,512]{2,1,0:T(2,128)S(1)}, f32[4,2,512]{2,1,0:T(2,128)S(1)}, u32[]{:S(2)}, u32[]{:S(2)}) collective-permute-start(f32[4,2,512]{2,1,0:T(2,128)S(1)} %get-tuple-element.59), channel_id=1, source_target_pairs={{0,240},{4,244},{8,248},{12,252},{16,0},{20,4},{24,8},{28,12},{32,... | collective-permute-start | bytes 49160 | tf_op jit(solution)/shard_map/ppermute | solution.py:336
  56.1 3.4 %shard_map.91 = (f32[512,256]{1,0:T(8,128)S(1)}, bf16[512,256]{1,0:T(8,128)(2,1)S(1)}, f32[4,1,512]{2,1,0:T(1,128)S(1)}) custom-call(s32[5]{0:T(128)S(1)} %copy-done, f32[4,1,512]{2,1,0:T(1,128)S(1)} %get-tuple-element.49.mix_ref, bf16[1024,512]{1,0:T(8,128)(2,1)S(1)} %get-tuple-element.69.k_ref, bf16[512,512]{1,0:T(8,128)(2,1)S(1)} %get-tuple-element.61.q_ref, ...), custom_call_target="tpu_custom_call" | custom-call | flops 300000000 | bytes 1000000 | tf_op jit(solution)/shard_map/pallas_call | solution.py:297
  59.5 2.3 %shard_map.89 = (f32[512,512]{1,0:T(8,128)S(1)}, f32[512,512]{1,0:T(8,128)S(1)}) custom-call(f32[4,1,512]{2,1,0:T(1,128)S(1)} %get-tuple-element.49.mix_ref, bf16[512,512]{1,0:T(8,128)(2,1)S(1)} %get-tuple-element.56.c_ref, bf16[512,512]{1,0:T(8,128)(2,1)S(1)} %get-tuple-element.61.q_ref, bf16[4,2,768,256]{3,2,1,0:T(8,128)(2,1)S(1)} %get-tuple-element.62.grad_ref, ...), custom_call_target="tpu_custom_call" | custom-call | flops 300000000 | bytes 1000000 | tf_op jit(solution)/shard_map/pallas_call | solution.py:297
  61.9 5.6 %shard_map.90 = (f32[512,256]{1,0:T(8,128)S(1)}, bf16[512,256]{1,0:T(8,128)(2,1)S(1)}, bf16[512,512]{1,0:T(8,128)(2,1)S(1)}) custom-call(s32[5]{0:T(128)S(1)} %copy-done, f32[4,1,512]{2,1,0:T(1,128)S(1)} %get-tuple-element.49.mix_ref, bf16[512,768]{1,0:T(8,128)(2,1)S(1)} %get-tuple-element.54.v_ref.km_ref, ...), custom_call_target="tpu_custom_call" | custom-call | flops 6000000000 | bytes 1000000 | tf_op jit(solution)/shard_map/pallas_call | solution.py:297
  67.5 0.3 collective-permute-start.14
  67.8 0.3 collective-permute-start.15
  68.1 1.1 %collective-permute-start.20 = (f32[4,512]{1,0:T(4,128)S(1)}, f32[4,512]{1,0:T(4,128)S(1)}, u32[]{:S(2)}, u32[]{:S(2)}) collective-permute-start(f32[4,512]{1,0:T(4,128)S(1)} %bitcast.10), channel_id=1, source_target_pairs={{0,16},{4,20},{8,24},{12,28},{16,0},{20,4},{24,8},{28,12},{32,48},... | collective-permute-start | bytes 24584 | tf_op jit(solution)/shard_map/ppermute | solution.py:401
  69.2 1.9 %collective-permute-start.21 = (f32[4,512]{1,0:T(4,128)S(1)}, f32[4,512]{1,0:T(4,128)S(1)}, u32[]{:S(2)}, u32[]{:S(2)}) collective-permute-start(f32[4,512]{1,0:T(4,128)S(1)} %bitcast.11), channel_id=1, source_target_pairs={{0,32},{4,36},{8,40},{12,44},{16,48},{20,52},{24,56},{28,60},{32,0... | collective-permute-start | bytes 24584 | tf_op jit(solution)/shard_map/ppermute | solution.py:401
  71.1 2.0 %collective-permute-start.22 = (f32[4,512]{1,0:T(4,128)S(1)}, f32[4,512]{1,0:T(4,128)S(1)}, u32[]{:S(2)}, u32[]{:S(2)}) collective-permute-start(f32[4,512]{1,0:T(4,128)S(1)} %bitcast.12), channel_id=1, source_target_pairs={{0,48},{4,52},{8,56},{12,60},{16,32},{20,36},{24,40},{28,44},{32,1... | collective-permute-start | bytes 24584 | tf_op jit(solution)/shard_map/ppermute | solution.py:401
  73.1 0.7 shard_map.92
  73.8 1.4 %collective-permute-start.16 = (bf16[128,1024]{1,0:T(8,128)(2,1)S(1)}, bf16[128,1024]{1,0:T(8,128)(2,1)S(1)}, u32[]{:S(2)}, u32[]{:S(2)}) collective-permute-start(bf16[128,1024]{1,0:T(8,128)(2,1)S(1)} %get-tuple-element.76), channel_id=1, source_target_pairs={{0,4},{4,8},{8,12},{12,0},{16,20},{20,24},{24,28},{28,16},{32,36},... | collective-permute-start | bytes 786440 | tf_op jit(solution)/shard_map/ppermute | solution.py:340
  75.1 2.4 %collective-permute-start.17 = (bf16[128,1024]{1,0:T(8,128)(2,1)S(1)}, bf16[128,1024]{1,0:T(8,128)(2,1)S(1)}, u32[]{:S(2)}, u32[]{:S(2)}) collective-permute-start(bf16[128,1024]{1,0:T(8,128)(2,1)S(1)} %get-tuple-element.77), channel_id=1, source_target_pairs={{0,8},{4,12},{8,0},{12,4},{16,24},{20,28},{24,16},{28,20},{32,40},... | collective-permute-start | bytes 786440 | tf_op jit(solution)/shard_map/ppermute | solution.py:340
  77.5 1.6 %collective-permute-start.18 = (bf16[128,1024]{1,0:T(8,128)(2,1)S(1)}, bf16[128,1024]{1,0:T(8,128)(2,1)S(1)}, u32[]{:S(2)}, u32[]{:S(2)}) collective-permute-start(bf16[128,1024]{1,0:T(8,128)(2,1)S(1)} %get-tuple-element.78), channel_id=1, source_target_pairs={{0,12},{4,0},{8,4},{12,8},{16,28},{20,16},{24,20},{28,24},{32,44},... | collective-permute-start | bytes 786440 | tf_op jit(solution)/shard_map/ppermute | solution.py:340
  79.1 3.8 %collective-permute-start.23 = (f32[4,512]{1,0:T(4,128)S(1)}, f32[4,512]{1,0:T(4,128)S(1)}, u32[]{:S(2)}, u32[]{:S(2)}) collective-permute-start(f32[4,512]{1,0:T(4,128)S(1)} %add_add_fusion.1), channel_id=1, source_target_pairs={{0,64},{4,68},{8,72},{12,76},{16,80},{20,84},{24,88},{28,92},{32,9... | collective-permute-start | bytes 24584 | tf_op jit(solution)/shard_map/ppermute | solution.py:401
  82.9 2.5 %collective-permute-start.24 = (f32[4,512]{1,0:T(4,128)S(1)}, f32[4,512]{1,0:T(4,128)S(1)}, u32[]{:S(2)}, u32[]{:S(2)}) collective-permute-start(f32[4,512]{1,0:T(4,128)S(1)} %add_add_fusion.1), channel_id=1, source_target_pairs={{0,128},{4,132},{8,136},{12,140},{16,144},{20,148},{24,152},{28,15... | collective-permute-start | bytes 24584 | tf_op jit(solution)/shard_map/ppermute | solution.py:401
  85.4 2.2 %collective-permute-start.25 = (f32[4,512]{1,0:T(4,128)S(1)}, f32[4,512]{1,0:T(4,128)S(1)}, u32[]{:S(2)}, u32[]{:S(2)}) collective-permute-start(f32[4,512]{1,0:T(4,128)S(1)} %add_add_fusion.1), channel_id=1, source_target_pairs={{0,192},{4,196},{8,200},{12,204},{16,208},{20,212},{24,216},{28,22... | collective-permute-start | bytes 24584 | tf_op jit(solution)/shard_map/ppermute | solution.py:401
  87.6 2.8 %collective-permute-done.24 = f32[4,512]{1,0:T(4,128)S(1)} collective-permute-done((f32[4,512]{1,0:T(4,128)S(1)}, f32[4,512]{1,0:T(4,128)S(1)}, u32[]{:S(2)}, u32[]{:S(2)}) %collective-permute-start.24) | collective-permute-done | bytes 8224 | tf_op jit(solution)/shard_map/ppermute | solution.py:401
  90.5 0.7 collective-permute-done.25
  91.2 0.6 collective-permute-start.26
  91.9 2.4 %collective-permute-start.27 = (f32[4,512]{1,0:T(4,128)S(1)}, f32[4,512]{1,0:T(4,128)S(1)}, u32[]{:S(2)}, u32[]{:S(2)}) collective-permute-start(f32[4,512]{1,0:T(4,128)S(1)} %add_add_fusion.refs_0_), channel_id=1, source_target_pairs={{0,8},{4,12},{8,0},{12,4},{16,24},{20,28},{24,16},{28,20},{32,40},... | collective-permute-start | bytes 24584 | tf_op jit(solution)/shard_map/ppermute | solution.py:340
  94.2 1.6 %collective-permute-start.28 = (f32[4,512]{1,0:T(4,128)S(1)}, f32[4,512]{1,0:T(4,128)S(1)}, u32[]{:S(2)}, u32[]{:S(2)}) collective-permute-start(f32[4,512]{1,0:T(4,128)S(1)} %add_add_fusion.refs_0_), channel_id=1, source_target_pairs={{0,12},{4,0},{8,4},{12,8},{16,28},{20,16},{24,20},{28,24},{32,44},... | collective-permute-start | bytes 24584 | tf_op jit(solution)/shard_map/ppermute | solution.py:340
  95.8 0.6 shard_map.93
  96.4 0.7 collective-permute-start.19
  97.1 0.8 collective-permute-done.28.refs_3_
  97.9 1.2 %shard_map.96 = f32[16,512]{1,0:T(8,128)} custom-call(s32[5]{0:T(128)S(1)} %copy-done, f32[4,512]{1,0:T(4,128)S(1)} %add_add_fusion.refs_0_, f32[4,512]{1,0:T(4,128)S(1)} %collective-permute-done.26.refs_1_, f32[4,512]{1,0:T(4,128)S(1)} %collective-permute-done.27.refs_2_, f32[4,512]{1,0:T(4,128)S(1)} %collective-permute-done.28.refs_3_), custom_call_target="tpu_custom_call" | custom-call | flops 1000000000 | bytes 1000000 | tf_op jit(solution)/shard_map/pallas_call | solution.py:297
  99.1 1.4 %shard_map.95 = bf16[128,2048]{1,0:T(8,128)(2,1)} custom-call(s32[5]{0:T(128)S(1)} %copy-done, bf16[128,1024]{1,0:T(8,128)(2,1)S(1)} %get-tuple-element.75.refs_0_, bf16[128,1024]{1,0:T(8,128)(2,1)S(1)} %collective-permute-done.16.refs_1_, bf16[128,1024]{1,0:T(8,128)(2,1)S(1)} %collective-permute-done.17.refs_2_, ...), custom_call_target="tpu_custom_call" | custom-call | flops 1000000000 | bytes 1000000 | tf_op jit(solution)/shard_map/pallas_call | solution.py:297
  100.5 1.0 %collective-permute-done.19.got_ref = f32[128,256]{1,0:T(8,128)S(1)} collective-permute-done((f32[128,256]{1,0:T(8,128)S(1)}, f32[128,256]{1,0:T(8,128)S(1)}, u32[]{:S(2)}, u32[]{:S(2)}) %collective-permute-start.19) | collective-permute-done | bytes 131104 | tf_op jit(solution)/shard_map/ppermute | solution.py:434
  101.5 0.6 shard_map.94
  (33 shorter events, 0.4 us)
Async XLA Ops:
  0.6 21.2 %collective-permute-start = (bf16[128,2048]{1,0:T(8,128)(2,1)}, bf16[128,2048]{1,0:T(8,128)(2,1)S(1)}, u32[]{:S(2)}, u32[]{:S(2)}) collective-permute-start(bf16[128,2048]{1,0:T(8,128)(2,1)} %v_ref.1), channel_id=1, source_target_pairs={{0,16},{4,20},{8,24},{12,28},{16,32},{20,36},{24,40},{28,44},{32,4... | collective-permute-start | bytes 1572872 | tf_op jit(solution)/shard_map/ppermute | solution.py:336
  3.7 18.2 %copy-start = (s32[5]{0:T(128)S(1)}, s32[5]{0:T(128)}, u32[]{:S(2)}) copy-start(s32[5]{0:T(128)} %stack.27.at_ref) | copy-start | bytes 64
  7.0 23.0 %copy-start.2 = (bf16[128,1536]{1,0:T(8,128)(2,1)S(1)}, bf16[128,1536]{1,0:T(8,128)(2,1)}, u32[]{:S(2)}) copy-start(bf16[128,1536]{1,0:T(8,128)(2,1)} %get-tuple-element.50.p0_ref) | copy-start | bytes 1179652
  7.0 19.7 %collective-permute-start.5 = (bf16[128,1536]{1,0:T(8,128)(2,1)}, bf16[128,1536]{1,0:T(8,128)(2,1)S(1)}, u32[]{:S(2)}, u32[]{:S(2)}) collective-permute-start(bf16[128,1536]{1,0:T(8,128)(2,1)} %get-tuple-element.51), channel_id=1, source_target_pairs={{0,4},{4,8},{8,12},{12,0},{16,20},{20,24},{24,28},{28,16},{32,36},... | collective-permute-start | bytes 1179656 | tf_op jit(solution)/shard_map/ppermute | solution.py:340
  8.6 21.4 %collective-permute-start.6 = (bf16[128,1536]{1,0:T(8,128)(2,1)}, bf16[128,1536]{1,0:T(8,128)(2,1)S(1)}, u32[]{:S(2)}, u32[]{:S(2)}) collective-permute-start(bf16[128,1536]{1,0:T(8,128)(2,1)} %get-tuple-element.52), channel_id=1, source_target_pairs={{0,8},{4,12},{8,0},{12,4},{16,24},{20,28},{24,16},{28,20},{32,40},... | collective-permute-start | bytes 1179656 | tf_op jit(solution)/shard_map/ppermute | solution.py:340
  11.3 18.7 %collective-permute-start.7 = (bf16[128,1536]{1,0:T(8,128)(2,1)}, bf16[128,1536]{1,0:T(8,128)(2,1)S(1)}, u32[]{:S(2)}, u32[]{:S(2)}) collective-permute-start(bf16[128,1536]{1,0:T(8,128)(2,1)} %get-tuple-element.53), channel_id=1, source_target_pairs={{0,12},{4,0},{8,4},{12,8},{16,28},{20,16},{24,20},{28,24},{32,44},... | collective-permute-start | bytes 1179656 | tf_op jit(solution)/shard_map/ppermute | solution.py:340
  12.8 24.2 %copy-start.1 = (f32[16,512]{1,0:T(8,128)S(1)}, f32[16,512]{1,0:T(8,128)}, u32[]{:S(2)}) copy-start(f32[16,512]{1,0:T(8,128)} %mixing_ref.1) | copy-start | bytes 98308
  12.8 9.1 %collective-permute-start.1 = (bf16[128,256]{1,0:T(8,128)(2,1)}, bf16[128,256]{1,0:T(8,128)(2,1)S(1)}, u32[]{:S(2)}, u32[]{:S(2)}) collective-permute-start(bf16[128,256]{1,0:T(8,128)(2,1)} %get-tuple-element.44), channel_id=1, source_target_pairs={{0,16},{4,20},{8,24},{12,28},{16,32},{20,36},{24,40},{28,44},{32,4... | collective-permute-start | bytes 196616 | tf_op jit(solution)/shard_map/ppermute | solution.py:336
  22.4 11.8 %collective-permute-start.2 = (bf16[128,768]{1,0:T(8,128)(2,1)S(1)}, bf16[128,768]{1,0:T(8,128)(2,1)S(1)}, u32[]{:S(2)}, u32[]{:S(2)}) collective-permute-start(bf16[128,768]{1,0:T(8,128)(2,1)S(1)} %get-tuple-element.46), channel_id=1, source_target_pairs={{0,4},{4,8},{8,12},{12,0},{16,20},{20,24},{24,28},{28,16},{32,36},... | collective-permute-start | bytes 589832 | tf_op jit(solution)/shard_map/ppermute | solution.py:340
  24.0 12.9 %collective-permute-start.3 = (bf16[128,768]{1,0:T(8,128)(2,1)S(1)}, bf16[128,768]{1,0:T(8,128)(2,1)S(1)}, u32[]{:S(2)}, u32[]{:S(2)}) collective-permute-start(bf16[128,768]{1,0:T(8,128)(2,1)S(1)} %get-tuple-element.47), channel_id=1, source_target_pairs={{0,8},{4,12},{8,0},{12,4},{16,24},{20,28},{24,16},{28,20},{32,40},... | collective-permute-start | bytes 589832 | tf_op jit(solution)/shard_map/ppermute | solution.py:340
  26.7 10.2 %collective-permute-start.4 = (bf16[128,768]{1,0:T(8,128)(2,1)S(1)}, bf16[128,768]{1,0:T(8,128)(2,1)S(1)}, u32[]{:S(2)}, u32[]{:S(2)}) collective-permute-start(bf16[128,768]{1,0:T(8,128)(2,1)S(1)} %get-tuple-element.48), channel_id=1, source_target_pairs={{0,12},{4,0},{8,4},{12,8},{16,28},{20,16},{24,20},{28,24},{32,44},... | collective-permute-start | bytes 589832 | tf_op jit(solution)/shard_map/ppermute | solution.py:340
  30.7 15.9 %collective-permute-start.8 = (bf16[512,512]{1,0:T(8,128)(2,1)S(1)}, bf16[512,512]{1,0:T(8,128)(2,1)S(1)}, u32[]{:S(2)}, u32[]{:S(2)}) collective-permute-start(bf16[512,512]{1,0:T(8,128)(2,1)S(1)} %get-tuple-element.55), channel_id=1, source_target_pairs={{0,1},{1,0},{2,3},{3,2},{4,5},{5,4},{6,7},{7,6},{8,9},{9,8},{10,11... | collective-permute-start | bytes 1572872 | tf_op jit(solution)/shard_map/ppermute | solution.py:346
  37.5 9.0 %collective-permute-start.11 = (bf16[512,256]{1,0:T(8,128)(2,1)S(1)}, bf16[512,256]{1,0:T(8,128)(2,1)S(1)}, u32[]{:S(2)}, u32[]{:S(2)}) collective-permute-start(bf16[512,256]{1,0:T(8,128)(2,1)S(1)} %get-tuple-element.58.kpm_ref), channel_id=1, source_target_pairs={{0,1},{1,0},{2,3},{3,2},{4,5},{5,4},{6,7},{7,6},{8,9},{9,8},{10,11... | collective-permute-start | bytes 786440 | tf_op jit(solution)/shard_map/ppermute | solution.py:346
  37.6 15.4 %collective-permute-start.10 = (bf16[512,256]{1,0:T(8,128)(2,1)S(1)}, bf16[512,256]{1,0:T(8,128)(2,1)S(1)}, u32[]{:S(2)}, u32[]{:S(2)}) collective-permute-start(bf16[512,256]{1,0:T(8,128)(2,1)S(1)} %get-tuple-element.57.qm_ref), channel_id=1, source_target_pairs={{0,240},{4,244},{8,248},{12,252},{16,0},{20,4},{24,8},{28,12},{32,... | collective-permute-start | bytes 786440 | tf_op jit(solution)/shard_map/ppermute | solution.py:336
  43.3 18.5 %collective-permute-start.9 = (bf16[512,512]{1,0:T(8,128)(2,1)S(1)}, bf16[512,512]{1,0:T(8,128)(2,1)S(1)}, u32[]{:S(2)}, u32[]{:S(2)}) collective-permute-start(bf16[512,512]{1,0:T(8,128)(2,1)S(1)} %get-tuple-element.56.c_ref), channel_id=1, source_target_pairs={{0,240},{4,244},{8,248},{12,252},{16,0},{20,4},{24,8},{28,12},{32,... | collective-permute-start | bytes 1572872 | tf_op jit(solution)/shard_map/ppermute | solution.py:336
  53.1 8.8 %collective-permute-start.12 = (bf16[512,256]{1,0:T(8,128)(2,1)S(1)}, bf16[512,256]{1,0:T(8,128)(2,1)S(1)}, u32[]{:S(2)}, u32[]{:S(2)}) collective-permute-start(bf16[512,256]{1,0:T(8,128)(2,1)S(1)} %collective-permute-done.10.qnm_ref), channel_id=1, source_target_pairs={{0,1},{1,0},{2,3},{3,2},{4,5},{5,4},{6,7},{7,6},{8,9},{9,8},{10,11... | collective-permute-start | bytes 786440 | tf_op jit(solution)/shard_map/ppermute | solution.py:346
  53.2 8.7 %collective-permute-start.13 = (f32[4,2,512]{2,1,0:T(2,128)S(1)}, f32[4,2,512]{2,1,0:T(2,128)S(1)}, u32[]{:S(2)}, u32[]{:S(2)}) collective-permute-start(f32[4,2,512]{2,1,0:T(2,128)S(1)} %get-tuple-element.59), channel_id=1, source_target_pairs={{0,240},{4,244},{8,248},{12,252},{16,0},{20,4},{24,8},{28,12},{32,... | collective-permute-start | bytes 49160 | tf_op jit(solution)/shard_map/ppermute | solution.py:336
  67.5 5.6 %collective-permute-start.14 = (bf16[512,256]{1,0:T(8,128)(2,1)S(1)}, bf16[512,256]{1,0:T(8,128)(2,1)S(1)}, u32[]{:S(2)}, u32[]{:S(2)}) collective-permute-start(bf16[512,256]{1,0:T(8,128)(2,1)S(1)} %get-tuple-element.72), channel_id=1, source_target_pairs={{0,1},{1,0},{2,3},{3,2},{4,5},{5,4},{6,7},{7,6},{8,9},{9,8},{10,11... | collective-permute-start | bytes 786440 | tf_op jit(solution)/shard_map/ppermute | solution.py:346
  67.8 5.3 %collective-permute-start.15 = (bf16[512,256]{1,0:T(8,128)(2,1)S(1)}, bf16[512,256]{1,0:T(8,128)(2,1)S(1)}, u32[]{:S(2)}, u32[]{:S(2)}) collective-permute-start(bf16[512,256]{1,0:T(8,128)(2,1)S(1)} %get-tuple-element.74), channel_id=1, source_target_pairs={{0,1},{1,0},{2,3},{3,2},{4,5},{5,4},{6,7},{7,6},{8,9},{9,8},{10,11... | collective-permute-start | bytes 786440 | tf_op jit(solution)/shard_map/ppermute | solution.py:346
  68.1 9.5 %collective-permute-start.20 = (f32[4,512]{1,0:T(4,128)S(1)}, f32[4,512]{1,0:T(4,128)S(1)}, u32[]{:S(2)}, u32[]{:S(2)}) collective-permute-start(f32[4,512]{1,0:T(4,128)S(1)} %bitcast.10), channel_id=1, source_target_pairs={{0,16},{4,20},{8,24},{12,28},{16,0},{20,4},{24,8},{28,12},{32,48},... | collective-permute-start | bytes 24584 | tf_op jit(solution)/shard_map/ppermute | solution.py:401
  69.2 10.0 %collective-permute-start.21 = (f32[4,512]{1,0:T(4,128)S(1)}, f32[4,512]{1,0:T(4,128)S(1)}, u32[]{:S(2)}, u32[]{:S(2)}) collective-permute-start(f32[4,512]{1,0:T(4,128)S(1)} %bitcast.11), channel_id=1, source_target_pairs={{0,32},{4,36},{8,40},{12,44},{16,48},{20,52},{24,56},{28,60},{32,0... | collective-permute-start | bytes 24584 | tf_op jit(solution)/shard_map/ppermute | solution.py:401
  71.1 8.1 %collective-permute-start.22 = (f32[4,512]{1,0:T(4,128)S(1)}, f32[4,512]{1,0:T(4,128)S(1)}, u32[]{:S(2)}, u32[]{:S(2)}) collective-permute-start(f32[4,512]{1,0:T(4,128)S(1)} %bitcast.12), channel_id=1, source_target_pairs={{0,48},{4,52},{8,56},{12,60},{16,32},{20,36},{24,40},{28,44},{32,1... | collective-permute-start | bytes 24584 | tf_op jit(solution)/shard_map/ppermute | solution.py:401
  73.8 20.5 %collective-permute-start.16 = (bf16[128,1024]{1,0:T(8,128)(2,1)S(1)}, bf16[128,1024]{1,0:T(8,128)(2,1)S(1)}, u32[]{:S(2)}, u32[]{:S(2)}) collective-permute-start(bf16[128,1024]{1,0:T(8,128)(2,1)S(1)} %get-tuple-element.76), channel_id=1, source_target_pairs={{0,4},{4,8},{8,12},{12,0},{16,20},{20,24},{24,28},{28,16},{32,36},... | collective-permute-start | bytes 786440 | tf_op jit(solution)/shard_map/ppermute | solution.py:340
  75.1 20.7 %collective-permute-start.17 = (bf16[128,1024]{1,0:T(8,128)(2,1)S(1)}, bf16[128,1024]{1,0:T(8,128)(2,1)S(1)}, u32[]{:S(2)}, u32[]{:S(2)}) collective-permute-start(bf16[128,1024]{1,0:T(8,128)(2,1)S(1)} %get-tuple-element.77), channel_id=1, source_target_pairs={{0,8},{4,12},{8,0},{12,4},{16,24},{20,28},{24,16},{28,20},{32,40},... | collective-permute-start | bytes 786440 | tf_op jit(solution)/shard_map/ppermute | solution.py:340
  77.5 18.3 %collective-permute-start.18 = (bf16[128,1024]{1,0:T(8,128)(2,1)S(1)}, bf16[128,1024]{1,0:T(8,128)(2,1)S(1)}, u32[]{:S(2)}, u32[]{:S(2)}) collective-permute-start(bf16[128,1024]{1,0:T(8,128)(2,1)S(1)} %get-tuple-element.78), channel_id=1, source_target_pairs={{0,12},{4,0},{8,4},{12,8},{16,28},{20,16},{24,20},{28,24},{32,44},... | collective-permute-start | bytes 786440 | tf_op jit(solution)/shard_map/ppermute | solution.py:340
  79.1 6.3 %collective-permute-start.23 = (f32[4,512]{1,0:T(4,128)S(1)}, f32[4,512]{1,0:T(4,128)S(1)}, u32[]{:S(2)}, u32[]{:S(2)}) collective-permute-start(f32[4,512]{1,0:T(4,128)S(1)} %add_add_fusion.1), channel_id=1, source_target_pairs={{0,64},{4,68},{8,72},{12,76},{16,80},{20,84},{24,88},{28,92},{32,9... | collective-permute-start | bytes 24584 | tf_op jit(solution)/shard_map/ppermute | solution.py:401
  82.9 7.6 %collective-permute-start.24 = (f32[4,512]{1,0:T(4,128)S(1)}, f32[4,512]{1,0:T(4,128)S(1)}, u32[]{:S(2)}, u32[]{:S(2)}) collective-permute-start(f32[4,512]{1,0:T(4,128)S(1)} %add_add_fusion.1), channel_id=1, source_target_pairs={{0,128},{4,132},{8,136},{12,140},{16,144},{20,148},{24,152},{28,15... | collective-permute-start | bytes 24584 | tf_op jit(solution)/shard_map/ppermute | solution.py:401
  85.4 5.8 %collective-permute-start.25 = (f32[4,512]{1,0:T(4,128)S(1)}, f32[4,512]{1,0:T(4,128)S(1)}, u32[]{:S(2)}, u32[]{:S(2)}) collective-permute-start(f32[4,512]{1,0:T(4,128)S(1)} %add_add_fusion.1), channel_id=1, source_target_pairs={{0,192},{4,196},{8,200},{12,204},{16,208},{20,212},{24,216},{28,22... | collective-permute-start | bytes 24584 | tf_op jit(solution)/shard_map/ppermute | solution.py:401
  91.2 5.9 %collective-permute-start.26 = (f32[4,512]{1,0:T(4,128)S(1)}, f32[4,512]{1,0:T(4,128)S(1)}, u32[]{:S(2)}, u32[]{:S(2)}) collective-permute-start(f32[4,512]{1,0:T(4,128)S(1)} %add_add_fusion.refs_0_), channel_id=1, source_target_pairs={{0,4},{4,8},{8,12},{12,0},{16,20},{20,24},{24,28},{28,16},{32,36},... | collective-permute-start | bytes 24584 | tf_op jit(solution)/shard_map/ppermute | solution.py:340
  91.9 5.3 %collective-permute-start.27 = (f32[4,512]{1,0:T(4,128)S(1)}, f32[4,512]{1,0:T(4,128)S(1)}, u32[]{:S(2)}, u32[]{:S(2)}) collective-permute-start(f32[4,512]{1,0:T(4,128)S(1)} %add_add_fusion.refs_0_), channel_id=1, source_target_pairs={{0,8},{4,12},{8,0},{12,4},{16,24},{20,28},{24,16},{28,20},{32,40},... | collective-permute-start | bytes 24584 | tf_op jit(solution)/shard_map/ppermute | solution.py:340
  94.2 3.7 %collective-permute-start.28 = (f32[4,512]{1,0:T(4,128)S(1)}, f32[4,512]{1,0:T(4,128)S(1)}, u32[]{:S(2)}, u32[]{:S(2)}) collective-permute-start(f32[4,512]{1,0:T(4,128)S(1)} %add_add_fusion.refs_0_), channel_id=1, source_target_pairs={{0,12},{4,0},{8,4},{12,8},{16,28},{20,16},{24,20},{28,24},{32,44},... | collective-permute-start | bytes 24584 | tf_op jit(solution)/shard_map/ppermute | solution.py:340
  96.4 5.1 %collective-permute-start.19 = (f32[128,256]{1,0:T(8,128)S(1)}, f32[128,256]{1,0:T(8,128)S(1)}, u32[]{:S(2)}, u32[]{:S(2)}) collective-permute-start(f32[128,256]{1,0:T(8,128)S(1)} %get-tuple-element.80), channel_id=1, source_target_pairs={{0,2},{1,3},{2,0},{3,1},{4,6},{5,7},{6,4},{7,5},{8,10},{9,11},{10,... | collective-permute-start | bytes 393224 | tf_op jit(solution)/shard_map/ppermute | solution.py:434

commit v4 on v3

--- a/solution.py
+++ b/solution.py
@@ -11,6 +11,7 @@
 GROUP = 4
 HALF = 256
 NEG = -1e30
+HEADS_AT_ONCE = 4
 LOG2E = 1.4426950408889634
 
 NT = (((1,), (1,)), ((), ()))
@@ -34,13 +35,12 @@
 
 def scores_kernel(scale, at_ref, mix_ref, v_ref, km_ref, c_ref, qm_ref, ko_ref, qo_ref,
                   vp0_ref, vp1_ref, vp2_ref, vp3_ref, kpm_ref, kpo_ref,
-                  stats_ref, grad_ref, w_ref, k_all_ref, q_all_ref, k_all, q_all, v_all):
-    head = pl.program_id(0)
+                  stats_ref, grad_ref, w_ref, k_all, q_all, v_all):
     span = q_all.shape[0]
     tile = span // 2
     half = km_ref.shape[1]
 
-    @pl.when(head == 0)
+    @pl.when(pl.program_id(0) == 0)
     def _():
         k_all[:span, :half] = kpm_ref[...]
         k_all[:span, half:] = kpo_ref[...]
@@ -48,22 +48,20 @@
         k_all[span:, half:] = ko_ref[...]
         q_all[:, :half] = qm_ref[...]
         q_all[:, half:] = qo_ref[...]
-        k_all_ref[...] = k_all[...]
-        q_all_ref[...] = q_all[...]
 
     for e, ref in enumerate((vp0_ref, vp1_ref, vp2_ref, vp3_ref)):
         v_all[rows_from(at_ref, e), :] = ref[...]
     v_all[span:, :] = v_ref[...]
-    mix = mix_ref[0]
     is_first = at_ref[2] == 0
     row = lax.broadcasted_iota(jnp.int32, (tile, tile), 0)
     col = lax.broadcasted_iota(jnp.int32, (tile, tile), 1)
-    for t in (0, 1):
+    for t, j in [(t, j) for t in (0, 1) for j in range(mix_ref.shape[0])]:
         lo = t * tile
-        mq = (q_all[lo:lo + tile, :].astype(jnp.float32) * mix).astype(jnp.bfloat16)
-        up = c_ref[lo:lo + tile, :]
+        cols = slice(j * 128, (j + 1) * 128)
+        mq = (q_all[lo:lo + tile, :].astype(jnp.float32) * mix_ref[j]).astype(jnp.bfloat16)
+        up = c_ref[lo:lo + tile, cols]
         s = dot(k_all[lo:lo + 3 * tile, :], mq, NT) * (scale * LOG2E)
-        d = dot(v_all[lo:lo + 3 * tile, :], up, NT)
+        d = dot(v_all[lo:lo + 3 * tile, cols], up, NT)
         s0 = jnp.where((row > col) & jnp.logical_not(is_first), s[:tile], NEG)
         s1 = s[tile:2 * tile]
         if t == 0:
@@ -75,67 +73,71 @@
         inv = 1.0 / total
         ds = [d[:tile], d[tile:2 * tile], d[2 * tile:]]
         delta = jnp.sum(p[0] * ds[0] + p[1] * ds[1] + p[2] * ds[2], 0, keepdims=True) * inv
-        stats_ref[0, 0:1, lo:lo + tile] = top + jnp.log2(total)
-        stats_ref[0, 1:2, lo:lo + tile] = delta
+        stats_ref[j, 0:1, lo:lo + tile] = top + jnp.log2(total)
+        stats_ref[j, 1:2, lo:lo + tile] = delta
         for i in range(3):
             w = p[i] * inv
-            grad_ref[0, t, i * tile:(i + 1) * tile, :] = (w * (ds[i] - delta)).astype(jnp.bfloat16)
+            grad_ref[j, t, i * tile:(i + 1) * tile, :] = (w * (ds[i] - delta)).astype(jnp.bfloat16)
             if i == 2:
-                w_ref[0, 2 * t, :, :] = w.astype(jnp.bfloat16)
+                w_ref[j, 2 * t, :, :] = w.astype(jnp.bfloat16)
             if i == 1 and t == 1:
-                w_ref[0, 1, :, :] = w.astype(jnp.bfloat16)
+                w_ref[j, 1, :, :] = w.astype(jnp.bfloat16)
 
 
 def query_kernel(scale, at_ref, mix_ref, k_ref, q_ref, grad_ref, dqm_ref, dqo_ref, dmix_ref, dq_acc):
-    head = pl.program_id(0)
     span, width = q_ref.shape
     tile = span // 2
-
-    @pl.when(head == 0)
+    many = mix_ref.shape[0]
+
+    @pl.when(pl.program_id(0) == 0)
     def _():
         dq_acc[...] = jnp.zeros_like(dq_acc)
 
-    mix = mix_ref[0]
-    dmix = jnp.zeros((1, width), jnp.float32)
+    dmix = [jnp.zeros((1, width), jnp.float32) for _ in range(many)]
     for t in (0, 1):
         lo = t * tile
-        qg = dot(grad_ref[0, t], k_ref[lo:lo + 3 * tile, :], TN) * scale
-        dq_acc[lo:lo + tile, :] += qg * mix
-        dmix = dmix + jnp.sum(qg * q_ref[lo:lo + tile, :].astype(jnp.float32), 0, keepdims=True)
-    for m, block in enumerate(blocks_of(at_ref)):
-        dmix_ref[0, :, pl.ds(pl.multiple_of(block * 128, 128), 128)] = dmix[:, m * 128:(m + 1) * 128]
-
-    @pl.when(head == pl.num_programs(0) - 1)
+        q_f32 = q_ref[lo:lo + tile, :].astype(jnp.float32)
+        dq = 0.0
+        for j in range(many):
+            qg = dot(grad_ref[j, t], k_ref[lo:lo + 3 * tile, :], TN) * scale
+            dq = dq + qg * mix_ref[j]
+            dmix[j] = dmix[j] + jnp.sum(qg * q_f32, 0, keepdims=True)
+        dq_acc[lo:lo + tile, :] += dq
+    for j in range(many):
+        for m, block in enumerate(blocks_of(at_ref)):
+            dst = pl.ds(pl.multiple_of(block * 128, 128), 128)
+            dmix_ref[j, :, dst] = dmix[j][:, m * 128:(m + 1) * 128]
+
+    @pl.when(pl.program_id(0) == pl.num_programs(0) - 1)
     def _():
         dqm_ref[...] = dq_acc[:, :width // 2]
         dqo_ref[...] = dq_acc[:, width // 2:].astype(jnp.bfloat16)
 
 
 def key_kernel(mix_ref, c_ref, q_ref, grad_ref, w_ref, dk_ref, dv_ref):
-    head = pl.program_id(0)
     span = q_ref.shape[0]
     tile = span // 2
 
-    @pl.when(head == 0)
+    @pl.when(pl.program_id(0) == 0)
     def _():
         dk_ref[...] = jnp.zeros_like(dk_ref)
 
-    mix = mix_ref[0]
-    mq = (q_ref[...].astype(jnp.float32) * mix).astype(jnp.bfloat16)
-    dk_ref[...] += dot(grad_ref[0, 1, tile:, :], mq[tile:], NN)
-    dk_ref[:tile, :] += dot(grad_ref[0, 0, 2 * tile:, :], mq[:tile], NN)
-    dv_ref[tile:, :] = dot(w_ref[0, 2], c_ref[tile:, :], NN)
-    dv_ref[:tile, :] = dot(w_ref[0, 1], c_ref[tile:, :], NN) + dot(w_ref[0, 0], c_ref[:tile, :], NN)
+    for j in range(mix_ref.shape[0]):
+        cols = slice(j * 128, (j + 1) * 128)
+        mq = (q_ref[...].astype(jnp.float32) * mix_ref[j]).astype(jnp.bfloat16)
+        dk_ref[...] += dot(grad_ref[j, 1, tile:, :], mq[tile:], NN)
+        dk_ref[:tile, :] += dot(grad_ref[j, 0, 2 * tile:, :], mq[:tile], NN)
+        dv_ref[tile:, cols] = dot(w_ref[j, 2], c_ref[tile:, cols], NN)
+        dv_ref[:tile, cols] = dot(w_ref[j, 1], c_ref[tile:, cols], NN) + dot(w_ref[j, 0], c_ref[:tile, cols], NN)
 
 
 def next_kernel(scale, at_ref, mix_ref, v_ref, km_ref, ko_ref, cn_ref, qnm_ref, qno_ref, stats_ref,
                 dk_ref, dv_ref, dkm_ref, dko_ref, dvo_ref, k_all, q_all, dk_acc):
-    head = pl.program_id(0)
     span = q_all.shape[0]
     tile = span // 2
     half = km_ref.shape[1]
 
-    @pl.when(head == 0)
+    @pl.when(pl.program_id(0) == 0)
     def _():
         k_all[:, :half] = km_ref[...]
         k_all[:, half:] = ko_ref[...]
@@ -143,34 +145,35 @@
         q_all[:, half:] = qno_ref[...]
         dk_acc[...] = dk_ref[...]
 
-    mix = mix_ref[0]
     row = lax.broadcasted_iota(jnp.int32, (tile, tile), 0)
     col = lax.broadcasted_iota(jnp.int32, (tile, tile), 1)
     is_last = at_ref[4] == 1
     seen = (row > col) & jnp.logical_not(is_last)
-    dv = [dv_ref[:tile, :], dv_ref[tile:, :]]
-    for t in (0, 1):
-        lo = t * tile
-        mq = (q_all[lo:lo + tile, :].astype(jnp.float32) * mix).astype(jnp.bfloat16)
-        up = cn_ref[lo:lo + tile, :]
-        lse = stats_ref[0, 0:1, lo:lo + tile]
-        delta = stats_ref[0, 1:2, lo:lo + tile]
-        s = dot(k_all[lo:, :], mq, NT) * (scale * LOG2E)
-        d = dot(v_ref[lo:, :], up, NT)
-        w = jnp.exp2(jnp.where(seen, s[:tile] - lse, NEG))
-        if t == 0:
-            w = jnp.concatenate([w, jnp.exp2(jnp.where(is_last, NEG, s[tile:] - lse))], 0)
-        grad = (w * (d - delta)).astype(jnp.bfloat16)
-        add = dot(w.astype(jnp.bfloat16), up, NN)
-        if t == 0:
-            dv = [dv[0] + add[:tile], dv[1] + add[tile:]]
-        else:
-            dv[1] = dv[1] + add
-        dk_acc[lo:, :] += dot(grad, mq, NN)
-    dvo_ref[:tile, :] = dv[0].astype(jnp.bfloat16)
-    dvo_ref[tile:, :] = dv[1].astype(jnp.bfloat16)
-
-    @pl.when(head == pl.num_programs(0) - 1)
+    for j in range(mix_ref.shape[0]):
+        cols = slice(j * 128, (j + 1) * 128)
+        dv = [dv_ref[:tile, cols], dv_ref[tile:, cols]]
+        for t in (0, 1):
+            lo = t * tile
+            mq = (q_all[lo:lo + tile, :].astype(jnp.float32) * mix_ref[j]).astype(jnp.bfloat16)
+            up = cn_ref[lo:lo + tile, cols]
+            lse = stats_ref[j, 0:1, lo:lo + tile]
+            delta = stats_ref[j, 1:2, lo:lo + tile]
+            s = dot(k_all[lo:, :], mq, NT) * (scale * LOG2E)
+            d = dot(v_ref[lo:, cols], up, NT)
+            w = jnp.exp2(jnp.where(seen, s[:tile] - lse, NEG))
+            if t == 0:
+                w = jnp.concatenate([w, jnp.exp2(jnp.where(is_last, NEG, s[tile:] - lse))], 0)
+            grad = (w * (d - delta)).astype(jnp.bfloat16)
+            add = dot(w.astype(jnp.bfloat16), up, NN)
+            if t == 0:
+                dv = [dv[0] + add[:tile], dv[1] + add[tile:]]
+            else:
+                dv[1] = dv[1] + add
+            dk_acc[lo:, :] += dot(grad, mq, NN)
+        dvo_ref[:tile, cols] = dv[0].astype(jnp.bfloat16)
+        dvo_ref[tile:, cols] = dv[1].astype(jnp.bfloat16)
+
+    @pl.when(pl.program_id(0) == pl.num_programs(0) - 1)
     def _():
         dkm_ref[...] = dk_acc[:, :half] * scale
         dko_ref[...] = (dk_acc[:, half:] * scale).astype(jnp.bfloat16)
@@ -216,13 +219,13 @@
         hop[:, cols:] = k_ref[...]
 
 
-def gather_kernel(at_ref, p0_ref, p1_ref, p2_ref, p3_ref, vk_ref, q_ref, c_ref, kq_ref):
+def gather_kernel(at_ref, p0_ref, p1_ref, p2_ref, p3_ref, vk_ref, cq_ref, kq_ref):
     half = vk_ref.shape[1]
     for e, ref in enumerate((p0_ref, p1_ref, p2_ref, p3_ref)):
         rows = rows_from(at_ref, e)
         vk_ref[rows, :] = ref[:, :half]
-        q_ref[rows, :] = ref[:, half:half + HALF]
-        c_ref[rows, :] = ref[:, half + HALF:]
+        cq_ref[rows, :half - HALF] = ref[:, half + HALF:]
+        cq_ref[rows, half - HALF:] = ref[:, half:half + HALF]
         kq_ref[rows, :] = ref[:, half - HALF:half + HALF]
 
 
@@ -311,12 +314,12 @@
     return pl.BlockSpec(shape, lambda h: at or (0,) * len(shape))
 
 
-def by_head(rows, base=0):
-    return pl.BlockSpec((rows, 128), lambda h: (0, base + h))
+def by_head(rows):
+    return pl.BlockSpec((rows, 128 * HEADS_AT_ONCE), lambda h: (0, h))
 
 
 def head_first(*shape):
-    return pl.BlockSpec((1,) + shape, lambda h: (h,) + (0,) * len(shape))
+    return pl.BlockSpec((HEADS_AT_ONCE,) + shape, lambda h: (h,) + (0,) * len(shape))
 
 
 def per_device(q_shared, k_shared, mixing, values, cotangent):
@@ -358,11 +361,11 @@
     before = call(split_kernel, (1,), [SMEM, whole(ahead_v), whole(ahead)],
                   [(fixed((tok, wide)), (tok, wide), B16)] * GROUP, [], (at, ahead_v, ahead), 1)
     before = turns(before)
-    vk, q_half, c_own, kq = call(
+    vk, cq, kq = call(
         gather_kernel, (1,), [SMEM] + [whole(own[0])] * GROUP,
-        [(fixed((span, wide)), (span, wide), B16), (fixed((span, HALF)), (span, HALF), B16),
-         (fixed((span, n_v)), (span, n_v), B16), (fixed((span, 2 * HALF)), (span, 2 * HALF), B16)], [], (at, *own), 1)
-    q_next, c_next = to_group(q_half, -1), to_group(c_own, -1)
+        [(fixed((span, wide)), (span, wide), B16)] * 2
+        + [(fixed((span, 2 * HALF)), (span, 2 * HALF), B16)], [], (at, *own), 1)
+    cq_next = to_group(cq, -1)
     kq_other = core_swap(kq)
     kp, mix = call(
         collect_kernel, (1,),
@@ -373,23 +376,20 @@
     kp_other = core_swap(kp)
 
     stats, grad, w, k_all, q_all = call(
-        functools.partial(scores_kernel, scale), (heads,),
+        functools.partial(scores_kernel, scale), (heads // HEADS_AT_ONCE,),
         [SMEM, head_first(1, width), by_head(span), fixed((span, HALF), 0, 2), by_head(span),
-         fixed((span, HALF)), fixed((span, HALF), 0, 0), fixed((span, HALF), 0, 1)]
+         fixed((span, HALF), 0, n_v // HALF), fixed((span, HALF), 0, 0), fixed((span, HALF), 0, 1)]
         + [by_head(tok)] * GROUP + [fixed((span, HALF))] * 2,
         [(head_first(2, span), (heads, 2, span), F32),
          (head_first(2, 768, 256), (heads, 2, 768, 256), B16),
          (head_first(3, 256, 256), (heads, 3, 256, 256), B16),
          (fixed((2 * span, width)), (2 * span, width), B16),
          (fixed((span, width)), (span, width), B16)],
-        [pltpu.VMEM((2 * span, width), B16), pltpu.VMEM((span, width), B16),
-         pltpu.VMEM((2 * span, 128), B16)],
-        (at, mix, vk, vk, c_own, q_half, kq_other, kq_other, *before, kp, kp_other), 1)
+        [pltpu.VMEM((2 * span, 128 * HEADS_AT_ONCE), B16)],
+        (at, mix, vk, vk, cq, cq, kq_other, kq_other, *before, kp, kp_other), 2.5)
     next_stats = to_group(stats, -1)
-    q_next, stats = lax.optimization_barrier((q_next, stats))
-    q_next_other = core_swap(q_next)
     dq_mine, dq_other, dmix = call(
-        functools.partial(query_kernel, scale), (heads,),
+        functools.partial(query_kernel, scale), (heads // HEADS_AT_ONCE,),
         [SMEM, head_first(1, width), fixed((2 * span, width)), fixed((span, width)),
          head_first(2, 768, 256)],
         [(fixed((span, HALF)), (span, HALF), F32), (fixed((span, HALF)), (span, HALF), B16),
@@ -404,21 +404,23 @@
         return (x + from_peer(x, a)) + (from_peer(x, b) + from_peer(x, a ^ b))
 
     dk, dv = call(
-        key_kernel, (heads,),
+        key_kernel, (heads // HEADS_AT_ONCE,),
         [head_first(1, width), by_head(span), fixed((span, width)),
          head_first(2, 768, 256), head_first(3, 256, 256)],
         [(fixed((span, width)), (span, width), F32), (by_head(span), (span, n_v), F32)],
-        [], (mix, c_own, q_all, grad, w), 0.3)
+        [], (mix, cq, q_all, grad, w), 0.3)
+    cq_next, next_stats, dk, dq_mine = lax.optimization_barrier((cq_next, next_stats, dk, dq_mine))
+    q_next_other = core_swap(cq_next[:, n_v:])
     dk_mine, dk_other, dv = call(
-        functools.partial(next_kernel, scale), (heads,),
+        functools.partial(next_kernel, scale), (heads // HEADS_AT_ONCE,),
         [SMEM, head_first(1, width), by_head(span), fixed((span, HALF), 0, 2),
-         fixed((span, HALF), 0, 0), by_head(span), fixed((span, HALF)),
+         fixed((span, HALF), 0, 0), by_head(span), fixed((span, HALF), 0, n_v // HALF),
          fixed((span, HALF)), head_first(2, span), fixed((span, width)), by_head(span)],
         [(fixed((span, HALF)), (span, HALF), F32), (fixed((span, HALF)), (span, HALF), B16),
          (by_head(span), (span, n_v), B16)],
         [pltpu.VMEM((span, width), B16), pltpu.VMEM((span, width), B16),
          pltpu.VMEM((span, width), F32)],
-        (at, mix, vk, vk, kq_other, c_next, q_next, q_next_other, next_stats, dk, dv), 6)
+        (at, mix, vk, vk, kq_other, cq_next, cq_next, q_next_other, next_stats, dk, dv), 6)
     dk_other, dq_other, dmix = lax.optimization_barrier((dk_other, dq_other, dmix))
     dmix = exchange(dmix.reshape(heads, width), GROUP, 2 * GROUP)
 

time: 102 us -> 96.2 us (0.943)
  Pallas kernels: 27.5 us -> 23.1 us
  waiting for transfers between devices: 19.9 us -> 17.3 us
    ppermute x12, waiting for transfers between devices: 8.77 us -> 3.38 us  [turn(): return lax.ppermute(x, 'seq', pairs)]
    pallas_call x13, Pallas kernels: 27.5 us -> 23.1 us  [call(): pl.pallas_call(body, grid=grid, in_specs=ins, out_specs=[spec for spec, _...]
    ppermute x5, waiting for transfers between devices: 0.01 us -> 3.04 us  [core_swap(): return lax.ppermute(x, 'head', [(0, 1), (1, 0), (2, 3), (3, 2)])]
    ppermute x5 -> x4, starting transfers between devices: 16.8 us -> 16.1 us  [to_group(): return lax.ppermute(x, 'seq', pairs)]
    ppermute x5 -> x4, waiting for transfers between devices: 6.49 us -> 6.55 us  [to_group(): return lax.ppermute(x, 'seq', pairs)]
  transfers between devices with their start and end apart: 29 -> 28, of which waited for: 8 -> 9; matrix products, arithmetic and copies ran while one was open for 1% -> 1% of each run, Pallas kernels for 21% -> 19%
where the time goes in v4:
time: 96.2 us; the launch traced here: 96.1 us
  starting transfers between devices  54.2 us (56%)
  Pallas kernels  23.1 us (24%)
  waiting for transfers between devices  17.3 us (18%)
    pallas_call x13, Pallas kernels, call(): pl.pallas_call(body, grid=grid, in_specs=ins, out_specs=[spec for spec, _...  23.1 us
    ppermute x12, starting transfers between devices, turn(): return lax.ppermute(x, 'seq', pairs)  21.9 us
    ppermute x4, starting transfers between devices, to_group(): return lax.ppermute(x, 'seq', pairs)  16.1 us
    ppermute x6, starting transfers between devices, from_peer(): return lax.ppermute(x, 'seq', [(i, i ^ by) for i in range(peers)])  14.1 us
    ppermute x4, waiting for transfers between devices, to_group(): return lax.ppermute(x, 'seq', pairs)  6.55 us
    ppermute x6, waiting for transfers between devices, from_peer(): return lax.ppermute(x, 'seq', [(i, i ^ by) for i in range(peers)])  3.59 us
    ppermute x12, waiting for transfers between devices, turn(): return lax.ppermute(x, 'seq', pairs)  3.38 us
    ppermute x5, waiting for transfers between devices, core_swap(): return lax.ppermute(x, 'head', [(0, 1), (1, 0), (2, 3), (3, 2)])  3.04 us
  transfers between devices with their start and end apart: 28, of which 9 were waited for; matrix products, arithmetic and copies ran while one was open for 1% of the time, Pallas kernels for 19%

profile of v4, /device:TPU:8, one launch (start us, length us, event | category | flops | bytes accessed | tf_op | source)
XLA Modules:
  0.0 96.1 jit_solution(8252373763530075264)
XLA Ops:
  0.6 2.4 %collective-permute-start = (bf16[128,2048]{1,0:T(8,128)(2,1)}, bf16[128,2048]{1,0:T(8,128)(2,1)S(1)}, u32[]{:S(2)}, u32[]{:S(2)}) collective-permute-start(bf16[128,2048]{1,0:T(8,128)(2,1)} %v_ref.1), channel_id=1, source_target_pairs={{0,16},{4,20},{8,24},{12,28},{16,32},{20,36},{24,40},{28,44},{32,4... | collective-permute-start | bytes 1572872 | tf_op jit(solution)/shard_map/ppermute | solution.py:339
  3.0 0.6 stack.27.at_ref
  3.6 3.3 %shard_map.84 = (bf16[128,1536]{1,0:T(8,128)(2,1)}, bf16[128,1536]{1,0:T(8,128)(2,1)}, bf16[128,1536]{1,0:T(8,128)(2,1)}, bf16[128,1536]{1,0:T(8,128)(2,1)}, bf16[128,256]{1,0:T(8,128)(2,1)}) custom-call(s32[5]{0:T(128)} %stack.27.at_ref, bf16[128,2048]{1,0:T(8,128)(2,1)} %v_ref.1, bf16[128,2048]{1,0:T(8,128)(2,1)} %c_ref.1, bf16[128,512]{1,0:T(8,128)(2,1)} %k_ref.1, ...), custom_call_target="tpu_custom_call" | custom-call | flops 3000000000 | bytes 1000000 | tf_op jit(solution)/shard_map/pallas_call | solution.py:300
  7.0 1.6 %collective-permute-start.5 = (bf16[128,1536]{1,0:T(8,128)(2,1)}, bf16[128,1536]{1,0:T(8,128)(2,1)S(1)}, u32[]{:S(2)}, u32[]{:S(2)}) collective-permute-start(bf16[128,1536]{1,0:T(8,128)(2,1)} %get-tuple-element.53), channel_id=1, source_target_pairs={{0,4},{4,8},{8,12},{12,0},{16,20},{20,24},{24,28},{28,16},{32,36},... | collective-permute-start | bytes 1179656 | tf_op jit(solution)/shard_map/ppermute | solution.py:343
  8.5 2.7 %collective-permute-start.6 = (bf16[128,1536]{1,0:T(8,128)(2,1)}, bf16[128,1536]{1,0:T(8,128)(2,1)S(1)}, u32[]{:S(2)}, u32[]{:S(2)}) collective-permute-start(bf16[128,1536]{1,0:T(8,128)(2,1)} %get-tuple-element.54), channel_id=1, source_target_pairs={{0,8},{4,12},{8,0},{12,4},{16,24},{20,28},{24,16},{28,20},{32,40},... | collective-permute-start | bytes 1179656 | tf_op jit(solution)/shard_map/ppermute | solution.py:343
  11.3 1.4 %collective-permute-start.7 = (bf16[128,1536]{1,0:T(8,128)(2,1)}, bf16[128,1536]{1,0:T(8,128)(2,1)S(1)}, u32[]{:S(2)}, u32[]{:S(2)}) collective-permute-start(bf16[128,1536]{1,0:T(8,128)(2,1)} %get-tuple-element.55), channel_id=1, source_target_pairs={{0,12},{4,0},{8,4},{12,8},{16,28},{20,16},{24,20},{28,24},{32,44},... | collective-permute-start | bytes 1179656 | tf_op jit(solution)/shard_map/ppermute | solution.py:343
  12.7 2.6 %collective-permute-start.1 = (bf16[128,256]{1,0:T(8,128)(2,1)}, bf16[128,256]{1,0:T(8,128)(2,1)S(1)}, u32[]{:S(2)}, u32[]{:S(2)}) collective-permute-start(bf16[128,256]{1,0:T(8,128)(2,1)} %get-tuple-element.46), channel_id=1, source_target_pairs={{0,16},{4,20},{8,24},{12,28},{16,32},{20,36},{24,40},{28,44},{32,4... | collective-permute-start | bytes 196616 | tf_op jit(solution)/shard_map/ppermute | solution.py:339
  15.3 6.5 %collective-permute-done.1.k_ref = bf16[128,256]{1,0:T(8,128)(2,1)S(1)} collective-permute-done((bf16[128,256]{1,0:T(8,128)(2,1)}, bf16[128,256]{1,0:T(8,128)(2,1)S(1)}, u32[]{:S(2)}, u32[]{:S(2)}) %collective-permute-start.1) | collective-permute-done | bytes 65568 | tf_op jit(solution)/shard_map/ppermute | solution.py:339
  21.8 0.6 shard_map.85
  22.4 1.6 %collective-permute-start.2 = (bf16[128,768]{1,0:T(8,128)(2,1)S(1)}, bf16[128,768]{1,0:T(8,128)(2,1)S(1)}, u32[]{:S(2)}, u32[]{:S(2)}) collective-permute-start(bf16[128,768]{1,0:T(8,128)(2,1)S(1)} %get-tuple-element.48), channel_id=1, source_target_pairs={{0,4},{4,8},{8,12},{12,0},{16,20},{20,24},{24,28},{28,16},{32,36},... | collective-permute-start | bytes 589832 | tf_op jit(solution)/shard_map/ppermute | solution.py:343
  24.0 2.7 %collective-permute-start.3 = (bf16[128,768]{1,0:T(8,128)(2,1)S(1)}, bf16[128,768]{1,0:T(8,128)(2,1)S(1)}, u32[]{:S(2)}, u32[]{:S(2)}) collective-permute-start(bf16[128,768]{1,0:T(8,128)(2,1)S(1)} %get-tuple-element.49), channel_id=1, source_target_pairs={{0,8},{4,12},{8,0},{12,4},{16,24},{20,28},{24,16},{28,20},{32,40},... | collective-permute-start | bytes 589832 | tf_op jit(solution)/shard_map/ppermute | solution.py:343
  26.7 1.4 %collective-permute-start.4 = (bf16[128,768]{1,0:T(8,128)(2,1)S(1)}, bf16[128,768]{1,0:T(8,128)(2,1)S(1)}, u32[]{:S(2)}, u32[]{:S(2)}) collective-permute-start(bf16[128,768]{1,0:T(8,128)(2,1)S(1)} %get-tuple-element.50), channel_id=1, source_target_pairs={{0,12},{4,0},{8,4},{12,8},{16,28},{20,16},{24,20},{28,24},{32,44},... | collective-permute-start | bytes 589832 | tf_op jit(solution)/shard_map/ppermute | solution.py:343
  28.2 1.7 %collective-permute-done.6.p2_ref = bf16[128,1536]{1,0:T(8,128)(2,1)S(1)} collective-permute-done((bf16[128,1536]{1,0:T(8,128)(2,1)}, bf16[128,1536]{1,0:T(8,128)(2,1)S(1)}, u32[]{:S(2)}, u32[]{:S(2)}) %collective-permute-start.6) | collective-permute-done | bytes 393248 | tf_op jit(solution)/shard_map/ppermute | solution.py:343
  29.9 0.7 shard_map.87
  30.7 5.4 %collective-permute-start.9 = (bf16[512,768]{1,0:T(8,128)(2,1)S(1)}, bf16[512,768]{1,0:T(8,128)(2,1)S(1)}, u32[]{:S(2)}, u32[]{:S(2)}) collective-permute-start(bf16[512,768]{1,0:T(8,128)(2,1)S(1)} %get-tuple-element.58.c_ref.qm_ref), channel_id=1, source_target_pairs={{0,240},{4,244},{8,248},{12,252},{16,0},{20,4},{24,8},{28,12},{32,... | collective-permute-start | bytes 2359304 | tf_op jit(solution)/shard_map/ppermute | solution.py:339
  36.1 0.8 collective-permute-done.3.k2_ref.vp2_ref
  36.9 0.6 shard_map.86
  37.8 1.5 %collective-permute-done.10.kpo_ref = bf16[512,256]{1,0:T(8,128)(2,1)S(1)} collective-permute-done((bf16[512,256]{1,0:T(8,128)(2,1)S(1)}, bf16[512,256]{1,0:T(8,128)(2,1)S(1)}, u32[]{:S(2)}, u32[]{:S(2)}) %collective-permute-start.10) | collective-permute-done | bytes 262176 | tf_op jit(solution)/shard_map/ppermute | solution.py:349
  39.3 5.5 %shard_map.88 = (f32[4,2,512]{2,1,0:T(2,128)S(1)}, bf16[4,2,768,256]{3,2,1,0:T(8,128)(2,1)S(1)}, bf16[4,3,256,256]{3,2,1,0:T(8,128)(2,1)S(1)}, bf16[1024,512]{1,0:T(8,128)(2,1)S(1)}, bf16[512,512]{1,0:T(8,128)(2,1)S(1)}) custom-call(s32[5]{0:T(128)S(1)} %copy-done, f32[4,1,512]{2,1,0:T(1,128)S(1)} %get-tuple-element.51.mix_ref, ...), custom_call_target="tpu_custom_call" | custom-call | flops 2500000000 | bytes 1000000 | tf_op jit(solution)/shard_map/pallas_call | solution.py:300
  44.8 5.7 %collective-permute-start.11 = (f32[4,2,512]{2,1,0:T(2,128)S(1)}, f32[4,2,512]{2,1,0:T(2,128)S(1)}, u32[]{:S(2)}, u32[]{:S(2)}) collective-permute-start(f32[4,2,512]{2,1,0:T(2,128)S(1)} %get-tuple-element.60), channel_id=1, source_target_pairs={{0,240},{4,244},{8,248},{12,252},{16,0},{20,4},{24,8},{28,12},{32,... | collective-permute-start | bytes 49160 | tf_op jit(solution)/shard_map/ppermute | solution.py:339
  50.5 2.7 %shard_map.90 = (f32[512,256]{1,0:T(8,128)S(1)}, bf16[512,256]{1,0:T(8,128)(2,1)S(1)}, f32[4,1,512]{2,1,0:T(1,128)S(1)}) custom-call(s32[5]{0:T(128)S(1)} %copy-done, f32[4,1,512]{2,1,0:T(1,128)S(1)} %get-tuple-element.51.mix_ref, bf16[1024,512]{1,0:T(8,128)(2,1)S(1)} %get-tuple-element.65.k_ref, bf16[512,512]{1,0:T(8,128)(2,1)S(1)} %get-tuple-element.61.q_ref, ...), custom_call_target="tpu_custom_call" | custom-call | flops 300000000 | bytes 1000000 | tf_op jit(solution)/shard_map/pallas_call | solution.py:300
  53.2 1.4 %shard_map.89 = (f32[512,512]{1,0:T(8,128)S(1)}, f32[512,512]{1,0:T(8,128)S(1)}) custom-call(f32[4,1,512]{2,1,0:T(1,128)S(1)} %get-tuple-element.51.mix_ref, bf16[512,768]{1,0:T(8,128)(2,1)S(1)} %get-tuple-element.58.c_ref.qm_ref, bf16[512,512]{1,0:T(8,128)(2,1)S(1)} %get-tuple-element.61.q_ref, bf16[4,2,768,256]{3,2,1,0:T(8,128)(2,1)S(1)} %get-tuple-element.62.grad_ref, ...), custom_call_target="tpu_custom_call" | custom-call | flops 300000000 | bytes 1000000 | tf_op jit(solution)/shard_map/pallas_call | solution.py:300
  54.7 0.3 collective-permute-start.12
  55.0 1.5 %collective-permute-done.12.qno_ref = bf16[512,256]{1,0:T(8,128)(2,1)S(1)} collective-permute-done((bf16[512,256]{1,0:T(8,128)(2,1)S(1)}, bf16[512,256]{1,0:T(8,128)(2,1)S(1)}, u32[]{:S(2)}, u32[]{:S(2)}) %collective-permute-start.12) | collective-permute-done | bytes 262176 | tf_op jit(solution)/shard_map/ppermute | solution.py:349
  56.5 3.8 %shard_map.91 = (f32[512,256]{1,0:T(8,128)S(1)}, bf16[512,256]{1,0:T(8,128)(2,1)S(1)}, bf16[512,512]{1,0:T(8,128)(2,1)S(1)}) custom-call(s32[5]{0:T(128)S(1)} %copy-done, f32[4,1,512]{2,1,0:T(1,128)S(1)} %get-tuple-element.51.mix_ref, bf16[512,768]{1,0:T(8,128)(2,1)S(1)} %get-tuple-element.56.v_ref.km_ref, ...), custom_call_target="tpu_custom_call" | custom-call | flops 6000000000 | bytes 1000000 | tf_op jit(solution)/shard_map/pallas_call | solution.py:300
  60.5 0.4 collective-permute-start.14
  60.9 1.4 %collective-permute-start.19 = (f32[4,512]{1,0:T(4,128)S(1)}, f32[4,512]{1,0:T(4,128)S(1)}, u32[]{:S(2)}, u32[]{:S(2)}) collective-permute-start(f32[4,512]{1,0:T(4,128)S(1)} %bitcast.10), channel_id=1, source_target_pairs={{0,16},{4,20},{8,24},{12,28},{16,0},{20,4},{24,8},{28,12},{32,48},... | collective-permute-start | bytes 24584 | tf_op jit(solution)/shard_map/ppermute | solution.py:401
  62.4 1.9 %collective-permute-start.20 = (f32[4,512]{1,0:T(4,128)S(1)}, f32[4,512]{1,0:T(4,128)S(1)}, u32[]{:S(2)}, u32[]{:S(2)}) collective-permute-start(f32[4,512]{1,0:T(4,128)S(1)} %bitcast.11), channel_id=1, source_target_pairs={{0,32},{4,36},{8,40},{12,44},{16,48},{20,52},{24,56},{28,60},{32,0... | collective-permute-start | bytes 24584 | tf_op jit(solution)/shard_map/ppermute | solution.py:401
  64.3 1.7 %collective-permute-start.21 = (f32[4,512]{1,0:T(4,128)S(1)}, f32[4,512]{1,0:T(4,128)S(1)}, u32[]{:S(2)}, u32[]{:S(2)}) collective-permute-start(f32[4,512]{1,0:T(4,128)S(1)} %bitcast.12), channel_id=1, source_target_pairs={{0,48},{4,52},{8,56},{12,60},{16,32},{20,36},{24,40},{28,44},{32,1... | collective-permute-start | bytes 24584 | tf_op jit(solution)/shard_map/ppermute | solution.py:401
  65.9 0.7 shard_map.92
  66.6 3.1 %collective-permute-start.15 = (bf16[128,1024]{1,0:T(8,128)(2,1)S(1)}, bf16[128,1024]{1,0:T(8,128)(2,1)S(1)}, u32[]{:S(2)}, u32[]{:S(2)}) collective-permute-start(bf16[128,1024]{1,0:T(8,128)(2,1)S(1)} %get-tuple-element.80), channel_id=1, source_target_pairs={{0,4},{4,8},{8,12},{12,0},{16,20},{20,24},{24,28},{28,16},{32,36},... | collective-permute-start | bytes 786440 | tf_op jit(solution)/shard_map/ppermute | solution.py:343
  69.8 0.6 collective-permute-start.16
  70.4 2.1 %collective-permute-start.17 = (bf16[128,1024]{1,0:T(8,128)(2,1)S(1)}, bf16[128,1024]{1,0:T(8,128)(2,1)S(1)}, u32[]{:S(2)}, u32[]{:S(2)}) collective-permute-start(bf16[128,1024]{1,0:T(8,128)(2,1)S(1)} %get-tuple-element.82), channel_id=1, source_target_pairs={{0,12},{4,0},{8,4},{12,8},{16,28},{20,16},{24,20},{28,24},{32,44},... | collective-permute-start | bytes 786440 | tf_op jit(solution)/shard_map/ppermute | solution.py:343
  72.5 4.3 %collective-permute-start.22 = (f32[4,512]{1,0:T(4,128)S(1)}, f32[4,512]{1,0:T(4,128)S(1)}, u32[]{:S(2)}, u32[]{:S(2)}) collective-permute-start(f32[4,512]{1,0:T(4,128)S(1)} %add_add_fusion.1), channel_id=1, source_target_pairs={{0,64},{4,68},{8,72},{12,76},{16,80},{20,84},{24,88},{28,92},{32,9... | collective-permute-start | bytes 24584 | tf_op jit(solution)/shard_map/ppermute | solution.py:401
  76.9 2.5 %collective-permute-start.23 = (f32[4,512]{1,0:T(4,128)S(1)}, f32[4,512]{1,0:T(4,128)S(1)}, u32[]{:S(2)}, u32[]{:S(2)}) collective-permute-start(f32[4,512]{1,0:T(4,128)S(1)} %add_add_fusion.1), channel_id=1, source_target_pairs={{0,128},{4,132},{8,136},{12,140},{16,144},{20,148},{24,152},{28,15... | collective-permute-start | bytes 24584 | tf_op jit(solution)/shard_map/ppermute | solution.py:401
  79.4 2.2 %collective-permute-start.24 = (f32[4,512]{1,0:T(4,128)S(1)}, f32[4,512]{1,0:T(4,128)S(1)}, u32[]{:S(2)}, u32[]{:S(2)}) collective-permute-start(f32[4,512]{1,0:T(4,128)S(1)} %add_add_fusion.1), channel_id=1, source_target_pairs={{0,192},{4,196},{8,200},{12,204},{16,208},{20,212},{24,216},{28,22... | collective-permute-start | bytes 24584 | tf_op jit(solution)/shard_map/ppermute | solution.py:401
  81.6 2.8 %collective-permute-done.23 = f32[4,512]{1,0:T(4,128)S(1)} collective-permute-done((f32[4,512]{1,0:T(4,128)S(1)}, f32[4,512]{1,0:T(4,128)S(1)}, u32[]{:S(2)}, u32[]{:S(2)}) %collective-permute-start.23) | collective-permute-done | bytes 8224 | tf_op jit(solution)/shard_map/ppermute | solution.py:401
  84.5 0.8 collective-permute-done.24
  85.2 1.8 %collective-permute-start.25 = (f32[4,512]{1,0:T(4,128)S(1)}, f32[4,512]{1,0:T(4,128)S(1)}, u32[]{:S(2)}, u32[]{:S(2)}) collective-permute-start(f32[4,512]{1,0:T(4,128)S(1)} %add_add_fusion.refs_0_), channel_id=1, source_target_pairs={{0,4},{4,8},{8,12},{12,0},{16,20},{20,24},{24,28},{28,16},{32,36},... | collective-permute-start | bytes 24584 | tf_op jit(solution)/shard_map/ppermute | solution.py:343
  87.0 1.0 %collective-permute-start.26 = (f32[4,512]{1,0:T(4,128)S(1)}, f32[4,512]{1,0:T(4,128)S(1)}, u32[]{:S(2)}, u32[]{:S(2)}) collective-permute-start(f32[4,512]{1,0:T(4,128)S(1)} %add_add_fusion.refs_0_), channel_id=1, source_target_pairs={{0,8},{4,12},{8,0},{12,4},{16,24},{20,28},{24,16},{28,20},{32,40},... | collective-permute-start | bytes 24584 | tf_op jit(solution)/shard_map/ppermute | solution.py:343
  88.1 1.7 %collective-permute-start.27 = (f32[4,512]{1,0:T(4,128)S(1)}, f32[4,512]{1,0:T(4,128)S(1)}, u32[]{:S(2)}, u32[]{:S(2)}) collective-permute-start(f32[4,512]{1,0:T(4,128)S(1)} %add_add_fusion.refs_0_), channel_id=1, source_target_pairs={{0,12},{4,0},{8,4},{12,8},{16,28},{20,16},{24,20},{28,24},{32,44},... | collective-permute-start | bytes 24584 | tf_op jit(solution)/shard_map/ppermute | solution.py:343
  89.8 0.6 shard_map.93
  90.4 0.9 collective-permute-start.18
  91.3 0.9 collective-permute-done.26.refs_2_
  92.2 1.2 %shard_map.96 = f32[16,512]{1,0:T(8,128)} custom-call(s32[5]{0:T(128)S(1)} %copy-done, f32[4,512]{1,0:T(4,128)S(1)} %add_add_fusion.refs_0_, f32[4,512]{1,0:T(4,128)S(1)} %collective-permute-done.25.refs_1_, f32[4,512]{1,0:T(4,128)S(1)} %collective-permute-done.26.refs_2_, f32[4,512]{1,0:T(4,128)S(1)} %collective-permute-done.27.refs_3_), custom_call_target="tpu_custom_call" | custom-call | flops 1000000000 | bytes 1000000 | tf_op jit(solution)/shard_map/pallas_call | solution.py:300
  93.4 1.4 %shard_map.95 = bf16[128,2048]{1,0:T(8,128)(2,1)} custom-call(s32[5]{0:T(128)S(1)} %copy-done, bf16[128,1024]{1,0:T(8,128)(2,1)S(1)} %get-tuple-element.79.refs_0_, bf16[128,1024]{1,0:T(8,128)(2,1)S(1)} %collective-permute-done.15.refs_1_, bf16[128,1024]{1,0:T(8,128)(2,1)S(1)} %collective-permute-done.16.refs_2_, ...), custom_call_target="tpu_custom_call" | custom-call | flops 1000000000 | bytes 1000000 | tf_op jit(solution)/shard_map/pallas_call | solution.py:300
  94.7 0.7 collective-permute-done.18.got_ref
  95.5 0.6 shard_map.94
  (32 shorter events, 0.7 us)
Async XLA Ops:
  0.6 21.2 %collective-permute-start = (bf16[128,2048]{1,0:T(8,128)(2,1)}, bf16[128,2048]{1,0:T(8,128)(2,1)S(1)}, u32[]{:S(2)}, u32[]{:S(2)}) collective-permute-start(bf16[128,2048]{1,0:T(8,128)(2,1)} %v_ref.1), channel_id=1, source_target_pairs={{0,16},{4,20},{8,24},{12,28},{16,32},{20,36},{24,40},{28,44},{32,4... | collective-permute-start | bytes 1572872 | tf_op jit(solution)/shard_map/ppermute | solution.py:339
  3.6 18.2 %copy-start = (s32[5]{0:T(128)S(1)}, s32[5]{0:T(128)}, u32[]{:S(2)}) copy-start(s32[5]{0:T(128)} %stack.27.at_ref) | copy-start | bytes 64
  7.0 23.0 %copy-start.2 = (bf16[128,1536]{1,0:T(8,128)(2,1)S(1)}, bf16[128,1536]{1,0:T(8,128)(2,1)}, u32[]{:S(2)}) copy-start(bf16[128,1536]{1,0:T(8,128)(2,1)} %get-tuple-element.52.p0_ref) | copy-start | bytes 1179652
  7.0 19.8 %collective-permute-start.5 = (bf16[128,1536]{1,0:T(8,128)(2,1)}, bf16[128,1536]{1,0:T(8,128)(2,1)S(1)}, u32[]{:S(2)}, u32[]{:S(2)}) collective-permute-start(bf16[128,1536]{1,0:T(8,128)(2,1)} %get-tuple-element.53), channel_id=1, source_target_pairs={{0,4},{4,8},{8,12},{12,0},{16,20},{20,24},{24,28},{28,16},{32,36},... | collective-permute-start | bytes 1179656 | tf_op jit(solution)/shard_map/ppermute | solution.py:343
  8.5 21.4 %collective-permute-start.6 = (bf16[128,1536]{1,0:T(8,128)(2,1)}, bf16[128,1536]{1,0:T(8,128)(2,1)S(1)}, u32[]{:S(2)}, u32[]{:S(2)}) collective-permute-start(bf16[128,1536]{1,0:T(8,128)(2,1)} %get-tuple-element.54), channel_id=1, source_target_pairs={{0,8},{4,12},{8,0},{12,4},{16,24},{20,28},{24,16},{28,20},{32,40},... | collective-permute-start | bytes 1179656 | tf_op jit(solution)/shard_map/ppermute | solution.py:343
  11.3 18.7 %collective-permute-start.7 = (bf16[128,1536]{1,0:T(8,128)(2,1)}, bf16[128,1536]{1,0:T(8,128)(2,1)S(1)}, u32[]{:S(2)}, u32[]{:S(2)}) collective-permute-start(bf16[128,1536]{1,0:T(8,128)(2,1)} %get-tuple-element.55), channel_id=1, source_target_pairs={{0,12},{4,0},{8,4},{12,8},{16,28},{20,16},{24,20},{28,24},{32,44},... | collective-permute-start | bytes 1179656 | tf_op jit(solution)/shard_map/ppermute | solution.py:343
  12.7 24.2 %copy-start.1 = (f32[16,512]{1,0:T(8,128)S(1)}, f32[16,512]{1,0:T(8,128)}, u32[]{:S(2)}) copy-start(f32[16,512]{1,0:T(8,128)} %mixing_ref.1) | copy-start | bytes 98308
  12.7 9.1 %collective-permute-start.1 = (bf16[128,256]{1,0:T(8,128)(2,1)}, bf16[128,256]{1,0:T(8,128)(2,1)S(1)}, u32[]{:S(2)}, u32[]{:S(2)}) collective-permute-start(bf16[128,256]{1,0:T(8,128)(2,1)} %get-tuple-element.46), channel_id=1, source_target_pairs={{0,16},{4,20},{8,24},{12,28},{16,32},{20,36},{24,40},{28,44},{32,4... | collective-permute-start | bytes 196616 | tf_op jit(solution)/shard_map/ppermute | solution.py:339
  22.4 13.7 %collective-permute-start.2 = (bf16[128,768]{1,0:T(8,128)(2,1)S(1)}, bf16[128,768]{1,0:T(8,128)(2,1)S(1)}, u32[]{:S(2)}, u32[]{:S(2)}) collective-permute-start(bf16[128,768]{1,0:T(8,128)(2,1)S(1)} %get-tuple-element.48), channel_id=1, source_target_pairs={{0,4},{4,8},{8,12},{12,0},{16,20},{20,24},{24,28},{28,16},{32,36},... | collective-permute-start | bytes 589832 | tf_op jit(solution)/shard_map/ppermute | solution.py:343
  24.0 12.9 %collective-permute-start.3 = (bf16[128,768]{1,0:T(8,128)(2,1)S(1)}, bf16[128,768]{1,0:T(8,128)(2,1)S(1)}, u32[]{:S(2)}, u32[]{:S(2)}) collective-permute-start(bf16[128,768]{1,0:T(8,128)(2,1)S(1)} %get-tuple-element.49), channel_id=1, source_target_pairs={{0,8},{4,12},{8,0},{12,4},{16,24},{20,28},{24,16},{28,20},{32,40},... | collective-permute-start | bytes 589832 | tf_op jit(solution)/shard_map/ppermute | solution.py:343
  26.7 10.1 %collective-permute-start.4 = (bf16[128,768]{1,0:T(8,128)(2,1)S(1)}, bf16[128,768]{1,0:T(8,128)(2,1)S(1)}, u32[]{:S(2)}, u32[]{:S(2)}) collective-permute-start(bf16[128,768]{1,0:T(8,128)(2,1)S(1)} %get-tuple-element.50), channel_id=1, source_target_pairs={{0,12},{4,0},{8,4},{12,8},{16,28},{20,16},{24,20},{28,24},{32,44},... | collective-permute-start | bytes 589832 | tf_op jit(solution)/shard_map/ppermute | solution.py:343
  30.6 7.1 %collective-permute-start.8 = (bf16[512,512]{1,0:T(8,128)(2,1)S(1)}, bf16[512,512]{1,0:T(8,128)(2,1)S(1)}, u32[]{:S(2)}, u32[]{:S(2)}) collective-permute-start(bf16[512,512]{1,0:T(8,128)(2,1)S(1)} %get-tuple-element.57), channel_id=1, source_target_pairs={{0,1},{1,0},{2,3},{3,2},{4,5},{5,4},{6,7},{7,6},{8,9},{9,8},{10,11... | collective-permute-start | bytes 1572872 | tf_op jit(solution)/shard_map/ppermute | solution.py:349
  30.7 23.9 %collective-permute-start.9 = (bf16[512,768]{1,0:T(8,128)(2,1)S(1)}, bf16[512,768]{1,0:T(8,128)(2,1)S(1)}, u32[]{:S(2)}, u32[]{:S(2)}) collective-permute-start(bf16[512,768]{1,0:T(8,128)(2,1)S(1)} %get-tuple-element.58.c_ref.qm_ref), channel_id=1, source_target_pairs={{0,240},{4,244},{8,248},{12,252},{16,0},{20,4},{24,8},{28,12},{32,... | collective-permute-start | bytes 2359304 | tf_op jit(solution)/shard_map/ppermute | solution.py:339
  37.5 1.8 %collective-permute-start.10 = (bf16[512,256]{1,0:T(8,128)(2,1)S(1)}, bf16[512,256]{1,0:T(8,128)(2,1)S(1)}, u32[]{:S(2)}, u32[]{:S(2)}) collective-permute-start(bf16[512,256]{1,0:T(8,128)(2,1)S(1)} %get-tuple-element.59.kpm_ref), channel_id=1, source_target_pairs={{0,1},{1,0},{2,3},{3,2},{4,5},{5,4},{6,7},{7,6},{8,9},{9,8},{10,11... | collective-permute-start | bytes 786440 | tf_op jit(solution)/shard_map/ppermute | solution.py:349
  44.8 9.8 %collective-permute-start.11 = (f32[4,2,512]{2,1,0:T(2,128)S(1)}, f32[4,2,512]{2,1,0:T(2,128)S(1)}, u32[]{:S(2)}, u32[]{:S(2)}) collective-permute-start(f32[4,2,512]{2,1,0:T(2,128)S(1)} %get-tuple-element.60), channel_id=1, source_target_pairs={{0,240},{4,244},{8,248},{12,252},{16,0},{20,4},{24,8},{28,12},{32,... | collective-permute-start | bytes 49160 | tf_op jit(solution)/shard_map/ppermute | solution.py:339
  54.7 1.8 %collective-permute-start.12 = (bf16[512,256]{1,0:T(8,128)(2,1)S(1)}, bf16[512,256]{1,0:T(8,128)(2,1)S(1)}, u32[]{:S(2)}, u32[]{:S(2)}) collective-permute-start(bf16[512,256]{1,0:T(8,128)(2,1)S(1)} %slice.3), channel_id=1, source_target_pairs={{0,1},{1,0},{2,3},{3,2},{4,5},{5,4},{6,7},{7,6},{8,9},{9,8},{10,11... | collective-permute-start | bytes 786440 | tf_op jit(solution)/shard_map/ppermute | solution.py:349
  60.3 5.6 %collective-permute-start.13 = (bf16[512,256]{1,0:T(8,128)(2,1)S(1)}, bf16[512,256]{1,0:T(8,128)(2,1)S(1)}, u32[]{:S(2)}, u32[]{:S(2)}) collective-permute-start(bf16[512,256]{1,0:T(8,128)(2,1)S(1)} %get-tuple-element.76), channel_id=1, source_target_pairs={{0,1},{1,0},{2,3},{3,2},{4,5},{5,4},{6,7},{7,6},{8,9},{9,8},{10,11... | collective-permute-start | bytes 786440 | tf_op jit(solution)/shard_map/ppermute | solution.py:349
  60.5 5.4 %collective-permute-start.14 = (bf16[512,256]{1,0:T(8,128)(2,1)S(1)}, bf16[512,256]{1,0:T(8,128)(2,1)S(1)}, u32[]{:S(2)}, u32[]{:S(2)}) collective-permute-start(bf16[512,256]{1,0:T(8,128)(2,1)S(1)} %get-tuple-element.78), channel_id=1, source_target_pairs={{0,1},{1,0},{2,3},{3,2},{4,5},{5,4},{6,7},{7,6},{8,9},{9,8},{10,11... | collective-permute-start | bytes 786440 | tf_op jit(solution)/shard_map/ppermute | solution.py:349
  60.9 9.5 %collective-permute-start.19 = (f32[4,512]{1,0:T(4,128)S(1)}, f32[4,512]{1,0:T(4,128)S(1)}, u32[]{:S(2)}, u32[]{:S(2)}) collective-permute-start(f32[4,512]{1,0:T(4,128)S(1)} %bitcast.10), channel_id=1, source_target_pairs={{0,16},{4,20},{8,24},{12,28},{16,0},{20,4},{24,8},{28,12},{32,48},... | collective-permute-start | bytes 24584 | tf_op jit(solution)/shard_map/ppermute | solution.py:401
  62.4 10.2 %collective-permute-start.20 = (f32[4,512]{1,0:T(4,128)S(1)}, f32[4,512]{1,0:T(4,128)S(1)}, u32[]{:S(2)}, u32[]{:S(2)}) collective-permute-start(f32[4,512]{1,0:T(4,128)S(1)} %bitcast.11), channel_id=1, source_target_pairs={{0,32},{4,36},{8,40},{12,44},{16,48},{20,52},{24,56},{28,60},{32,0... | collective-permute-start | bytes 24584 | tf_op jit(solution)/shard_map/ppermute | solution.py:401
  64.3 8.3 %collective-permute-start.21 = (f32[4,512]{1,0:T(4,128)S(1)}, f32[4,512]{1,0:T(4,128)S(1)}, u32[]{:S(2)}, u32[]{:S(2)}) collective-permute-start(f32[4,512]{1,0:T(4,128)S(1)} %bitcast.12), channel_id=1, source_target_pairs={{0,48},{4,52},{8,56},{12,60},{16,32},{20,36},{24,40},{28,44},{32,1... | collective-permute-start | bytes 24584 | tf_op jit(solution)/shard_map/ppermute | solution.py:401
  66.6 21.4 %collective-permute-start.15 = (bf16[128,1024]{1,0:T(8,128)(2,1)S(1)}, bf16[128,1024]{1,0:T(8,128)(2,1)S(1)}, u32[]{:S(2)}, u32[]{:S(2)}) collective-permute-start(bf16[128,1024]{1,0:T(8,128)(2,1)S(1)} %get-tuple-element.80), channel_id=1, source_target_pairs={{0,4},{4,8},{8,12},{12,0},{16,20},{20,24},{24,28},{28,16},{32,36},... | collective-permute-start | bytes 786440 | tf_op jit(solution)/shard_map/ppermute | solution.py:343
  69.8 20.0 %collective-permute-start.16 = (bf16[128,1024]{1,0:T(8,128)(2,1)S(1)}, bf16[128,1024]{1,0:T(8,128)(2,1)S(1)}, u32[]{:S(2)}, u32[]{:S(2)}) collective-permute-start(bf16[128,1024]{1,0:T(8,128)(2,1)S(1)} %get-tuple-element.81), channel_id=1, source_target_pairs={{0,8},{4,12},{8,0},{12,4},{16,24},{20,28},{24,16},{28,20},{32,40},... | collective-permute-start | bytes 786440 | tf_op jit(solution)/shard_map/ppermute | solution.py:343
  70.4 19.4 %collective-permute-start.17 = (bf16[128,1024]{1,0:T(8,128)(2,1)S(1)}, bf16[128,1024]{1,0:T(8,128)(2,1)S(1)}, u32[]{:S(2)}, u32[]{:S(2)}) collective-permute-start(bf16[128,1024]{1,0:T(8,128)(2,1)S(1)} %get-tuple-element.82), channel_id=1, source_target_pairs={{0,12},{4,0},{8,4},{12,8},{16,28},{20,16},{24,20},{28,24},{32,44},... | collective-permute-start | bytes 786440 | tf_op jit(solution)/shard_map/ppermute | solution.py:343
  72.5 6.9 %collective-permute-start.22 = (f32[4,512]{1,0:T(4,128)S(1)}, f32[4,512]{1,0:T(4,128)S(1)}, u32[]{:S(2)}, u32[]{:S(2)}) collective-permute-start(f32[4,512]{1,0:T(4,128)S(1)} %add_add_fusion.1), channel_id=1, source_target_pairs={{0,64},{4,68},{8,72},{12,76},{16,80},{20,84},{24,88},{28,92},{32,9... | collective-permute-start | bytes 24584 | tf_op jit(solution)/shard_map/ppermute | solution.py:401
  76.9 7.6 %collective-permute-start.23 = (f32[4,512]{1,0:T(4,128)S(1)}, f32[4,512]{1,0:T(4,128)S(1)}, u32[]{:S(2)}, u32[]{:S(2)}) collective-permute-start(f32[4,512]{1,0:T(4,128)S(1)} %add_add_fusion.1), channel_id=1, source_target_pairs={{0,128},{4,132},{8,136},{12,140},{16,144},{20,148},{24,152},{28,15... | collective-permute-start | bytes 24584 | tf_op jit(solution)/shard_map/ppermute | solution.py:401
  79.4 5.8 %collective-permute-start.24 = (f32[4,512]{1,0:T(4,128)S(1)}, f32[4,512]{1,0:T(4,128)S(1)}, u32[]{:S(2)}, u32[]{:S(2)}) collective-permute-start(f32[4,512]{1,0:T(4,128)S(1)} %add_add_fusion.1), channel_id=1, source_target_pairs={{0,192},{4,196},{8,200},{12,204},{16,208},{20,212},{24,216},{28,22... | collective-permute-start | bytes 24584 | tf_op jit(solution)/shard_map/ppermute | solution.py:401
  85.2 6.1 %collective-permute-start.25 = (f32[4,512]{1,0:T(4,128)S(1)}, f32[4,512]{1,0:T(4,128)S(1)}, u32[]{:S(2)}, u32[]{:S(2)}) collective-permute-start(f32[4,512]{1,0:T(4,128)S(1)} %add_add_fusion.refs_0_), channel_id=1, source_target_pairs={{0,4},{4,8},{8,12},{12,0},{16,20},{20,24},{24,28},{28,16},{32,36},... | collective-permute-start | bytes 24584 | tf_op jit(solution)/shard_map/ppermute | solution.py:343
  87.0 5.2 %collective-permute-start.26 = (f32[4,512]{1,0:T(4,128)S(1)}, f32[4,512]{1,0:T(4,128)S(1)}, u32[]{:S(2)}, u32[]{:S(2)}) collective-permute-start(f32[4,512]{1,0:T(4,128)S(1)} %add_add_fusion.refs_0_), channel_id=1, source_target_pairs={{0,8},{4,12},{8,0},{12,4},{16,24},{20,28},{24,16},{28,20},{32,40},... | collective-permute-start | bytes 24584 | tf_op jit(solution)/shard_map/ppermute | solution.py:343
  88.1 4.1 %collective-permute-start.27 = (f32[4,512]{1,0:T(4,128)S(1)}, f32[4,512]{1,0:T(4,128)S(1)}, u32[]{:S(2)}, u32[]{:S(2)}) collective-permute-start(f32[4,512]{1,0:T(4,128)S(1)} %add_add_fusion.refs_0_), channel_id=1, source_target_pairs={{0,12},{4,0},{8,4},{12,8},{16,28},{20,16},{24,20},{28,24},{32,44},... | collective-permute-start | bytes 24584 | tf_op jit(solution)/shard_map/ppermute | solution.py:343
  90.4 5.1 %collective-permute-start.18 = (f32[128,256]{1,0:T(8,128)S(1)}, f32[128,256]{1,0:T(8,128)S(1)}, u32[]{:S(2)}, u32[]{:S(2)}) collective-permute-start(f32[128,256]{1,0:T(8,128)S(1)} %get-tuple-element.84), channel_id=1, source_target_pairs={{0,2},{1,3},{2,0},{3,1},{4,6},{5,7},{6,4},{7,5},{8,10},{9,11},{10,... | collective-permute-start | bytes 393224 | tf_op jit(solution)/shard_map/ppermute | solution.py:436

commit v5 on v4

--- a/solution.py
+++ b/solution.py
@@ -179,9 +179,9 @@
         dko_ref[...] = (dk_acc[:, half:] * scale).astype(jnp.bfloat16)
 
 
-def load_kernel(at_ref, v_ref, c_ref, k_ref, q_ref, own0_ref, own1_ref, own2_ref, own3_ref,
+def load_kernel(v_ref, c_ref, k_ref, q_ref, own0_ref, own1_ref, own2_ref, own3_ref,
                 ahead_ref, k_in, q_in, sems):
-    core, place = at_ref[0], at_ref[1]
+    core, place = lax.rem(lax.axis_index("head"), 2), lax.rem(lax.axis_index("seq"), GROUP)
     wide = v_ref.shape[1]
     cols = wide // GROUP
     pending = []
@@ -352,10 +352,10 @@
     wide = n_v + HALF
     ahead_v = to_group(values, 1)
     *own, ahead = call(
-        load_kernel, (), [SMEM] + [ANY] * 4,
+        load_kernel, (), [ANY] * 4,
         [(VMEM, (tok, 2 * wide), B16)] * GROUP + [(VMEM, (tok, HALF), B16)],
         [pltpu.VMEM((tok, width), B16)] * 2 + [pltpu.SemaphoreType.DMA((10,))],
-        (at, values, cotangent, k_shared, q_shared), 3, vmem=56)
+        (values, cotangent, k_shared, q_shared), 3, vmem=56)
     ahead = to_group(ahead, 1)
     own = turns(own)
     before = call(split_kernel, (1,), [SMEM, whole(ahead_v), whole(ahead)],
@@ -421,7 +421,7 @@
         [pltpu.VMEM((span, width), B16), pltpu.VMEM((span, width), B16),
          pltpu.VMEM((span, width), F32)],
         (at, mix, vk, vk, kq_other, cq_next, cq_next, q_next_other, next_stats, dk, dv), 6)
-    dk_other, dq_other, dmix = lax.optimization_barrier((dk_other, dq_other, dmix))
+    dk_other, dmix = lax.optimization_barrier((dk_other, dmix))
     dmix = exchange(dmix.reshape(heads, width), GROUP, 2 * GROUP)
 
     dk_got, dq_got = core_swap(dk_other), core_swap(dq_other)

time: 96.2 us -> 94.3 us (0.980)
  waiting for transfers between devices: 17.3 us -> 16.3 us
    ppermute x12, waiting for transfers between devices: 3.38 us -> 1.65 us  [turn(): return lax.ppermute(x, 'seq', pairs)]
    ppermute x4, waiting for transfers between devices: 6.55 us -> 7.81 us  [to_group(): return lax.ppermute(x, 'seq', pairs)]
  transfers between devices with their start and end apart: 28 -> 28, of which waited for: 9 -> 8; matrix products, arithmetic and copies ran while one was open for 1% -> 0% of each run, Pallas kernels for 19% -> 23%
where the time goes in v5:
time: 94.3 us; the launch traced here: 94.2 us
  starting transfers between devices  54.6 us (58%)
  Pallas kernels  22.4 us (24%)
  waiting for transfers between devices  16.3 us (17%)
    pallas_call x13, Pallas kernels, call(): pl.pallas_call(body, grid=grid, in_specs=ins, out_specs=[spec for spec, _...  22.4 us
    ppermute x12, starting transfers between devices, turn(): return lax.ppermute(x, 'seq', pairs)  22 us
    ppermute x4, starting transfers between devices, to_group(): return lax.ppermute(x, 'seq', pairs)  16.5 us
    ppermute x6, starting transfers between devices, from_peer(): return lax.ppermute(x, 'seq', [(i, i ^ by) for i in range(peers)])  14.1 us
    ppermute x4, waiting for transfers between devices, to_group(): return lax.ppermute(x, 'seq', pairs)  7.81 us
    ppermute x6, waiting for transfers between devices, from_peer(): return lax.ppermute(x, 'seq', [(i, i ^ by) for i in range(peers)])  3.59 us
    ppermute x5, waiting for transfers between devices, core_swap(): return lax.ppermute(x, 'head', [(0, 1), (1, 0), (2, 3), (3, 2)])  2.54 us
  transfers between devices with their start and end apart: 28, of which 8 were waited for; matrix products, arithmetic and copies ran while one was open for 0% of the time, Pallas kernels for 23%

profile of v5, /device:TPU:8, one launch (start us, length us, event | category | flops | bytes accessed | tf_op | source)
XLA Modules:
  0.0 94.2 jit_solution(9045610027328722167)
XLA Ops:
  0.6 2.4 %collective-permute-start = (bf16[128,2048]{1,0:T(8,128)(2,1)}, bf16[128,2048]{1,0:T(8,128)(2,1)S(1)}, u32[]{:S(2)}, u32[]{:S(2)}) collective-permute-start(bf16[128,2048]{1,0:T(8,128)(2,1)} %v_ref.1), channel_id=1, source_target_pairs={{0,16},{4,20},{8,24},{12,28},{16,32},{20,36},{24,40},{28,44},{32,4... | collective-permute-start | bytes 1572872 | tf_op jit(solution)/shard_map/ppermute | solution.py:339
  3.0 2.6 %shard_map.84 = (bf16[128,1536]{1,0:T(8,128)(2,1)}, bf16[128,1536]{1,0:T(8,128)(2,1)}, bf16[128,1536]{1,0:T(8,128)(2,1)}, bf16[128,1536]{1,0:T(8,128)(2,1)}, bf16[128,256]{1,0:T(8,128)(2,1)}) custom-call(bf16[128,2048]{1,0:T(8,128)(2,1)} %v_ref.1, bf16[128,2048]{1,0:T(8,128)(2,1)} %c_ref.1, bf16[128,512]{1,0:T(8,128)(2,1)} %k_ref.1, bf16[128,512]{1,0:T(8,128)(2,1)} %q_ref.1), custom_call_target="tpu_custom_call" | custom-call | flops 3000000000 | bytes 1000000 | tf_op jit(solution)/shard_map/pallas_call | solution.py:300
  5.6 1.6 %collective-permute-start.5 = (bf16[128,1536]{1,0:T(8,128)(2,1)}, bf16[128,1536]{1,0:T(8,128)(2,1)S(1)}, u32[]{:S(2)}, u32[]{:S(2)}) collective-permute-start(bf16[128,1536]{1,0:T(8,128)(2,1)} %get-tuple-element.52), channel_id=1, source_target_pairs={{0,4},{4,8},{8,12},{12,0},{16,20},{20,24},{24,28},{28,16},{32,36},... | collective-permute-start | bytes 1179656 | tf_op jit(solution)/shard_map/ppermute | solution.py:343
  7.2 2.7 %collective-permute-start.6 = (bf16[128,1536]{1,0:T(8,128)(2,1)}, bf16[128,1536]{1,0:T(8,128)(2,1)S(1)}, u32[]{:S(2)}, u32[]{:S(2)}) collective-permute-start(bf16[128,1536]{1,0:T(8,128)(2,1)} %get-tuple-element.53), channel_id=1, source_target_pairs={{0,8},{4,12},{8,0},{12,4},{16,24},{20,28},{24,16},{28,20},{32,40},... | collective-permute-start | bytes 1179656 | tf_op jit(solution)/shard_map/ppermute | solution.py:343
  9.9 1.4 %collective-permute-start.7 = (bf16[128,1536]{1,0:T(8,128)(2,1)}, bf16[128,1536]{1,0:T(8,128)(2,1)S(1)}, u32[]{:S(2)}, u32[]{:S(2)}) collective-permute-start(bf16[128,1536]{1,0:T(8,128)(2,1)} %get-tuple-element.54), channel_id=1, source_target_pairs={{0,12},{4,0},{8,4},{12,8},{16,28},{20,16},{24,20},{28,24},{32,44},... | collective-permute-start | bytes 1179656 | tf_op jit(solution)/shard_map/ppermute | solution.py:343
  11.4 2.6 %collective-permute-start.1 = (bf16[128,256]{1,0:T(8,128)(2,1)}, bf16[128,256]{1,0:T(8,128)(2,1)S(1)}, u32[]{:S(2)}, u32[]{:S(2)}) collective-permute-start(bf16[128,256]{1,0:T(8,128)(2,1)} %get-tuple-element.45), channel_id=1, source_target_pairs={{0,16},{4,20},{8,24},{12,28},{16,32},{20,36},{24,40},{28,44},{32,4... | collective-permute-start | bytes 196616 | tf_op jit(solution)/shard_map/ppermute | solution.py:339
  14.0 7.8 %collective-permute-done.1.k_ref = bf16[128,256]{1,0:T(8,128)(2,1)S(1)} collective-permute-done((bf16[128,256]{1,0:T(8,128)(2,1)}, bf16[128,256]{1,0:T(8,128)(2,1)S(1)}, u32[]{:S(2)}, u32[]{:S(2)}) %collective-permute-start.1) | collective-permute-done | bytes 65568 | tf_op jit(solution)/shard_map/ppermute | solution.py:339
  21.8 0.6 shard_map.85
  22.4 1.6 %collective-permute-start.2 = (bf16[128,768]{1,0:T(8,128)(2,1)S(1)}, bf16[128,768]{1,0:T(8,128)(2,1)S(1)}, u32[]{:S(2)}, u32[]{:S(2)}) collective-permute-start(bf16[128,768]{1,0:T(8,128)(2,1)S(1)} %get-tuple-element.47), channel_id=1, source_target_pairs={{0,4},{4,8},{8,12},{12,0},{16,20},{20,24},{24,28},{28,16},{32,36},... | collective-permute-start | bytes 589832 | tf_op jit(solution)/shard_map/ppermute | solution.py:343
  24.0 2.7 %collective-permute-start.3 = (bf16[128,768]{1,0:T(8,128)(2,1)S(1)}, bf16[128,768]{1,0:T(8,128)(2,1)S(1)}, u32[]{:S(2)}, u32[]{:S(2)}) collective-permute-start(bf16[128,768]{1,0:T(8,128)(2,1)S(1)} %get-tuple-element.48), channel_id=1, source_target_pairs={{0,8},{4,12},{8,0},{12,4},{16,24},{20,28},{24,16},{28,20},{32,40},... | collective-permute-start | bytes 589832 | tf_op jit(solution)/shard_map/ppermute | solution.py:343
  26.7 1.4 %collective-permute-start.4 = (bf16[128,768]{1,0:T(8,128)(2,1)S(1)}, bf16[128,768]{1,0:T(8,128)(2,1)S(1)}, u32[]{:S(2)}, u32[]{:S(2)}) collective-permute-start(bf16[128,768]{1,0:T(8,128)(2,1)S(1)} %get-tuple-element.49), channel_id=1, source_target_pairs={{0,12},{4,0},{8,4},{12,8},{16,28},{20,16},{24,20},{28,24},{32,44},... | collective-permute-start | bytes 589832 | tf_op jit(solution)/shard_map/ppermute | solution.py:343
  28.2 0.7 shard_map.87
  28.9 0.1 collective-permute-start.8
  29.0 5.8 %collective-permute-start.9 = (bf16[512,768]{1,0:T(8,128)(2,1)S(1)}, bf16[512,768]{1,0:T(8,128)(2,1)S(1)}, u32[]{:S(2)}, u32[]{:S(2)}) collective-permute-start(bf16[512,768]{1,0:T(8,128)(2,1)S(1)} %get-tuple-element.57.c_ref.qm_ref), channel_id=1, source_target_pairs={{0,240},{4,244},{8,248},{12,252},{16,0},{20,4},{24,8},{28,12},{32,... | collective-permute-start | bytes 2359304 | tf_op jit(solution)/shard_map/ppermute | solution.py:339
  34.8 0.8 collective-permute-done.3.k2_ref.vp2_ref
  35.5 0.6 shard_map.86
  36.1 0.3 collective-permute-start.10
  36.4 1.5 %collective-permute-done.10.kpo_ref = bf16[512,256]{1,0:T(8,128)(2,1)S(1)} collective-permute-done((bf16[512,256]{1,0:T(8,128)(2,1)S(1)}, bf16[512,256]{1,0:T(8,128)(2,1)S(1)}, u32[]{:S(2)}, u32[]{:S(2)}) %collective-permute-start.10) | collective-permute-done | bytes 262176 | tf_op jit(solution)/shard_map/ppermute | solution.py:349
  37.9 5.5 %shard_map.88 = (f32[4,2,512]{2,1,0:T(2,128)S(1)}, bf16[4,2,768,256]{3,2,1,0:T(8,128)(2,1)S(1)}, bf16[4,3,256,256]{3,2,1,0:T(8,128)(2,1)S(1)}, bf16[1024,512]{1,0:T(8,128)(2,1)S(1)}, bf16[512,512]{1,0:T(8,128)(2,1)S(1)}) custom-call(s32[5]{0:T(128)S(1)} %stack.27.at_ref, f32[4,1,512]{2,1,0:T(1,128)S(1)} %get-tuple-element.50.mix_ref, ...), custom_call_target="tpu_custom_call" | custom-call | flops 2500000000 | bytes 1000000 | tf_op jit(solution)/shard_map/pallas_call | solution.py:300
  43.5 5.7 %collective-permute-start.11 = (f32[4,2,512]{2,1,0:T(2,128)S(1)}, f32[4,2,512]{2,1,0:T(2,128)S(1)}, u32[]{:S(2)}, u32[]{:S(2)}) collective-permute-start(f32[4,2,512]{2,1,0:T(2,128)S(1)} %get-tuple-element.59), channel_id=1, source_target_pairs={{0,240},{4,244},{8,248},{12,252},{16,0},{20,4},{24,8},{28,12},{32,... | collective-permute-start | bytes 49160 | tf_op jit(solution)/shard_map/ppermute | solution.py:339
  49.2 2.7 %shard_map.90 = (f32[512,256]{1,0:T(8,128)S(1)}, bf16[512,256]{1,0:T(8,128)(2,1)S(1)}, f32[4,1,512]{2,1,0:T(1,128)S(1)}) custom-call(s32[5]{0:T(128)S(1)} %stack.27.at_ref, f32[4,1,512]{2,1,0:T(1,128)S(1)} %get-tuple-element.50.mix_ref, bf16[1024,512]{1,0:T(8,128)(2,1)S(1)} %get-tuple-element.64.k_ref, bf16[512,512]{1,0:T(8,128)(2,1)S(1)} %get-tuple-element.60.q_ref, ...), custom_call_target="tpu_custom_call" | custom-call | flops 300000000 | bytes 1000000 | tf_op jit(solution)/shard_map/pallas_call | solution.py:300
  51.9 1.4 %shard_map.89 = (f32[512,512]{1,0:T(8,128)S(1)}, f32[512,512]{1,0:T(8,128)S(1)}) custom-call(f32[4,1,512]{2,1,0:T(1,128)S(1)} %get-tuple-element.50.mix_ref, bf16[512,768]{1,0:T(8,128)(2,1)S(1)} %get-tuple-element.57.c_ref.qm_ref, bf16[512,512]{1,0:T(8,128)(2,1)S(1)} %get-tuple-element.60.q_ref, bf16[4,2,768,256]{3,2,1,0:T(8,128)(2,1)S(1)} %get-tuple-element.61.grad_ref, ...), custom_call_target="tpu_custom_call" | custom-call | flops 300000000 | bytes 1000000 | tf_op jit(solution)/shard_map/pallas_call | solution.py:300
  53.4 0.5 collective-permute-start.14
  53.9 1.0 %collective-permute-done.12.qno_ref = bf16[512,256]{1,0:T(8,128)(2,1)S(1)} collective-permute-done((bf16[512,256]{1,0:T(8,128)(2,1)S(1)}, bf16[512,256]{1,0:T(8,128)(2,1)S(1)}, u32[]{:S(2)}, u32[]{:S(2)}) %collective-permute-start.12) | collective-permute-done | bytes 262176 | tf_op jit(solution)/shard_map/ppermute | solution.py:349
  55.0 3.8 %shard_map.91 = (f32[512,256]{1,0:T(8,128)S(1)}, bf16[512,256]{1,0:T(8,128)(2,1)S(1)}, bf16[512,512]{1,0:T(8,128)(2,1)S(1)}) custom-call(s32[5]{0:T(128)S(1)} %stack.27.at_ref, f32[4,1,512]{2,1,0:T(1,128)S(1)} %get-tuple-element.50.mix_ref, bf16[512,768]{1,0:T(8,128)(2,1)S(1)} %get-tuple-element.55.v_ref.km_ref, ...), custom_call_target="tpu_custom_call" | custom-call | flops 6000000000 | bytes 1000000 | tf_op jit(solution)/shard_map/pallas_call | solution.py:300
  58.8 0.2 collective-permute-start.13
  59.0 1.4 %collective-permute-start.19 = (f32[4,512]{1,0:T(4,128)S(1)}, f32[4,512]{1,0:T(4,128)S(1)}, u32[]{:S(2)}, u32[]{:S(2)}) collective-permute-start(f32[4,512]{1,0:T(4,128)S(1)} %bitcast.10), channel_id=1, source_target_pairs={{0,16},{4,20},{8,24},{12,28},{16,0},{20,4},{24,8},{28,12},{32,48},... | collective-permute-start | bytes 24584 | tf_op jit(solution)/shard_map/ppermute | solution.py:401
  60.4 1.9 %collective-permute-start.20 = (f32[4,512]{1,0:T(4,128)S(1)}, f32[4,512]{1,0:T(4,128)S(1)}, u32[]{:S(2)}, u32[]{:S(2)}) collective-permute-start(f32[4,512]{1,0:T(4,128)S(1)} %bitcast.11), channel_id=1, source_target_pairs={{0,32},{4,36},{8,40},{12,44},{16,48},{20,52},{24,56},{28,60},{32,0... | collective-permute-start | bytes 24584 | tf_op jit(solution)/shard_map/ppermute | solution.py:401
  62.3 1.7 %collective-permute-start.21 = (f32[4,512]{1,0:T(4,128)S(1)}, f32[4,512]{1,0:T(4,128)S(1)}, u32[]{:S(2)}, u32[]{:S(2)}) collective-permute-start(f32[4,512]{1,0:T(4,128)S(1)} %bitcast.12), channel_id=1, source_target_pairs={{0,48},{4,52},{8,56},{12,60},{16,32},{20,36},{24,40},{28,44},{32,1... | collective-permute-start | bytes 24584 | tf_op jit(solution)/shard_map/ppermute | solution.py:401
  64.0 0.7 shard_map.92
  64.7 3.1 %collective-permute-start.15 = (bf16[128,1024]{1,0:T(8,128)(2,1)S(1)}, bf16[128,1024]{1,0:T(8,128)(2,1)S(1)}, u32[]{:S(2)}, u32[]{:S(2)}) collective-permute-start(bf16[128,1024]{1,0:T(8,128)(2,1)S(1)} %get-tuple-element.78), channel_id=1, source_target_pairs={{0,4},{4,8},{8,12},{12,0},{16,20},{20,24},{24,28},{28,16},{32,36},... | collective-permute-start | bytes 786440 | tf_op jit(solution)/shard_map/ppermute | solution.py:343
  67.8 0.6 collective-permute-start.16
  68.4 2.1 %collective-permute-start.17 = (bf16[128,1024]{1,0:T(8,128)(2,1)S(1)}, bf16[128,1024]{1,0:T(8,128)(2,1)S(1)}, u32[]{:S(2)}, u32[]{:S(2)}) collective-permute-start(bf16[128,1024]{1,0:T(8,128)(2,1)S(1)} %get-tuple-element.80), channel_id=1, source_target_pairs={{0,12},{4,0},{8,4},{12,8},{16,28},{20,16},{24,20},{28,24},{32,44},... | collective-permute-start | bytes 786440 | tf_op jit(solution)/shard_map/ppermute | solution.py:343
  70.6 4.3 %collective-permute-start.22 = (f32[4,512]{1,0:T(4,128)S(1)}, f32[4,512]{1,0:T(4,128)S(1)}, u32[]{:S(2)}, u32[]{:S(2)}) collective-permute-start(f32[4,512]{1,0:T(4,128)S(1)} %add_add_fusion.1), channel_id=1, source_target_pairs={{0,64},{4,68},{8,72},{12,76},{16,80},{20,84},{24,88},{28,92},{32,9... | collective-permute-start | bytes 24584 | tf_op jit(solution)/shard_map/ppermute | solution.py:401
  75.0 2.5 %collective-permute-start.23 = (f32[4,512]{1,0:T(4,128)S(1)}, f32[4,512]{1,0:T(4,128)S(1)}, u32[]{:S(2)}, u32[]{:S(2)}) collective-permute-start(f32[4,512]{1,0:T(4,128)S(1)} %add_add_fusion.1), channel_id=1, source_target_pairs={{0,128},{4,132},{8,136},{12,140},{16,144},{20,148},{24,152},{28,15... | collective-permute-start | bytes 24584 | tf_op jit(solution)/shard_map/ppermute | solution.py:401
  77.5 2.2 %collective-permute-start.24 = (f32[4,512]{1,0:T(4,128)S(1)}, f32[4,512]{1,0:T(4,128)S(1)}, u32[]{:S(2)}, u32[]{:S(2)}) collective-permute-start(f32[4,512]{1,0:T(4,128)S(1)} %add_add_fusion.1), channel_id=1, source_target_pairs={{0,192},{4,196},{8,200},{12,204},{16,208},{20,212},{24,216},{28,22... | collective-permute-start | bytes 24584 | tf_op jit(solution)/shard_map/ppermute | solution.py:401
  79.7 2.8 %collective-permute-done.23 = f32[4,512]{1,0:T(4,128)S(1)} collective-permute-done((f32[4,512]{1,0:T(4,128)S(1)}, f32[4,512]{1,0:T(4,128)S(1)}, u32[]{:S(2)}, u32[]{:S(2)}) %collective-permute-start.23) | collective-permute-done | bytes 8224 | tf_op jit(solution)/shard_map/ppermute | solution.py:401
  82.5 0.8 collective-permute-done.24
  83.3 1.8 %collective-permute-start.25 = (f32[4,512]{1,0:T(4,128)S(1)}, f32[4,512]{1,0:T(4,128)S(1)}, u32[]{:S(2)}, u32[]{:S(2)}) collective-permute-start(f32[4,512]{1,0:T(4,128)S(1)} %add_add_fusion.refs_0_), channel_id=1, source_target_pairs={{0,4},{4,8},{8,12},{12,0},{16,20},{20,24},{24,28},{28,16},{32,36},... | collective-permute-start | bytes 24584 | tf_op jit(solution)/shard_map/ppermute | solution.py:343
  85.1 1.0 %collective-permute-start.26 = (f32[4,512]{1,0:T(4,128)S(1)}, f32[4,512]{1,0:T(4,128)S(1)}, u32[]{:S(2)}, u32[]{:S(2)}) collective-permute-start(f32[4,512]{1,0:T(4,128)S(1)} %add_add_fusion.refs_0_), channel_id=1, source_target_pairs={{0,8},{4,12},{8,0},{12,4},{16,24},{20,28},{24,16},{28,20},{32,40},... | collective-permute-start | bytes 24584 | tf_op jit(solution)/shard_map/ppermute | solution.py:343
  86.1 1.8 %collective-permute-start.27 = (f32[4,512]{1,0:T(4,128)S(1)}, f32[4,512]{1,0:T(4,128)S(1)}, u32[]{:S(2)}, u32[]{:S(2)}) collective-permute-start(f32[4,512]{1,0:T(4,128)S(1)} %add_add_fusion.refs_0_), channel_id=1, source_target_pairs={{0,12},{4,0},{8,4},{12,8},{16,28},{20,16},{24,20},{28,24},{32,44},... | collective-permute-start | bytes 24584 | tf_op jit(solution)/shard_map/ppermute | solution.py:343
  87.9 0.6 shard_map.93
  88.5 0.9 collective-permute-start.18
  89.4 0.9 collective-permute-done.26.refs_2_
  90.3 1.2 %shard_map.96 = f32[16,512]{1,0:T(8,128)} custom-call(s32[5]{0:T(128)S(1)} %stack.27.at_ref, f32[4,512]{1,0:T(4,128)S(1)} %add_add_fusion.refs_0_, f32[4,512]{1,0:T(4,128)S(1)} %collective-permute-done.25.refs_1_, f32[4,512]{1,0:T(4,128)S(1)} %collective-permute-done.26.refs_2_, f32[4,512]{1,0:T(4,128)S(1)} %collective-permute-done.27.refs_3_), custom_call_target="tpu_custom_call" | custom-call | flops 1000000000 | bytes 1000000 | tf_op jit(solution)/shard_map/pallas_call | solution.py:300
  91.4 1.4 %shard_map.95 = bf16[128,2048]{1,0:T(8,128)(2,1)} custom-call(s32[5]{0:T(128)S(1)} %stack.27.at_ref, bf16[128,1024]{1,0:T(8,128)(2,1)S(1)} %get-tuple-element.77.refs_0_, bf16[128,1024]{1,0:T(8,128)(2,1)S(1)} %collective-permute-done.15.refs_1_, bf16[128,1024]{1,0:T(8,128)(2,1)S(1)} %collective-permute-done.16.refs_2_, ...), custom_call_target="tpu_custom_call" | custom-call | flops 1000000000 | bytes 1000000 | tf_op jit(solution)/shard_map/pallas_call | solution.py:300
  92.8 0.7 collective-permute-done.18.got_ref
  93.6 0.6 shard_map.94
  (30 shorter events, 0.3 us)
Async XLA Ops:
  0.6 21.2 %collective-permute-start = (bf16[128,2048]{1,0:T(8,128)(2,1)}, bf16[128,2048]{1,0:T(8,128)(2,1)S(1)}, u32[]{:S(2)}, u32[]{:S(2)}) collective-permute-start(bf16[128,2048]{1,0:T(8,128)(2,1)} %v_ref.1), channel_id=1, source_target_pairs={{0,16},{4,20},{8,24},{12,28},{16,32},{20,36},{24,40},{28,44},{32,4... | collective-permute-start | bytes 1572872 | tf_op jit(solution)/shard_map/ppermute | solution.py:339
  5.6 22.6 %copy-start.1 = (bf16[128,1536]{1,0:T(8,128)(2,1)S(1)}, bf16[128,1536]{1,0:T(8,128)(2,1)}, u32[]{:S(2)}) copy-start(bf16[128,1536]{1,0:T(8,128)(2,1)} %get-tuple-element.51.p0_ref) | copy-start | bytes 1179652
  5.6 21.1 %collective-permute-start.5 = (bf16[128,1536]{1,0:T(8,128)(2,1)}, bf16[128,1536]{1,0:T(8,128)(2,1)S(1)}, u32[]{:S(2)}, u32[]{:S(2)}) collective-permute-start(bf16[128,1536]{1,0:T(8,128)(2,1)} %get-tuple-element.52), channel_id=1, source_target_pairs={{0,4},{4,8},{8,12},{12,0},{16,20},{20,24},{24,28},{28,16},{32,36},... | collective-permute-start | bytes 1179656 | tf_op jit(solution)/shard_map/ppermute | solution.py:343
  7.2 21.0 %collective-permute-start.6 = (bf16[128,1536]{1,0:T(8,128)(2,1)}, bf16[128,1536]{1,0:T(8,128)(2,1)S(1)}, u32[]{:S(2)}, u32[]{:S(2)}) collective-permute-start(bf16[128,1536]{1,0:T(8,128)(2,1)} %get-tuple-element.53), channel_id=1, source_target_pairs={{0,8},{4,12},{8,0},{12,4},{16,24},{20,28},{24,16},{28,20},{32,40},... | collective-permute-start | bytes 1179656 | tf_op jit(solution)/shard_map/ppermute | solution.py:343
  9.9 18.3 %collective-permute-start.7 = (bf16[128,1536]{1,0:T(8,128)(2,1)}, bf16[128,1536]{1,0:T(8,128)(2,1)S(1)}, u32[]{:S(2)}, u32[]{:S(2)}) collective-permute-start(bf16[128,1536]{1,0:T(8,128)(2,1)} %get-tuple-element.54), channel_id=1, source_target_pairs={{0,12},{4,0},{8,4},{12,8},{16,28},{20,16},{24,20},{28,24},{32,44},... | collective-permute-start | bytes 1179656 | tf_op jit(solution)/shard_map/ppermute | solution.py:343
  11.4 10.5 %collective-permute-start.1 = (bf16[128,256]{1,0:T(8,128)(2,1)}, bf16[128,256]{1,0:T(8,128)(2,1)S(1)}, u32[]{:S(2)}, u32[]{:S(2)}) collective-permute-start(bf16[128,256]{1,0:T(8,128)(2,1)} %get-tuple-element.45), channel_id=1, source_target_pairs={{0,16},{4,20},{8,24},{12,28},{16,32},{20,36},{24,40},{28,44},{32,4... | collective-permute-start | bytes 196616 | tf_op jit(solution)/shard_map/ppermute | solution.py:339
  14.0 21.5 %copy-start = (f32[16,512]{1,0:T(8,128)S(1)}, f32[16,512]{1,0:T(8,128)}, u32[]{:S(2)}) copy-start(f32[16,512]{1,0:T(8,128)} %mixing_ref.1) | copy-start | bytes 98308
  22.4 12.3 %collective-permute-start.2 = (bf16[128,768]{1,0:T(8,128)(2,1)S(1)}, bf16[128,768]{1,0:T(8,128)(2,1)S(1)}, u32[]{:S(2)}, u32[]{:S(2)}) collective-permute-start(bf16[128,768]{1,0:T(8,128)(2,1)S(1)} %get-tuple-element.47), channel_id=1, source_target_pairs={{0,4},{4,8},{8,12},{12,0},{16,20},{20,24},{24,28},{28,16},{32,36},... | collective-permute-start | bytes 589832 | tf_op jit(solution)/shard_map/ppermute | solution.py:343
  24.0 11.5 %collective-permute-start.3 = (bf16[128,768]{1,0:T(8,128)(2,1)S(1)}, bf16[128,768]{1,0:T(8,128)(2,1)S(1)}, u32[]{:S(2)}, u32[]{:S(2)}) collective-permute-start(bf16[128,768]{1,0:T(8,128)(2,1)S(1)} %get-tuple-element.48), channel_id=1, source_target_pairs={{0,8},{4,12},{8,0},{12,4},{16,24},{20,28},{24,16},{28,20},{32,40},... | collective-permute-start | bytes 589832 | tf_op jit(solution)/shard_map/ppermute | solution.py:343
  26.7 8.8 %collective-permute-start.4 = (bf16[128,768]{1,0:T(8,128)(2,1)S(1)}, bf16[128,768]{1,0:T(8,128)(2,1)S(1)}, u32[]{:S(2)}, u32[]{:S(2)}) collective-permute-start(bf16[128,768]{1,0:T(8,128)(2,1)S(1)} %get-tuple-element.49), channel_id=1, source_target_pairs={{0,12},{4,0},{8,4},{12,8},{16,28},{20,16},{24,20},{28,24},{32,44},... | collective-permute-start | bytes 589832 | tf_op jit(solution)/shard_map/ppermute | solution.py:343
  28.9 7.5 %collective-permute-start.8 = (bf16[512,512]{1,0:T(8,128)(2,1)S(1)}, bf16[512,512]{1,0:T(8,128)(2,1)S(1)}, u32[]{:S(2)}, u32[]{:S(2)}) collective-permute-start(bf16[512,512]{1,0:T(8,128)(2,1)S(1)} %get-tuple-element.56), channel_id=1, source_target_pairs={{0,1},{1,0},{2,3},{3,2},{4,5},{5,4},{6,7},{7,6},{8,9},{9,8},{10,11... | collective-permute-start | bytes 1572872 | tf_op jit(solution)/shard_map/ppermute | solution.py:349
  29.0 24.3 %collective-permute-start.9 = (bf16[512,768]{1,0:T(8,128)(2,1)S(1)}, bf16[512,768]{1,0:T(8,128)(2,1)S(1)}, u32[]{:S(2)}, u32[]{:S(2)}) collective-permute-start(bf16[512,768]{1,0:T(8,128)(2,1)S(1)} %get-tuple-element.57.c_ref.qm_ref), channel_id=1, source_target_pairs={{0,240},{4,244},{8,248},{12,252},{16,0},{20,4},{24,8},{28,12},{32,... | collective-permute-start | bytes 2359304 | tf_op jit(solution)/shard_map/ppermute | solution.py:339
  36.1 1.8 %collective-permute-start.10 = (bf16[512,256]{1,0:T(8,128)(2,1)S(1)}, bf16[512,256]{1,0:T(8,128)(2,1)S(1)}, u32[]{:S(2)}, u32[]{:S(2)}) collective-permute-start(bf16[512,256]{1,0:T(8,128)(2,1)S(1)} %get-tuple-element.58.kpm_ref), channel_id=1, source_target_pairs={{0,1},{1,0},{2,3},{3,2},{4,5},{5,4},{6,7},{7,6},{8,9},{9,8},{10,11... | collective-permute-start | bytes 786440 | tf_op jit(solution)/shard_map/ppermute | solution.py:349
  43.5 9.8 %collective-permute-start.11 = (f32[4,2,512]{2,1,0:T(2,128)S(1)}, f32[4,2,512]{2,1,0:T(2,128)S(1)}, u32[]{:S(2)}, u32[]{:S(2)}) collective-permute-start(f32[4,2,512]{2,1,0:T(2,128)S(1)} %get-tuple-element.59), channel_id=1, source_target_pairs={{0,240},{4,244},{8,248},{12,252},{16,0},{20,4},{24,8},{28,12},{32,... | collective-permute-start | bytes 49160 | tf_op jit(solution)/shard_map/ppermute | solution.py:339
  53.3 1.6 %collective-permute-start.12 = (bf16[512,256]{1,0:T(8,128)(2,1)S(1)}, bf16[512,256]{1,0:T(8,128)(2,1)S(1)}, u32[]{:S(2)}, u32[]{:S(2)}) collective-permute-start(bf16[512,256]{1,0:T(8,128)(2,1)S(1)} %slice.3), channel_id=1, source_target_pairs={{0,1},{1,0},{2,3},{3,2},{4,5},{5,4},{6,7},{7,6},{8,9},{9,8},{10,11... | collective-permute-start | bytes 786440 | tf_op jit(solution)/shard_map/ppermute | solution.py:349
  53.4 10.6 %collective-permute-start.14 = (bf16[512,256]{1,0:T(8,128)(2,1)S(1)}, bf16[512,256]{1,0:T(8,128)(2,1)S(1)}, u32[]{:S(2)}, u32[]{:S(2)}) collective-permute-start(bf16[512,256]{1,0:T(8,128)(2,1)S(1)} %get-tuple-element.76), channel_id=1, source_target_pairs={{0,1},{1,0},{2,3},{3,2},{4,5},{5,4},{6,7},{7,6},{8,9},{9,8},{10,11... | collective-permute-start | bytes 786440 | tf_op jit(solution)/shard_map/ppermute | solution.py:349
  58.8 5.2 %collective-permute-start.13 = (bf16[512,256]{1,0:T(8,128)(2,1)S(1)}, bf16[512,256]{1,0:T(8,128)(2,1)S(1)}, u32[]{:S(2)}, u32[]{:S(2)}) collective-permute-start(bf16[512,256]{1,0:T(8,128)(2,1)S(1)} %get-tuple-element.74), channel_id=1, source_target_pairs={{0,1},{1,0},{2,3},{3,2},{4,5},{5,4},{6,7},{7,6},{8,9},{9,8},{10,11... | collective-permute-start | bytes 786440 | tf_op jit(solution)/shard_map/ppermute | solution.py:349
  59.0 9.4 %collective-permute-start.19 = (f32[4,512]{1,0:T(4,128)S(1)}, f32[4,512]{1,0:T(4,128)S(1)}, u32[]{:S(2)}, u32[]{:S(2)}) collective-permute-start(f32[4,512]{1,0:T(4,128)S(1)} %bitcast.10), channel_id=1, source_target_pairs={{0,16},{4,20},{8,24},{12,28},{16,0},{20,4},{24,8},{28,12},{32,48},... | collective-permute-start | bytes 24584 | tf_op jit(solution)/shard_map/ppermute | solution.py:401
  60.4 10.2 %collective-permute-start.20 = (f32[4,512]{1,0:T(4,128)S(1)}, f32[4,512]{1,0:T(4,128)S(1)}, u32[]{:S(2)}, u32[]{:S(2)}) collective-permute-start(f32[4,512]{1,0:T(4,128)S(1)} %bitcast.11), channel_id=1, source_target_pairs={{0,32},{4,36},{8,40},{12,44},{16,48},{20,52},{24,56},{28,60},{32,0... | collective-permute-start | bytes 24584 | tf_op jit(solution)/shard_map/ppermute | solution.py:401
  62.3 8.3 %collective-permute-start.21 = (f32[4,512]{1,0:T(4,128)S(1)}, f32[4,512]{1,0:T(4,128)S(1)}, u32[]{:S(2)}, u32[]{:S(2)}) collective-permute-start(f32[4,512]{1,0:T(4,128)S(1)} %bitcast.12), channel_id=1, source_target_pairs={{0,48},{4,52},{8,56},{12,60},{16,32},{20,36},{24,40},{28,44},{32,1... | collective-permute-start | bytes 24584 | tf_op jit(solution)/shard_map/ppermute | solution.py:401
  64.7 21.5 %collective-permute-start.15 = (bf16[128,1024]{1,0:T(8,128)(2,1)S(1)}, bf16[128,1024]{1,0:T(8,128)(2,1)S(1)}, u32[]{:S(2)}, u32[]{:S(2)}) collective-permute-start(bf16[128,1024]{1,0:T(8,128)(2,1)S(1)} %get-tuple-element.78), channel_id=1, source_target_pairs={{0,4},{4,8},{8,12},{12,0},{16,20},{20,24},{24,28},{28,16},{32,36},... | collective-permute-start | bytes 786440 | tf_op jit(solution)/shard_map/ppermute | solution.py:343
  67.8 20.1 %collective-permute-start.16 = (bf16[128,1024]{1,0:T(8,128)(2,1)S(1)}, bf16[128,1024]{1,0:T(8,128)(2,1)S(1)}, u32[]{:S(2)}, u32[]{:S(2)}) collective-permute-start(bf16[128,1024]{1,0:T(8,128)(2,1)S(1)} %get-tuple-element.79), channel_id=1, source_target_pairs={{0,8},{4,12},{8,0},{12,4},{16,24},{20,28},{24,16},{28,20},{32,40},... | collective-permute-start | bytes 786440 | tf_op jit(solution)/shard_map/ppermute | solution.py:343
  68.4 19.4 %collective-permute-start.17 = (bf16[128,1024]{1,0:T(8,128)(2,1)S(1)}, bf16[128,1024]{1,0:T(8,128)(2,1)S(1)}, u32[]{:S(2)}, u32[]{:S(2)}) collective-permute-start(bf16[128,1024]{1,0:T(8,128)(2,1)S(1)} %get-tuple-element.80), channel_id=1, source_target_pairs={{0,12},{4,0},{8,4},{12,8},{16,28},{20,16},{24,20},{28,24},{32,44},... | collective-permute-start | bytes 786440 | tf_op jit(solution)/shard_map/ppermute | solution.py:343
  70.6 6.9 %collective-permute-start.22 = (f32[4,512]{1,0:T(4,128)S(1)}, f32[4,512]{1,0:T(4,128)S(1)}, u32[]{:S(2)}, u32[]{:S(2)}) collective-permute-start(f32[4,512]{1,0:T(4,128)S(1)} %add_add_fusion.1), channel_id=1, source_target_pairs={{0,64},{4,68},{8,72},{12,76},{16,80},{20,84},{24,88},{28,92},{32,9... | collective-permute-start | bytes 24584 | tf_op jit(solution)/shard_map/ppermute | solution.py:401
  75.0 7.6 %collective-permute-start.23 = (f32[4,512]{1,0:T(4,128)S(1)}, f32[4,512]{1,0:T(4,128)S(1)}, u32[]{:S(2)}, u32[]{:S(2)}) collective-permute-start(f32[4,512]{1,0:T(4,128)S(1)} %add_add_fusion.1), channel_id=1, source_target_pairs={{0,128},{4,132},{8,136},{12,140},{16,144},{20,148},{24,152},{28,15... | collective-permute-start | bytes 24584 | tf_op jit(solution)/shard_map/ppermute | solution.py:401
  77.5 5.8 %collective-permute-start.24 = (f32[4,512]{1,0:T(4,128)S(1)}, f32[4,512]{1,0:T(4,128)S(1)}, u32[]{:S(2)}, u32[]{:S(2)}) collective-permute-start(f32[4,512]{1,0:T(4,128)S(1)} %add_add_fusion.1), channel_id=1, source_target_pairs={{0,192},{4,196},{8,200},{12,204},{16,208},{20,212},{24,216},{28,22... | collective-permute-start | bytes 24584 | tf_op jit(solution)/shard_map/ppermute | solution.py:401
  83.3 6.1 %collective-permute-start.25 = (f32[4,512]{1,0:T(4,128)S(1)}, f32[4,512]{1,0:T(4,128)S(1)}, u32[]{:S(2)}, u32[]{:S(2)}) collective-permute-start(f32[4,512]{1,0:T(4,128)S(1)} %add_add_fusion.refs_0_), channel_id=1, source_target_pairs={{0,4},{4,8},{8,12},{12,0},{16,20},{20,24},{24,28},{28,16},{32,36},... | collective-permute-start | bytes 24584 | tf_op jit(solution)/shard_map/ppermute | solution.py:343
  85.1 5.2 %collective-permute-start.26 = (f32[4,512]{1,0:T(4,128)S(1)}, f32[4,512]{1,0:T(4,128)S(1)}, u32[]{:S(2)}, u32[]{:S(2)}) collective-permute-start(f32[4,512]{1,0:T(4,128)S(1)} %add_add_fusion.refs_0_), channel_id=1, source_target_pairs={{0,8},{4,12},{8,0},{12,4},{16,24},{20,28},{24,16},{28,20},{32,40},... | collective-permute-start | bytes 24584 | tf_op jit(solution)/shard_map/ppermute | solution.py:343
  86.1 4.1 %collective-permute-start.27 = (f32[4,512]{1,0:T(4,128)S(1)}, f32[4,512]{1,0:T(4,128)S(1)}, u32[]{:S(2)}, u32[]{:S(2)}) collective-permute-start(f32[4,512]{1,0:T(4,128)S(1)} %add_add_fusion.refs_0_), channel_id=1, source_target_pairs={{0,12},{4,0},{8,4},{12,8},{16,28},{20,16},{24,20},{28,24},{32,44},... | collective-permute-start | bytes 24584 | tf_op jit(solution)/shard_map/ppermute | solution.py:343
  88.5 5.1 %collective-permute-start.18 = (f32[128,256]{1,0:T(8,128)S(1)}, f32[128,256]{1,0:T(8,128)S(1)}, u32[]{:S(2)}, u32[]{:S(2)}) collective-permute-start(f32[128,256]{1,0:T(8,128)S(1)} %get-tuple-element.82), channel_id=1, source_target_pairs={{0,2},{1,3},{2,0},{3,1},{4,6},{5,7},{6,4},{7,5},{8,10},{9,11},{10,... | collective-permute-start | bytes 393224 | tf_op jit(solution)/shard_map/ppermute | solution.py:436

commit v6 on v5

--- a/solution.py
+++ b/solution.py
@@ -422,7 +422,7 @@
          pltpu.VMEM((span, width), F32)],
         (at, mix, vk, vk, kq_other, cq_next, cq_next, q_next_other, next_stats, dk, dv), 6)
     dk_other, dmix = lax.optimization_barrier((dk_other, dmix))
-    dmix = exchange(dmix.reshape(heads, width), GROUP, 2 * GROUP)
+    dmix = exchange(dmix.reshape(heads, width), GROUP, 8 * GROUP)
 
     dk_got, dq_got = core_swap(dk_other), core_swap(dq_other)
     back = call(
@@ -432,7 +432,7 @@
     back = turns(back)
     keep, give = call(sums_kernel, (1,), [SMEM] + [fixed((tok, 2 * HALF), 0, n_v // (2 * HALF))] * GROUP,
                       [(fixed((tok, HALF)), (tok, HALF), F32)] * 2, [], (at, *back), 1)
-    dmix = exchange(dmix, 4 * GROUP, 8 * GROUP)
+    dmix = exchange(dmix, 2 * GROUP, 4 * GROUP)
     got = lax.ppermute(give, "head", [(0, 2), (1, 3), (2, 0), (3, 1)])
     (d_values,) = call(values_kernel, (1,), [SMEM] + [fixed((tok, n_v))] * GROUP,
                        [(fixed((tok, GROUP * n_v)), (tok, GROUP * n_v), B16)], [], (at, *back), 1)

time: 94.3 us -> 98.5 us (1.045)
  starting transfers between devices: 54.6 us -> 57.1 us
  waiting for transfers between devices: 16.3 us -> 18 us
    ppermute x12, starting transfers between devices: 22 us -> 23.5 us  [turn(): return lax.ppermute(x, 'seq', pairs)]
    ppermute x6, starting transfers between devices: 14.1 us -> 15.5 us  [from_peer(): return lax.ppermute(x, 'seq', [(i, i ^ by) for i in range(peers)])]
    ppermute x6, waiting for transfers between devices: 3.59 us -> 4.88 us  [from_peer(): return lax.ppermute(x, 'seq', [(i, i ^ by) for i in range(peers)])]
  transfers between devices with their start and end apart: 28 -> 28, of which waited for: 8 -> 9; matrix products, arithmetic and copies ran while one was open for 0% -> 0% of each run, Pallas kernels for 23% -> 22%
where the time goes in v6:
time: 98.5 us; the launch traced here: 98.4 us
  starting transfers between devices  57.1 us (58%)
  Pallas kernels  22.4 us (23%)
  waiting for transfers between devices  18 us (18%)
    ppermute x12, starting transfers between devices, turn(): return lax.ppermute(x, 'seq', pairs)  23.5 us
    pallas_call x13, Pallas kernels, call(): pl.pallas_call(body, grid=grid, in_specs=ins, out_specs=[spec for spec, _...  22.4 us
    ppermute x4, starting transfers between devices, to_group(): return lax.ppermute(x, 'seq', pairs)  16.5 us
    ppermute x6, starting transfers between devices, from_peer(): return lax.ppermute(x, 'seq', [(i, i ^ by) for i in range(peers)])  15.5 us
    ppermute x4, waiting for transfers between devices, to_group(): return lax.ppermute(x, 'seq', pairs)  7.81 us
    ppermute x6, waiting for transfers between devices, from_peer(): return lax.ppermute(x, 'seq', [(i, i ^ by) for i in range(peers)])  4.88 us
    ppermute x5, waiting for transfers between devices, core_swap(): return lax.ppermute(x, 'head', [(0, 1), (1, 0), (2, 3), (3, 2)])  2.54 us
    ppermute x12, waiting for transfers between devices, turn(): return lax.ppermute(x, 'seq', pairs)  1.99 us
  transfers between devices with their start and end apart: 28, of which 9 were waited for; matrix products, arithmetic and copies ran while one was open for 0% of the time, Pallas kernels for 22%

profile of v6, /device:TPU:8, one launch (start us, length us, event | category | flops | bytes accessed | tf_op | source)
XLA Modules:
  0.0 98.4 jit_solution(6198909477271192478)
XLA Ops:
  0.6 2.4 %collective-permute-start = (bf16[128,2048]{1,0:T(8,128)(2,1)}, bf16[128,2048]{1,0:T(8,128)(2,1)S(1)}, u32[]{:S(2)}, u32[]{:S(2)}) collective-permute-start(bf16[128,2048]{1,0:T(8,128)(2,1)} %v_ref.1), channel_id=1, source_target_pairs={{0,16},{4,20},{8,24},{12,28},{16,32},{20,36},{24,40},{28,44},{32,4... | collective-permute-start | bytes 1572872 | tf_op jit(solution)/shard_map/ppermute | solution.py:339
  3.0 2.6 %shard_map.84 = (bf16[128,1536]{1,0:T(8,128)(2,1)}, bf16[128,1536]{1,0:T(8,128)(2,1)}, bf16[128,1536]{1,0:T(8,128)(2,1)}, bf16[128,1536]{1,0:T(8,128)(2,1)}, bf16[128,256]{1,0:T(8,128)(2,1)}) custom-call(bf16[128,2048]{1,0:T(8,128)(2,1)} %v_ref.1, bf16[128,2048]{1,0:T(8,128)(2,1)} %c_ref.1, bf16[128,512]{1,0:T(8,128)(2,1)} %k_ref.1, bf16[128,512]{1,0:T(8,128)(2,1)} %q_ref.1), custom_call_target="tpu_custom_call" | custom-call | flops 3000000000 | bytes 1000000 | tf_op jit(solution)/shard_map/pallas_call | solution.py:300
  5.6 1.6 %collective-permute-start.5 = (bf16[128,1536]{1,0:T(8,128)(2,1)}, bf16[128,1536]{1,0:T(8,128)(2,1)S(1)}, u32[]{:S(2)}, u32[]{:S(2)}) collective-permute-start(bf16[128,1536]{1,0:T(8,128)(2,1)} %get-tuple-element.52), channel_id=1, source_target_pairs={{0,4},{4,8},{8,12},{12,0},{16,20},{20,24},{24,28},{28,16},{32,36},... | collective-permute-start | bytes 1179656 | tf_op jit(solution)/shard_map/ppermute | solution.py:343
  7.2 2.7 %collective-permute-start.6 = (bf16[128,1536]{1,0:T(8,128)(2,1)}, bf16[128,1536]{1,0:T(8,128)(2,1)S(1)}, u32[]{:S(2)}, u32[]{:S(2)}) collective-permute-start(bf16[128,1536]{1,0:T(8,128)(2,1)} %get-tuple-element.53), channel_id=1, source_target_pairs={{0,8},{4,12},{8,0},{12,4},{16,24},{20,28},{24,16},{28,20},{32,40},... | collective-permute-start | bytes 1179656 | tf_op jit(solution)/shard_map/ppermute | solution.py:343
  9.9 1.4 %collective-permute-start.7 = (bf16[128,1536]{1,0:T(8,128)(2,1)}, bf16[128,1536]{1,0:T(8,128)(2,1)S(1)}, u32[]{:S(2)}, u32[]{:S(2)}) collective-permute-start(bf16[128,1536]{1,0:T(8,128)(2,1)} %get-tuple-element.54), channel_id=1, source_target_pairs={{0,12},{4,0},{8,4},{12,8},{16,28},{20,16},{24,20},{28,24},{32,44},... | collective-permute-start | bytes 1179656 | tf_op jit(solution)/shard_map/ppermute | solution.py:343
  11.4 2.6 %collective-permute-start.1 = (bf16[128,256]{1,0:T(8,128)(2,1)}, bf16[128,256]{1,0:T(8,128)(2,1)S(1)}, u32[]{:S(2)}, u32[]{:S(2)}) collective-permute-start(bf16[128,256]{1,0:T(8,128)(2,1)} %get-tuple-element.45), channel_id=1, source_target_pairs={{0,16},{4,20},{8,24},{12,28},{16,32},{20,36},{24,40},{28,44},{32,4... | collective-permute-start | bytes 196616 | tf_op jit(solution)/shard_map/ppermute | solution.py:339
  14.0 7.8 %collective-permute-done.1.k_ref = bf16[128,256]{1,0:T(8,128)(2,1)S(1)} collective-permute-done((bf16[128,256]{1,0:T(8,128)(2,1)}, bf16[128,256]{1,0:T(8,128)(2,1)S(1)}, u32[]{:S(2)}, u32[]{:S(2)}) %collective-permute-start.1) | collective-permute-done | bytes 65568 | tf_op jit(solution)/shard_map/ppermute | solution.py:339
  21.8 0.6 shard_map.85
  22.4 1.6 %collective-permute-start.2 = (bf16[128,768]{1,0:T(8,128)(2,1)S(1)}, bf16[128,768]{1,0:T(8,128)(2,1)S(1)}, u32[]{:S(2)}, u32[]{:S(2)}) collective-permute-start(bf16[128,768]{1,0:T(8,128)(2,1)S(1)} %get-tuple-element.47), channel_id=1, source_target_pairs={{0,4},{4,8},{8,12},{12,0},{16,20},{20,24},{24,28},{28,16},{32,36},... | collective-permute-start | bytes 589832 | tf_op jit(solution)/shard_map/ppermute | solution.py:343
  24.0 2.7 %collective-permute-start.3 = (bf16[128,768]{1,0:T(8,128)(2,1)S(1)}, bf16[128,768]{1,0:T(8,128)(2,1)S(1)}, u32[]{:S(2)}, u32[]{:S(2)}) collective-permute-start(bf16[128,768]{1,0:T(8,128)(2,1)S(1)} %get-tuple-element.48), channel_id=1, source_target_pairs={{0,8},{4,12},{8,0},{12,4},{16,24},{20,28},{24,16},{28,20},{32,40},... | collective-permute-start | bytes 589832 | tf_op jit(solution)/shard_map/ppermute | solution.py:343
  26.7 1.4 %collective-permute-start.4 = (bf16[128,768]{1,0:T(8,128)(2,1)S(1)}, bf16[128,768]{1,0:T(8,128)(2,1)S(1)}, u32[]{:S(2)}, u32[]{:S(2)}) collective-permute-start(bf16[128,768]{1,0:T(8,128)(2,1)S(1)} %get-tuple-element.49), channel_id=1, source_target_pairs={{0,12},{4,0},{8,4},{12,8},{16,28},{20,16},{24,20},{28,24},{32,44},... | collective-permute-start | bytes 589832 | tf_op jit(solution)/shard_map/ppermute | solution.py:343
  28.2 0.7 shard_map.87
  29.0 5.8 %collective-permute-start.9 = (bf16[512,768]{1,0:T(8,128)(2,1)S(1)}, bf16[512,768]{1,0:T(8,128)(2,1)S(1)}, u32[]{:S(2)}, u32[]{:S(2)}) collective-permute-start(bf16[512,768]{1,0:T(8,128)(2,1)S(1)} %get-tuple-element.57.c_ref.qm_ref), channel_id=1, source_target_pairs={{0,240},{4,244},{8,248},{12,252},{16,0},{20,4},{24,8},{28,12},{32,... | collective-permute-start | bytes 2359304 | tf_op jit(solution)/shard_map/ppermute | solution.py:339
  34.8 0.8 collective-permute-done.3.k2_ref.vp2_ref
  35.5 0.6 shard_map.86
  36.1 0.3 collective-permute-start.10
  36.4 1.5 %collective-permute-done.10.kpo_ref = bf16[512,256]{1,0:T(8,128)(2,1)S(1)} collective-permute-done((bf16[512,256]{1,0:T(8,128)(2,1)S(1)}, bf16[512,256]{1,0:T(8,128)(2,1)S(1)}, u32[]{:S(2)}, u32[]{:S(2)}) %collective-permute-start.10) | collective-permute-done | bytes 262176 | tf_op jit(solution)/shard_map/ppermute | solution.py:349
  37.9 5.5 %shard_map.88 = (f32[4,2,512]{2,1,0:T(2,128)S(1)}, bf16[4,2,768,256]{3,2,1,0:T(8,128)(2,1)S(1)}, bf16[4,3,256,256]{3,2,1,0:T(8,128)(2,1)S(1)}, bf16[1024,512]{1,0:T(8,128)(2,1)S(1)}, bf16[512,512]{1,0:T(8,128)(2,1)S(1)}) custom-call(s32[5]{0:T(128)S(1)} %stack.27.at_ref, f32[4,1,512]{2,1,0:T(1,128)S(1)} %get-tuple-element.50.mix_ref, ...), custom_call_target="tpu_custom_call" | custom-call | flops 2500000000 | bytes 1000000 | tf_op jit(solution)/shard_map/pallas_call | solution.py:300
  43.5 5.7 %collective-permute-start.11 = (f32[4,2,512]{2,1,0:T(2,128)S(1)}, f32[4,2,512]{2,1,0:T(2,128)S(1)}, u32[]{:S(2)}, u32[]{:S(2)}) collective-permute-start(f32[4,2,512]{2,1,0:T(2,128)S(1)} %get-tuple-element.59), channel_id=1, source_target_pairs={{0,240},{4,244},{8,248},{12,252},{16,0},{20,4},{24,8},{28,12},{32,... | collective-permute-start | bytes 49160 | tf_op jit(solution)/shard_map/ppermute | solution.py:339
  49.2 2.7 %shard_map.90 = (f32[512,256]{1,0:T(8,128)S(1)}, bf16[512,256]{1,0:T(8,128)(2,1)S(1)}, f32[4,1,512]{2,1,0:T(1,128)S(1)}) custom-call(s32[5]{0:T(128)S(1)} %stack.27.at_ref, f32[4,1,512]{2,1,0:T(1,128)S(1)} %get-tuple-element.50.mix_ref, bf16[1024,512]{1,0:T(8,128)(2,1)S(1)} %get-tuple-element.64.k_ref, bf16[512,512]{1,0:T(8,128)(2,1)S(1)} %get-tuple-element.60.q_ref, ...), custom_call_target="tpu_custom_call" | custom-call | flops 300000000 | bytes 1000000 | tf_op jit(solution)/shard_map/pallas_call | solution.py:300
  51.9 1.4 %shard_map.89 = (f32[512,512]{1,0:T(8,128)S(1)}, f32[512,512]{1,0:T(8,128)S(1)}) custom-call(f32[4,1,512]{2,1,0:T(1,128)S(1)} %get-tuple-element.50.mix_ref, bf16[512,768]{1,0:T(8,128)(2,1)S(1)} %get-tuple-element.57.c_ref.qm_ref, bf16[512,512]{1,0:T(8,128)(2,1)S(1)} %get-tuple-element.60.q_ref, bf16[4,2,768,256]{3,2,1,0:T(8,128)(2,1)S(1)} %get-tuple-element.61.grad_ref, ...), custom_call_target="tpu_custom_call" | custom-call | flops 300000000 | bytes 1000000 | tf_op jit(solution)/shard_map/pallas_call | solution.py:300
  53.4 0.5 collective-permute-start.14
  53.9 1.0 %collective-permute-done.12.qno_ref = bf16[512,256]{1,0:T(8,128)(2,1)S(1)} collective-permute-done((bf16[512,256]{1,0:T(8,128)(2,1)S(1)}, bf16[512,256]{1,0:T(8,128)(2,1)S(1)}, u32[]{:S(2)}, u32[]{:S(2)}) %collective-permute-start.12) | collective-permute-done | bytes 262176 | tf_op jit(solution)/shard_map/ppermute | solution.py:349
  55.0 3.8 %shard_map.91 = (f32[512,256]{1,0:T(8,128)S(1)}, bf16[512,256]{1,0:T(8,128)(2,1)S(1)}, bf16[512,512]{1,0:T(8,128)(2,1)S(1)}) custom-call(s32[5]{0:T(128)S(1)} %stack.27.at_ref, f32[4,1,512]{2,1,0:T(1,128)S(1)} %get-tuple-element.50.mix_ref, bf16[512,768]{1,0:T(8,128)(2,1)S(1)} %get-tuple-element.55.v_ref.km_ref, ...), custom_call_target="tpu_custom_call" | custom-call | flops 6000000000 | bytes 1000000 | tf_op jit(solution)/shard_map/pallas_call | solution.py:300
  58.8 0.2 collective-permute-start.13
  59.0 1.4 %collective-permute-start.19 = (f32[4,512]{1,0:T(4,128)S(1)}, f32[4,512]{1,0:T(4,128)S(1)}, u32[]{:S(2)}, u32[]{:S(2)}) collective-permute-start(f32[4,512]{1,0:T(4,128)S(1)} %bitcast.10), channel_id=1, source_target_pairs={{0,16},{4,20},{8,24},{12,28},{16,0},{20,4},{24,8},{28,12},{32,48},... | collective-permute-start | bytes 24584 | tf_op jit(solution)/shard_map/ppermute | solution.py:401
  60.4 6.3 %collective-permute-start.20 = (f32[4,512]{1,0:T(4,128)S(1)}, f32[4,512]{1,0:T(4,128)S(1)}, u32[]{:S(2)}, u32[]{:S(2)}) collective-permute-start(f32[4,512]{1,0:T(4,128)S(1)} %bitcast.11), channel_id=1, source_target_pairs={{0,128},{4,132},{8,136},{12,140},{16,144},{20,148},{24,152},{28,15... | collective-permute-start | bytes 24584 | tf_op jit(solution)/shard_map/ppermute | solution.py:401
  66.7 1.2 %collective-permute-start.21 = (f32[4,512]{1,0:T(4,128)S(1)}, f32[4,512]{1,0:T(4,128)S(1)}, u32[]{:S(2)}, u32[]{:S(2)}) collective-permute-start(f32[4,512]{1,0:T(4,128)S(1)} %bitcast.12), channel_id=1, source_target_pairs={{0,144},{4,148},{8,152},{12,156},{16,128},{20,132},{24,136},{28,14... | collective-permute-start | bytes 24584 | tf_op jit(solution)/shard_map/ppermute | solution.py:401
  67.9 0.7 shard_map.92
  68.6 3.1 %collective-permute-start.15 = (bf16[128,1024]{1,0:T(8,128)(2,1)S(1)}, bf16[128,1024]{1,0:T(8,128)(2,1)S(1)}, u32[]{:S(2)}, u32[]{:S(2)}) collective-permute-start(bf16[128,1024]{1,0:T(8,128)(2,1)S(1)} %get-tuple-element.78), channel_id=1, source_target_pairs={{0,4},{4,8},{8,12},{12,0},{16,20},{20,24},{24,28},{28,16},{32,36},... | collective-permute-start | bytes 786440 | tf_op jit(solution)/shard_map/ppermute | solution.py:343
  71.7 0.6 collective-permute-start.16
  72.4 2.1 %collective-permute-start.17 = (bf16[128,1024]{1,0:T(8,128)(2,1)S(1)}, bf16[128,1024]{1,0:T(8,128)(2,1)S(1)}, u32[]{:S(2)}, u32[]{:S(2)}) collective-permute-start(bf16[128,1024]{1,0:T(8,128)(2,1)S(1)} %get-tuple-element.80), channel_id=1, source_target_pairs={{0,12},{4,0},{8,4},{12,8},{16,28},{20,16},{24,20},{28,24},{32,44},... | collective-permute-start | bytes 786440 | tf_op jit(solution)/shard_map/ppermute | solution.py:343
  74.5 2.3 %collective-permute-done.21 = f32[4,512]{1,0:T(4,128)S(1)} collective-permute-done((f32[4,512]{1,0:T(4,128)S(1)}, f32[4,512]{1,0:T(4,128)S(1)}, u32[]{:S(2)}, u32[]{:S(2)}) %collective-permute-start.21) | collective-permute-done | bytes 8224 | tf_op jit(solution)/shard_map/ppermute | solution.py:401
  76.8 1.0 %collective-permute-start.22 = (f32[4,512]{1,0:T(4,128)S(1)}, f32[4,512]{1,0:T(4,128)S(1)}, u32[]{:S(2)}, u32[]{:S(2)}) collective-permute-start(f32[4,512]{1,0:T(4,128)S(1)} %add_add_fusion.1), channel_id=1, source_target_pairs={{0,32},{4,36},{8,40},{12,44},{16,48},{20,52},{24,56},{28,60},{32,0... | collective-permute-start | bytes 24584 | tf_op jit(solution)/shard_map/ppermute | solution.py:401
  77.8 2.6 %collective-permute-start.23 = (f32[4,512]{1,0:T(4,128)S(1)}, f32[4,512]{1,0:T(4,128)S(1)}, u32[]{:S(2)}, u32[]{:S(2)}) collective-permute-start(f32[4,512]{1,0:T(4,128)S(1)} %add_add_fusion.1), channel_id=1, source_target_pairs={{0,64},{4,68},{8,72},{12,76},{16,80},{20,84},{24,88},{28,92},{32,9... | collective-permute-start | bytes 24584 | tf_op jit(solution)/shard_map/ppermute | solution.py:401
  80.4 0.1 collective-permute-done.22
  80.5 3.0 %collective-permute-start.24 = (f32[4,512]{1,0:T(4,128)S(1)}, f32[4,512]{1,0:T(4,128)S(1)}, u32[]{:S(2)}, u32[]{:S(2)}) collective-permute-start(f32[4,512]{1,0:T(4,128)S(1)} %add_add_fusion.1), channel_id=1, source_target_pairs={{0,96},{4,100},{8,104},{12,108},{16,112},{20,116},{24,120},{28,124... | collective-permute-start | bytes 24584 | tf_op jit(solution)/shard_map/ppermute | solution.py:401
  83.5 2.5 %collective-permute-done.24 = f32[4,512]{1,0:T(4,128)S(1)} collective-permute-done((f32[4,512]{1,0:T(4,128)S(1)}, f32[4,512]{1,0:T(4,128)S(1)}, u32[]{:S(2)}, u32[]{:S(2)}) %collective-permute-start.24) | collective-permute-done | bytes 8224 | tf_op jit(solution)/shard_map/ppermute | solution.py:401
  86.0 3.3 %collective-permute-start.25 = (f32[4,512]{1,0:T(4,128)S(1)}, f32[4,512]{1,0:T(4,128)S(1)}, u32[]{:S(2)}, u32[]{:S(2)}) collective-permute-start(f32[4,512]{1,0:T(4,128)S(1)} %add_add_fusion.refs_0_), channel_id=1, source_target_pairs={{0,4},{4,8},{8,12},{12,0},{16,20},{20,24},{24,28},{28,16},{32,36},... | collective-permute-start | bytes 24584 | tf_op jit(solution)/shard_map/ppermute | solution.py:343
  89.3 0.8 collective-permute-start.26
  90.1 2.0 %collective-permute-start.27 = (f32[4,512]{1,0:T(4,128)S(1)}, f32[4,512]{1,0:T(4,128)S(1)}, u32[]{:S(2)}, u32[]{:S(2)}) collective-permute-start(f32[4,512]{1,0:T(4,128)S(1)} %add_add_fusion.refs_0_), channel_id=1, source_target_pairs={{0,12},{4,0},{8,4},{12,8},{16,28},{20,16},{24,20},{28,24},{32,44},... | collective-permute-start | bytes 24584 | tf_op jit(solution)/shard_map/ppermute | solution.py:343
  92.1 0.6 shard_map.93
  92.7 0.5 collective-permute-start.18
  93.3 1.2 %collective-permute-done.26.refs_2_ = f32[4,512]{1,0:T(4,128)S(1)} collective-permute-done((f32[4,512]{1,0:T(4,128)S(1)}, f32[4,512]{1,0:T(4,128)S(1)}, u32[]{:S(2)}, u32[]{:S(2)}) %collective-permute-start.26) | collective-permute-done | bytes 8224 | tf_op jit(solution)/shard_map/ppermute | solution.py:343
  94.5 1.2 %shard_map.96 = f32[16,512]{1,0:T(8,128)} custom-call(s32[5]{0:T(128)S(1)} %stack.27.at_ref, f32[4,512]{1,0:T(4,128)S(1)} %add_add_fusion.refs_0_, f32[4,512]{1,0:T(4,128)S(1)} %collective-permute-done.25.refs_1_, f32[4,512]{1,0:T(4,128)S(1)} %collective-permute-done.26.refs_2_, f32[4,512]{1,0:T(4,128)S(1)} %collective-permute-done.27.refs_3_), custom_call_target="tpu_custom_call" | custom-call | flops 1000000000 | bytes 1000000 | tf_op jit(solution)/shard_map/pallas_call | solution.py:300
  95.6 1.4 %shard_map.95 = bf16[128,2048]{1,0:T(8,128)(2,1)} custom-call(s32[5]{0:T(128)S(1)} %stack.27.at_ref, bf16[128,1024]{1,0:T(8,128)(2,1)S(1)} %get-tuple-element.77.refs_0_, bf16[128,1024]{1,0:T(8,128)(2,1)S(1)} %collective-permute-done.15.refs_1_, bf16[128,1024]{1,0:T(8,128)(2,1)S(1)} %collective-permute-done.16.refs_2_, ...), custom_call_target="tpu_custom_call" | custom-call | flops 1000000000 | bytes 1000000 | tf_op jit(solution)/shard_map/pallas_call | solution.py:300
  97.0 0.7 collective-permute-done.18.got_ref
  97.8 0.6 shard_map.94
  (30 shorter events, 0.4 us)
Async XLA Ops:
  0.6 21.2 %collective-permute-start = (bf16[128,2048]{1,0:T(8,128)(2,1)}, bf16[128,2048]{1,0:T(8,128)(2,1)S(1)}, u32[]{:S(2)}, u32[]{:S(2)}) collective-permute-start(bf16[128,2048]{1,0:T(8,128)(2,1)} %v_ref.1), channel_id=1, source_target_pairs={{0,16},{4,20},{8,24},{12,28},{16,32},{20,36},{24,40},{28,44},{32,4... | collective-permute-start | bytes 1572872 | tf_op jit(solution)/shard_map/ppermute | solution.py:339
  5.6 22.6 %copy-start.1 = (bf16[128,1536]{1,0:T(8,128)(2,1)S(1)}, bf16[128,1536]{1,0:T(8,128)(2,1)}, u32[]{:S(2)}) copy-start(bf16[128,1536]{1,0:T(8,128)(2,1)} %get-tuple-element.51.p0_ref) | copy-start | bytes 1179652
  5.6 21.1 %collective-permute-start.5 = (bf16[128,1536]{1,0:T(8,128)(2,1)}, bf16[128,1536]{1,0:T(8,128)(2,1)S(1)}, u32[]{:S(2)}, u32[]{:S(2)}) collective-permute-start(bf16[128,1536]{1,0:T(8,128)(2,1)} %get-tuple-element.52), channel_id=1, source_target_pairs={{0,4},{4,8},{8,12},{12,0},{16,20},{20,24},{24,28},{28,16},{32,36},... | collective-permute-start | bytes 1179656 | tf_op jit(solution)/shard_map/ppermute | solution.py:343
  7.2 21.0 %collective-permute-start.6 = (bf16[128,1536]{1,0:T(8,128)(2,1)}, bf16[128,1536]{1,0:T(8,128)(2,1)S(1)}, u32[]{:S(2)}, u32[]{:S(2)}) collective-permute-start(bf16[128,1536]{1,0:T(8,128)(2,1)} %get-tuple-element.53), channel_id=1, source_target_pairs={{0,8},{4,12},{8,0},{12,4},{16,24},{20,28},{24,16},{28,20},{32,40},... | collective-permute-start | bytes 1179656 | tf_op jit(solution)/shard_map/ppermute | solution.py:343
  9.9 18.3 %collective-permute-start.7 = (bf16[128,1536]{1,0:T(8,128)(2,1)}, bf16[128,1536]{1,0:T(8,128)(2,1)S(1)}, u32[]{:S(2)}, u32[]{:S(2)}) collective-permute-start(bf16[128,1536]{1,0:T(8,128)(2,1)} %get-tuple-element.54), channel_id=1, source_target_pairs={{0,12},{4,0},{8,4},{12,8},{16,28},{20,16},{24,20},{28,24},{32,44},... | collective-permute-start | bytes 1179656 | tf_op jit(solution)/shard_map/ppermute | solution.py:343
  11.4 10.5 %collective-permute-start.1 = (bf16[128,256]{1,0:T(8,128)(2,1)}, bf16[128,256]{1,0:T(8,128)(2,1)S(1)}, u32[]{:S(2)}, u32[]{:S(2)}) collective-permute-start(bf16[128,256]{1,0:T(8,128)(2,1)} %get-tuple-element.45), channel_id=1, source_target_pairs={{0,16},{4,20},{8,24},{12,28},{16,32},{20,36},{24,40},{28,44},{32,4... | collective-permute-start | bytes 196616 | tf_op jit(solution)/shard_map/ppermute | solution.py:339
  14.0 21.5 %copy-start = (f32[16,512]{1,0:T(8,128)S(1)}, f32[16,512]{1,0:T(8,128)}, u32[]{:S(2)}) copy-start(f32[16,512]{1,0:T(8,128)} %mixing_ref.1) | copy-start | bytes 98308
  22.4 12.3 %collective-permute-start.2 = (bf16[128,768]{1,0:T(8,128)(2,1)S(1)}, bf16[128,768]{1,0:T(8,128)(2,1)S(1)}, u32[]{:S(2)}, u32[]{:S(2)}) collective-permute-start(bf16[128,768]{1,0:T(8,128)(2,1)S(1)} %get-tuple-element.47), channel_id=1, source_target_pairs={{0,4},{4,8},{8,12},{12,0},{16,20},{20,24},{24,28},{28,16},{32,36},... | collective-permute-start | bytes 589832 | tf_op jit(solution)/shard_map/ppermute | solution.py:343
  24.0 11.5 %collective-permute-start.3 = (bf16[128,768]{1,0:T(8,128)(2,1)S(1)}, bf16[128,768]{1,0:T(8,128)(2,1)S(1)}, u32[]{:S(2)}, u32[]{:S(2)}) collective-permute-start(bf16[128,768]{1,0:T(8,128)(2,1)S(1)} %get-tuple-element.48), channel_id=1, source_target_pairs={{0,8},{4,12},{8,0},{12,4},{16,24},{20,28},{24,16},{28,20},{32,40},... | collective-permute-start | bytes 589832 | tf_op jit(solution)/shard_map/ppermute | solution.py:343
  26.7 8.8 %collective-permute-start.4 = (bf16[128,768]{1,0:T(8,128)(2,1)S(1)}, bf16[128,768]{1,0:T(8,128)(2,1)S(1)}, u32[]{:S(2)}, u32[]{:S(2)}) collective-permute-start(bf16[128,768]{1,0:T(8,128)(2,1)S(1)} %get-tuple-element.49), channel_id=1, source_target_pairs={{0,12},{4,0},{8,4},{12,8},{16,28},{20,16},{24,20},{28,24},{32,44},... | collective-permute-start | bytes 589832 | tf_op jit(solution)/shard_map/ppermute | solution.py:343
  28.9 7.5 %collective-permute-start.8 = (bf16[512,512]{1,0:T(8,128)(2,1)S(1)}, bf16[512,512]{1,0:T(8,128)(2,1)S(1)}, u32[]{:S(2)}, u32[]{:S(2)}) collective-permute-start(bf16[512,512]{1,0:T(8,128)(2,1)S(1)} %get-tuple-element.56), channel_id=1, source_target_pairs={{0,1},{1,0},{2,3},{3,2},{4,5},{5,4},{6,7},{7,6},{8,9},{9,8},{10,11... | collective-permute-start | bytes 1572872 | tf_op jit(solution)/shard_map/ppermute | solution.py:349
  29.0 24.3 %collective-permute-start.9 = (bf16[512,768]{1,0:T(8,128)(2,1)S(1)}, bf16[512,768]{1,0:T(8,128)(2,1)S(1)}, u32[]{:S(2)}, u32[]{:S(2)}) collective-permute-start(bf16[512,768]{1,0:T(8,128)(2,1)S(1)} %get-tuple-element.57.c_ref.qm_ref), channel_id=1, source_target_pairs={{0,240},{4,244},{8,248},{12,252},{16,0},{20,4},{24,8},{28,12},{32,... | collective-permute-start | bytes 2359304 | tf_op jit(solution)/shard_map/ppermute | solution.py:339
  36.1 1.8 %collective-permute-start.10 = (bf16[512,256]{1,0:T(8,128)(2,1)S(1)}, bf16[512,256]{1,0:T(8,128)(2,1)S(1)}, u32[]{:S(2)}, u32[]{:S(2)}) collective-permute-start(bf16[512,256]{1,0:T(8,128)(2,1)S(1)} %get-tuple-element.58.kpm_ref), channel_id=1, source_target_pairs={{0,1},{1,0},{2,3},{3,2},{4,5},{5,4},{6,7},{7,6},{8,9},{9,8},{10,11... | collective-permute-start | bytes 786440 | tf_op jit(solution)/shard_map/ppermute | solution.py:349
  43.5 9.8 %collective-permute-start.11 = (f32[4,2,512]{2,1,0:T(2,128)S(1)}, f32[4,2,512]{2,1,0:T(2,128)S(1)}, u32[]{:S(2)}, u32[]{:S(2)}) collective-permute-start(f32[4,2,512]{2,1,0:T(2,128)S(1)} %get-tuple-element.59), channel_id=1, source_target_pairs={{0,240},{4,244},{8,248},{12,252},{16,0},{20,4},{24,8},{28,12},{32,... | collective-permute-start | bytes 49160 | tf_op jit(solution)/shard_map/ppermute | solution.py:339
  53.3 1.6 %collective-permute-start.12 = (bf16[512,256]{1,0:T(8,128)(2,1)S(1)}, bf16[512,256]{1,0:T(8,128)(2,1)S(1)}, u32[]{:S(2)}, u32[]{:S(2)}) collective-permute-start(bf16[512,256]{1,0:T(8,128)(2,1)S(1)} %slice.3), channel_id=1, source_target_pairs={{0,1},{1,0},{2,3},{3,2},{4,5},{5,4},{6,7},{7,6},{8,9},{9,8},{10,11... | collective-permute-start | bytes 786440 | tf_op jit(solution)/shard_map/ppermute | solution.py:349
  53.4 14.5 %collective-permute-start.14 = (bf16[512,256]{1,0:T(8,128)(2,1)S(1)}, bf16[512,256]{1,0:T(8,128)(2,1)S(1)}, u32[]{:S(2)}, u32[]{:S(2)}) collective-permute-start(bf16[512,256]{1,0:T(8,128)(2,1)S(1)} %get-tuple-element.76), channel_id=1, source_target_pairs={{0,1},{1,0},{2,3},{3,2},{4,5},{5,4},{6,7},{7,6},{8,9},{9,8},{10,11... | collective-permute-start | bytes 786440 | tf_op jit(solution)/shard_map/ppermute | solution.py:349
  58.8 9.1 %collective-permute-start.13 = (bf16[512,256]{1,0:T(8,128)(2,1)S(1)}, bf16[512,256]{1,0:T(8,128)(2,1)S(1)}, u32[]{:S(2)}, u32[]{:S(2)}) collective-permute-start(bf16[512,256]{1,0:T(8,128)(2,1)S(1)} %get-tuple-element.74), channel_id=1, source_target_pairs={{0,1},{1,0},{2,3},{3,2},{4,5},{5,4},{6,7},{7,6},{8,9},{9,8},{10,11... | collective-permute-start | bytes 786440 | tf_op jit(solution)/shard_map/ppermute | solution.py:349
  59.0 13.4 %collective-permute-start.19 = (f32[4,512]{1,0:T(4,128)S(1)}, f32[4,512]{1,0:T(4,128)S(1)}, u32[]{:S(2)}, u32[]{:S(2)}) collective-permute-start(f32[4,512]{1,0:T(4,128)S(1)} %bitcast.10), channel_id=1, source_target_pairs={{0,16},{4,20},{8,24},{12,28},{16,0},{20,4},{24,8},{28,12},{32,48},... | collective-permute-start | bytes 24584 | tf_op jit(solution)/shard_map/ppermute | solution.py:401
  60.4 14.1 %collective-permute-start.20 = (f32[4,512]{1,0:T(4,128)S(1)}, f32[4,512]{1,0:T(4,128)S(1)}, u32[]{:S(2)}, u32[]{:S(2)}) collective-permute-start(f32[4,512]{1,0:T(4,128)S(1)} %bitcast.11), channel_id=1, source_target_pairs={{0,128},{4,132},{8,136},{12,140},{16,144},{20,148},{24,152},{28,15... | collective-permute-start | bytes 24584 | tf_op jit(solution)/shard_map/ppermute | solution.py:401
  66.7 10.0 %collective-permute-start.21 = (f32[4,512]{1,0:T(4,128)S(1)}, f32[4,512]{1,0:T(4,128)S(1)}, u32[]{:S(2)}, u32[]{:S(2)}) collective-permute-start(f32[4,512]{1,0:T(4,128)S(1)} %bitcast.12), channel_id=1, source_target_pairs={{0,144},{4,148},{8,152},{12,156},{16,128},{20,132},{24,136},{28,14... | collective-permute-start | bytes 24584 | tf_op jit(solution)/shard_map/ppermute | solution.py:401
  68.6 21.5 %collective-permute-start.15 = (bf16[128,1024]{1,0:T(8,128)(2,1)S(1)}, bf16[128,1024]{1,0:T(8,128)(2,1)S(1)}, u32[]{:S(2)}, u32[]{:S(2)}) collective-permute-start(bf16[128,1024]{1,0:T(8,128)(2,1)S(1)} %get-tuple-element.78), channel_id=1, source_target_pairs={{0,4},{4,8},{8,12},{12,0},{16,20},{20,24},{24,28},{28,16},{32,36},... | collective-permute-start | bytes 786440 | tf_op jit(solution)/shard_map/ppermute | solution.py:343
  71.7 20.4 %collective-permute-start.16 = (bf16[128,1024]{1,0:T(8,128)(2,1)S(1)}, bf16[128,1024]{1,0:T(8,128)(2,1)S(1)}, u32[]{:S(2)}, u32[]{:S(2)}) collective-permute-start(bf16[128,1024]{1,0:T(8,128)(2,1)S(1)} %get-tuple-element.79), channel_id=1, source_target_pairs={{0,8},{4,12},{8,0},{12,4},{16,24},{20,28},{24,16},{28,20},{32,40},... | collective-permute-start | bytes 786440 | tf_op jit(solution)/shard_map/ppermute | solution.py:343
  72.4 19.7 %collective-permute-start.17 = (bf16[128,1024]{1,0:T(8,128)(2,1)S(1)}, bf16[128,1024]{1,0:T(8,128)(2,1)S(1)}, u32[]{:S(2)}, u32[]{:S(2)}) collective-permute-start(bf16[128,1024]{1,0:T(8,128)(2,1)S(1)} %get-tuple-element.80), channel_id=1, source_target_pairs={{0,12},{4,0},{8,4},{12,8},{16,28},{20,16},{24,20},{28,24},{32,44},... | collective-permute-start | bytes 786440 | tf_op jit(solution)/shard_map/ppermute | solution.py:343
  76.8 3.7 %collective-permute-start.22 = (f32[4,512]{1,0:T(4,128)S(1)}, f32[4,512]{1,0:T(4,128)S(1)}, u32[]{:S(2)}, u32[]{:S(2)}) collective-permute-start(f32[4,512]{1,0:T(4,128)S(1)} %add_add_fusion.1), channel_id=1, source_target_pairs={{0,32},{4,36},{8,40},{12,44},{16,48},{20,52},{24,56},{28,60},{32,0... | collective-permute-start | bytes 24584 | tf_op jit(solution)/shard_map/ppermute | solution.py:401
  77.8 5.7 %collective-permute-start.23 = (f32[4,512]{1,0:T(4,128)S(1)}, f32[4,512]{1,0:T(4,128)S(1)}, u32[]{:S(2)}, u32[]{:S(2)}) collective-permute-start(f32[4,512]{1,0:T(4,128)S(1)} %add_add_fusion.1), channel_id=1, source_target_pairs={{0,64},{4,68},{8,72},{12,76},{16,80},{20,84},{24,88},{28,92},{32,9... | collective-permute-start | bytes 24584 | tf_op jit(solution)/shard_map/ppermute | solution.py:401
  80.5 5.4 %collective-permute-start.24 = (f32[4,512]{1,0:T(4,128)S(1)}, f32[4,512]{1,0:T(4,128)S(1)}, u32[]{:S(2)}, u32[]{:S(2)}) collective-permute-start(f32[4,512]{1,0:T(4,128)S(1)} %add_add_fusion.1), channel_id=1, source_target_pairs={{0,96},{4,100},{8,104},{12,108},{16,112},{20,116},{24,120},{28,124... | collective-permute-start | bytes 24584 | tf_op jit(solution)/shard_map/ppermute | solution.py:401
  86.0 7.3 %collective-permute-start.25 = (f32[4,512]{1,0:T(4,128)S(1)}, f32[4,512]{1,0:T(4,128)S(1)}, u32[]{:S(2)}, u32[]{:S(2)}) collective-permute-start(f32[4,512]{1,0:T(4,128)S(1)} %add_add_fusion.refs_0_), channel_id=1, source_target_pairs={{0,4},{4,8},{8,12},{12,0},{16,20},{20,24},{24,28},{28,16},{32,36},... | collective-permute-start | bytes 24584 | tf_op jit(solution)/shard_map/ppermute | solution.py:343
  89.3 5.2 %collective-permute-start.26 = (f32[4,512]{1,0:T(4,128)S(1)}, f32[4,512]{1,0:T(4,128)S(1)}, u32[]{:S(2)}, u32[]{:S(2)}) collective-permute-start(f32[4,512]{1,0:T(4,128)S(1)} %add_add_fusion.refs_0_), channel_id=1, source_target_pairs={{0,8},{4,12},{8,0},{12,4},{16,24},{20,28},{24,16},{28,20},{32,40},... | collective-permute-start | bytes 24584 | tf_op jit(solution)/shard_map/ppermute | solution.py:343
  90.1 4.3 %collective-permute-start.27 = (f32[4,512]{1,0:T(4,128)S(1)}, f32[4,512]{1,0:T(4,128)S(1)}, u32[]{:S(2)}, u32[]{:S(2)}) collective-permute-start(f32[4,512]{1,0:T(4,128)S(1)} %add_add_fusion.refs_0_), channel_id=1, source_target_pairs={{0,12},{4,0},{8,4},{12,8},{16,28},{20,16},{24,20},{28,24},{32,44},... | collective-permute-start | bytes 24584 | tf_op jit(solution)/shard_map/ppermute | solution.py:343
  92.7 5.1 %collective-permute-start.18 = (f32[128,256]{1,0:T(8,128)S(1)}, f32[128,256]{1,0:T(8,128)S(1)}, u32[]{:S(2)}, u32[]{:S(2)}) collective-permute-start(f32[128,256]{1,0:T(8,128)S(1)} %get-tuple-element.82), channel_id=1, source_target_pairs={{0,2},{1,3},{2,0},{3,1},{4,6},{5,7},{6,4},{7,5},{8,10},{9,11},{10,... | collective-permute-start | bytes 393224 | tf_op jit(solution)/shard_map/ppermute | solution.py:436
